TPU v7x, 1024 devices: a whole 4x4x32 slice. The times are simulated.
1024 devices in a mesh: prow: 16 (over x, z_hi, core), pcol: 64 (over z_lo, y).
Axes of the slice: x: 4, y: 4, z: 32 (z_hi: 2, z_lo: 16; z = z_hi * 16 + z_lo), core: 2. Of those that a mesh axis runs over, the one named last changes fastest.
Arguments:
- left_blocks: bfloat16 [38912, 128, 128], P(('prow', 'pcol')), may hold values from -6 to 6
- left_mask: int32 [38912], P(('prow', 'pcol')), may hold values from 0 to 1, as said below
- right_blocks: bfloat16 [24576, 128, 128], P(('prow', 'pcol')), may hold values from -0.125 to 0.125
- pair_lists: int32 [1024, 4, 3, 12], P(('prow', 'pcol')), may hold values from 0 to 37, as said below
- pair_counts: int32 [1024, 4], P(('prow', 'pcol')), may hold values from 0 to 12, as said below
Outputs:
- product: bfloat16 [4096, 8192], P('prow', 'pcol')
Inputs may be any that keep to these rules, and one draw needn't show every extreme that they name: `left_mask`: each process's 38 entries hold between 9 and 19 ones; some process holds exactly 19. `pair_lists`: each slot of a right sub-panel stores one block (k, j) of the right matrix, k < 19 a contraction block of the panel and j < 1 a block column, distinct within the sub-panel (the keys are not given). For process (r, c) and step u with s = u - 2, the live pairs are exactly all pairs of an occupied left block i * 19 + k of the panel of process (r, (c + s) mod 64) with the slot of the step's sub-panel that stores (k, j), each listed once with entry 2 = i + j. Every entry 0, live or not, names an occupied left block of that panel; entry 1 is below 6; entry 2 is below 2. `pair_counts`: some process has 12 live pairs in every step.
All inputs are finite; a program needn't handle non-finite values.
Results may differ from a plain program's by a relative error of at most 0.001.
Values may be sent and summed in bfloat16 or wider, within the bound.
No kernel may reach another device: no remote copies, remote signals or barrier semaphores. Data moves between devices by JAX's collectives and lax.ppermute only.
A program may use at most 32 MiB of HBM per device.

v0:
```python
import jax
import jax.numpy as jnp
from jax import lax
from jax.sharding import PartitionSpec as P

BR = 2
BC = 1


def from_behind(shard, axis, by):
    size = lax.axis_size(axis)
    return lax.ppermute(shard, axis, [(i, (i + by) % size) for i in range(size)])


def dense_take(package, indices):
    blocks, occupancy = package
    return blocks[indices] * occupancy[indices].astype(jnp.bfloat16)[:, None, None]


def on_device(left_blocks, left_mask, right_blocks, pair_lists, pair_counts):
    ratio_count = lax.axis_size("pcol") // lax.axis_size("prow")
    sub_count = max(2, ratio_count - ratio_count % 2)
    half_span = sub_count // 2
    block_order = left_blocks.shape[1]
    sub_slots = right_blocks.shape[0] // sub_count
    out_blocks = BR * BC
    pair_slots = pair_lists.shape[3]
    all_lists = pair_lists[0]
    all_counts = pair_counts[0]
    own_right = right_blocks.reshape(sub_count, sub_slots, block_order, block_order)
    upper_half = from_behind(own_right[half_span:], "prow", 1)
    accumulated = jnp.zeros((out_blocks, block_order * block_order), jnp.float32)
    package = (left_blocks, left_mask)
    panels = {0: package}
    current = package
    offset = 1
    current = from_behind((current[0], current[1]), "pcol", -1)
    panels[offset] = current
    current = package
    for offset in range(1, half_span + 1):
        current = from_behind((current[0], current[1]), "pcol", 1)
        panels[-offset] = current
    for step_index in range(2 * half_span):
        offset = step_index - half_span
        step_lists = all_lists[step_index]
        left_taken = dense_take(panels[offset], step_lists[0])
        chosen = (upper_half[offset + half_span] if offset < 0 else own_right[offset])[
            step_lists[1]
        ]
        products = jnp.einsum(
            "pij,pjk->pik", left_taken, chosen, preferred_element_type=jnp.float32
        )
        live_pairs = jnp.arange(pair_slots) < all_counts[step_index : step_index + 1][0]
        onehot = (
            (step_lists[2][None, :] == jnp.arange(out_blocks)[:, None]) & live_pairs[None, :]
        ).astype(jnp.float32)
        accumulated = accumulated + jnp.dot(
            onehot,
            products.reshape(pair_slots, block_order * block_order),
            precision=lax.Precision.HIGHEST,
            preferred_element_type=jnp.float32,
        )
    tiles = accumulated.reshape(BR, BC, block_order, block_order).transpose(0, 2, 1, 3)
    return tiles.reshape(BR * block_order, BC * block_order).astype(jnp.bfloat16)


def solution(mesh):
    in_specs = (
        P(("prow", "pcol"), None, None),
        P(("prow", "pcol")),
        P(("prow", "pcol"), None, None),
        P(("prow", "pcol"), None, None, None),
        P(("prow", "pcol"), None),
    )
    out_specs = P("prow", "pcol")
    return jax.shard_map(
        on_device, mesh=mesh, in_specs=in_specs, out_specs=out_specs, check_vma=False
    )
```

profile of v0, /device:TPU:1, one launch (start us, length us, event | category | flops | bytes accessed | tf_op | source)
XLA Modules:
  0.0 148.6 jit_solution(75633336297290588)
XLA Ops:
  0.0 4.2 %collective-permute-start = (bf16[38,128,128]{2,1,0:T(8,128)(2,1)}, bf16[38,128,128]{2,1,0:T(8,128)(2,1)}, u32[]{:S(2)}, u32[]{:S(2)}) collective-permute-start(bf16[38,128,128]{2,1,0:T(8,128)(2,1)} %param.5), channel_id=1, source_target_pairs={{0,1},{1,2},{2,3},{3,4},{4,5},{5,6},{6,7},{7,8},{8,9},{9,10},{10,1... | collective-permute-start | bytes 3735560 | tf_op jit(solution)/shard_map/ppermute | solution.py:12
  4.2 27.3 %collective-permute-start.5 = (bf16[38,128,128]{2,1,0:T(8,128)(2,1)}, bf16[38,128,128]{2,1,0:T(8,128)(2,1)}, u32[]{:S(2)}, u32[]{:S(2)}) collective-permute-start(bf16[38,128,128]{2,1,0:T(8,128)(2,1)} %param.5), channel_id=1, source_target_pairs={{0,63},{1,0},{2,1},{3,2},{4,3},{5,4},{6,5},{7,6},{8,7},{9,8},{10,9... | collective-permute-start | bytes 3735560 | tf_op jit(solution)/shard_map/ppermute | solution.py:12
  31.5 1.9 %collective-permute-start.2 = (s32[38]{0:T(128)}, s32[38]{0:T(128)S(1)}, u32[]{:S(2)}, u32[]{:S(2)}) collective-permute-start(s32[38]{0:T(128)} %param.6), channel_id=1, source_target_pairs={{0,1},{1,2},{2,3},{3,4},{4,5},{5,6},{6,7},{7,8},{8,9},{9,10},{10,1... | collective-permute-start | bytes 464 | tf_op jit(solution)/shard_map/ppermute | solution.py:12
  33.4 21.7 %collective-permute-start.6 = (s32[38]{0:T(128)}, s32[38]{0:T(128)S(1)}, u32[]{:S(2)}, u32[]{:S(2)}) collective-permute-start(s32[38]{0:T(128)} %param.6), channel_id=1, source_target_pairs={{0,63},{1,0},{2,1},{3,2},{4,3},{5,4},{6,5},{7,6},{8,7},{9,8},{10,9... | collective-permute-start | bytes 464 | tf_op jit(solution)/shard_map/ppermute | solution.py:12
  55.1 1.0 slice.107
  56.1 23.5 %collective-permute-start.4 = (bf16[2,6,128,128]{3,2,1,0:T(8,128)(2,1)S(1)}, bf16[2,6,128,128]{3,2,1,0:T(8,128)(2,1)S(1)}, u32[]{:S(2)}, u32[]{:S(2)}) collective-permute-start(bf16[2,6,128,128]{3,2,1,0:T(8,128)(2,1)S(1)} %bitcast.77), channel_id=1, source_target_pairs={{0,64},{64,128},{128,192},{192,256},{256,320},{320,384},{384,448},... | collective-permute-start | bytes 1179656 | tf_op jit(solution)/shard_map/ppermute | solution.py:12
  79.6 0.9 fusion.36
  80.5 1.9 %gather_fusion.6 = bf16[12,128,128]{2,1,0:T(8,128)(2,1)S(1)} fusion(bf16[38,128,128]{2,1,0:T(8,128)(2,1)} %param.5, s32[1024]{0:T(1024)S(1)} %get-tuple-element.28), kind=kCustom, calls=%fused_computation.6 | custom fusion | bytes 786480 | tf_op jit(solution)/shard_map/gather | solution.py:17
  82.4 0.0 copy-done
  82.4 0.0 copy-start.2
  82.5 0.7 gather_fusion.7
  83.1 0.0 copy-done.1
  83.2 0.6 gather_fusion.8
  83.8 0.0 copy-done.2
  83.8 0.7 fusion.43
  84.5 1.1 iota_compare_fusion.3
  85.6 0.3 fusion.3
  85.9 1.2 iota_compare_fusion.2
  87.2 0.0 collective-permute-done
  87.2 1.9 %collective-permute-start.1 = (bf16[38,128,128]{2,1,0:T(8,128)(2,1)}, bf16[38,128,128]{2,1,0:T(8,128)(2,1)}, u32[]{:S(2)}, u32[]{:S(2)}) collective-permute-start(bf16[38,128,128]{2,1,0:T(8,128)(2,1)} %collective-permute-done), channel_id=1, source_target_pairs={{0,1},{1,2},{2,3},{3,4},{4,5},{5,6},{6,7},{7,8},{8,9},{9,10},{10,1... | collective-permute-start | bytes 3735560 | tf_op jit(solution)/shard_map/ppermute | solution.py:12
  89.1 1.2 iota_compare_fusion.1
  90.3 1.2 iota_compare_fusion
  91.4 0.1 pad.14
  91.5 0.6 copy.8
  92.1 0.0 copy-start.3
  92.2 1.4 slice_bitcast_fusion.2
  93.6 0.6 gather_fusion.11
  94.2 0.0 collective-permute-done.2
  94.2 0.7 gather_fusion.4
  94.9 1.9 %collective-permute-start.3 = (s32[38]{0:T(128)S(1)}, s32[38]{0:T(128)S(1)}, u32[]{:S(2)}, u32[]{:S(2)}) collective-permute-start(s32[38]{0:T(128)S(1)} %collective-permute-done.2), channel_id=1, source_target_pairs={{0,1},{1,2},{2,3},{3,4},{4,5},{5,6},{6,7},{7,8},{8,9},{9,10},{10,1... | collective-permute-start | bytes 464 | tf_op jit(solution)/shard_map/ppermute | solution.py:12
  96.8 0.0 collective-permute-done.6
  96.8 0.7 gather_fusion.10
  97.5 35.6 %collective-permute-done.3 = s32[38]{0:T(128)S(1)} collective-permute-done((s32[38]{0:T(128)S(1)}, s32[38]{0:T(128)S(1)}, u32[]{:S(2)}, u32[]{:S(2)}) %collective-permute-start.3) | collective-permute-done | bytes 184 | tf_op jit(solution)/shard_map/ppermute | solution.py:12
  133.1 0.7 gather_fusion.1
  133.7 0.0 copy-done.3
  133.8 0.0 collective-permute-done.4
  133.8 0.6 gather_fusion.2
  134.4 0.6 gather_fusion.5
  135.1 1.9 %gather_fusion.3 = bf16[12,128,128]{2,1,0:T(8,128)(2,1)S(1)} fusion(bf16[38,128,128]{2,1,0:T(8,128)(2,1)} %collective-permute-done, s32[1024]{0:T(1024)S(1)} %get-tuple-element.30), kind=kCustom, calls=%fused_computation.3 | custom fusion | bytes 786480 | tf_op jit(solution)/shard_map/gather | solution.py:17
  137.0 0.3 fusion.5
  137.3 0.1 pad.13
  137.4 0.6 copy.7
  138.0 0.0 collective-permute-done.5
  138.0 2.0 %gather_fusion.9 = bf16[12,128,128]{2,1,0:T(8,128)(2,1)S(1)} fusion(bf16[38,128,128]{2,1,0:T(8,128)(2,1)} %collective-permute-done.5, s32[1024]{0:T(1024)} %copy-done.3), kind=kCustom, calls=%fused_computation.9 | custom fusion | bytes 786480 | tf_op jit(solution)/shard_map/gather | solution.py:17
  140.1 0.3 fusion.1
  140.4 0.1 pad.15
  140.5 0.6 copy.9
  141.1 0.0 collective-permute-done.1
  141.1 2.6 %gather_fusion = bf16[12,128,128]{2,1,0:T(8,128)(2,1)} fusion(bf16[38,128,128]{2,1,0:T(8,128)(2,1)} %collective-permute-done.1, s32[1024]{0:T(1024)S(1)} %get-tuple-element.32), kind=kCustom, calls=%fused_computation | custom fusion | bytes 786480 | tf_op jit(solution)/shard_map/gather | solution.py:17
  143.8 1.3 fusion.7
  145.1 0.1 pad.12
  145.2 0.0 copy-start.7
  145.2 0.0 copy-start.8
  145.2 0.0 copy-start.6
  145.2 0.0 copy-start.9
  145.2 0.6 copy.6
  145.8 0.0 copy-done.7
  145.8 0.0 copy-done.8
  145.8 0.0 copy-start.5
  145.9 0.5 fusion.19
  146.4 0.5 convolution_add_fusion.2
  146.9 0.5 convolution_add_fusion.1
  147.4 0.5 fusion
  147.9 0.7 convert_element_type.43
  (21 shorter events, 0.1 us)
Async XLA Ops:
  0.0 82.4 %copy-start = (s32[38]{0:T(128)S(1)}, s32[38]{0:T(128)}, u32[]{:S(2)}) copy-start(s32[38]{0:T(128)} %param.6) | copy-start | bytes 460
  0.0 83.1 %copy-start.1 = (bf16[24,128,128]{2,1,0:T(8,128)(2,1)S(1)}, bf16[24,128,128]{2,1,0:T(8,128)(2,1)}, u32[]{:S(2)}) copy-start(bf16[24,128,128]{2,1,0:T(8,128)(2,1)} %param.7) | copy-start | bytes 2359300
  0.0 87.2 %collective-permute-start = (bf16[38,128,128]{2,1,0:T(8,128)(2,1)}, bf16[38,128,128]{2,1,0:T(8,128)(2,1)}, u32[]{:S(2)}, u32[]{:S(2)}) collective-permute-start(bf16[38,128,128]{2,1,0:T(8,128)(2,1)} %param.5), channel_id=1, source_target_pairs={{0,1},{1,2},{2,3},{3,4},{4,5},{5,6},{6,7},{7,8},{8,9},{9,10},{10,1... | collective-permute-start | bytes 3735560 | tf_op jit(solution)/shard_map/ppermute | solution.py:12
  4.2 133.8 %collective-permute-start.5 = (bf16[38,128,128]{2,1,0:T(8,128)(2,1)}, bf16[38,128,128]{2,1,0:T(8,128)(2,1)}, u32[]{:S(2)}, u32[]{:S(2)}) collective-permute-start(bf16[38,128,128]{2,1,0:T(8,128)(2,1)} %param.5), channel_id=1, source_target_pairs={{0,63},{1,0},{2,1},{3,2},{4,3},{5,4},{6,5},{7,6},{8,7},{9,8},{10,9... | collective-permute-start | bytes 3735560 | tf_op jit(solution)/shard_map/ppermute | solution.py:12
  31.5 62.7 %collective-permute-start.2 = (s32[38]{0:T(128)}, s32[38]{0:T(128)S(1)}, u32[]{:S(2)}, u32[]{:S(2)}) collective-permute-start(s32[38]{0:T(128)} %param.6), channel_id=1, source_target_pairs={{0,1},{1,2},{2,3},{3,4},{4,5},{5,6},{6,7},{7,8},{8,9},{9,10},{10,1... | collective-permute-start | bytes 464 | tf_op jit(solution)/shard_map/ppermute | solution.py:12
  33.4 63.4 %collective-permute-start.6 = (s32[38]{0:T(128)}, s32[38]{0:T(128)S(1)}, u32[]{:S(2)}, u32[]{:S(2)}) collective-permute-start(s32[38]{0:T(128)} %param.6), channel_id=1, source_target_pairs={{0,63},{1,0},{2,1},{3,2},{4,3},{5,4},{6,5},{7,6},{8,7},{9,8},{10,9... | collective-permute-start | bytes 464 | tf_op jit(solution)/shard_map/ppermute | solution.py:12
  56.1 77.6 %collective-permute-start.4 = (bf16[2,6,128,128]{3,2,1,0:T(8,128)(2,1)S(1)}, bf16[2,6,128,128]{3,2,1,0:T(8,128)(2,1)S(1)}, u32[]{:S(2)}, u32[]{:S(2)}) collective-permute-start(bf16[2,6,128,128]{3,2,1,0:T(8,128)(2,1)S(1)} %bitcast.77), channel_id=1, source_target_pairs={{0,64},{64,128},{128,192},{192,256},{256,320},{320,384},{384,448},... | collective-permute-start | bytes 1179656 | tf_op jit(solution)/shard_map/ppermute | solution.py:12
  82.4 1.4 copy-start.2
  87.2 53.9 %collective-permute-start.1 = (bf16[38,128,128]{2,1,0:T(8,128)(2,1)}, bf16[38,128,128]{2,1,0:T(8,128)(2,1)}, u32[]{:S(2)}, u32[]{:S(2)}) collective-permute-start(bf16[38,128,128]{2,1,0:T(8,128)(2,1)} %collective-permute-done), channel_id=1, source_target_pairs={{0,1},{1,2},{2,3},{3,4},{4,5},{5,6},{6,7},{7,8},{8,9},{9,10},{10,1... | collective-permute-start | bytes 3735560 | tf_op jit(solution)/shard_map/ppermute | solution.py:12
  92.1 41.6 %copy-start.3 = (s32[1024]{0:T(1024)}, s32[1024]{0:T(1024)S(1)}, u32[]{:S(2)}) copy-start(s32[1024]{0:T(1024)S(1)} %get-tuple-element.26) | copy-start | bytes 12292
  94.9 38.2 %collective-permute-start.3 = (s32[38]{0:T(128)S(1)}, s32[38]{0:T(128)S(1)}, u32[]{:S(2)}, u32[]{:S(2)}) collective-permute-start(s32[38]{0:T(128)S(1)} %collective-permute-done.2), channel_id=1, source_target_pairs={{0,1},{1,2},{2,3},{3,4},{4,5},{5,6},{6,7},{7,8},{8,9},{9,10},{10,1... | collective-permute-start | bytes 464 | tf_op jit(solution)/shard_map/ppermute | solution.py:12
  145.2 0.7 copy-start.7
  145.2 0.7 copy-start.8
  145.2 1.2 copy-start.6
  145.2 1.2 copy-start.9
  145.8 1.1 copy-start.5
  145.9 1.1 copy-start.11
  146.4 1.0 copy-start.4
  146.4 1.0 copy-start.10
where the time goes:
time: 149 us
  starting transfers between devices  82.4 us (55%)
  waiting for transfers between devices  35.6 us (24%)
  local copies, waits for them, and re-layouts  20.3 us (14%)
  other arithmetic  5.61 us (4%)
  matrix products  4.22 us (3%)
    ppermute x7, starting transfers between devices, from_behind(): lax.ppermute(shard, axis, [(i, (i + by) % size) for i in range(size)])  82.4 us
    ppermute x7, waiting for transfers between devices, from_behind(): lax.ppermute(shard, axis, [(i, (i + by) % size) for i in range(size)])  35.6 us
    gather x4, local copies, waits for them, and re-layouts, dense_take(): blocks[indices] * occupancy[indices].astype(jnp.bfloat16)[:, None, None]  8.51 us
    lt x4, other arithmetic, on_device(): jnp.arange(pair_slots) < all_counts[step_index:step_index + 1][0]  4.68 us
  transfers between devices with their start and end apart: 7, of which 1 were waited for; matrix products, arithmetic and copies ran while one was open for 15% of the time, Pallas kernels for 0%

commit v1 on v0

v1 whole, which is shorter than its diff:
```python
import functools

import jax
import jax.numpy as jnp
from jax import lax
from jax.experimental import pallas as pl
from jax.experimental.pallas import tpu as pltpu
from jax.sharding import PartitionSpec as P

BR = 2
BC = 1
BS = 128
CAP_L = 19
CAPM = 6
META = 16
DEAR = pl.CostEstimate(flops=1 << 36, bytes_accessed=1 << 28, transcendentals=0)
CHEAP = pl.CostEstimate(flops=0, bytes_accessed=1024, transcendentals=0)


def by_pairs(array, pairs):
    return lax.ppermute(array, ("prow", "pcol"), pairs)


def pack_kernel(mask_ref, left_ref, meta_ref, after_ref, packed_ref, sem):
    del after_ref
    panel = left_ref.shape[0]
    tail = pltpu.make_async_copy(meta_ref, packed_ref.at[pl.ds(CAP_L * BS, META)], sem)
    tail.start()
    slot = jnp.int32(0)
    for q in range(panel):
        taken = jnp.logical_and(mask_ref[q] != 0, slot < CAP_L)

        @pl.when(taken)
        def _(q=q, slot=slot):
            row = pl.multiple_of(slot * BS, BS)
            pltpu.make_async_copy(left_ref.at[q], packed_ref.at[pl.ds(row, BS)], sem).start()

        slot = slot + taken.astype(jnp.int32)

    @pl.loop(slot, CAP_L)
    def _(spare):
        row = pl.multiple_of(spare * BS, BS)
        pltpu.make_async_copy(left_ref.at[0], packed_ref.at[pl.ds(row, BS)], sem).start()

    pltpu.make_async_copy(packed_ref, packed_ref, sem).wait()


def pack(left_blocks, left_mask, after):
    meta = jnp.zeros((META, BS), jnp.bfloat16)
    row = jnp.pad(left_mask.astype(jnp.bfloat16), (0, BS - left_mask.shape[0]))
    meta = jnp.broadcast_to(row[None, :], (META, BS))
    return pl.pallas_call(
        pack_kernel,
        out_shape=jax.ShapeDtypeStruct((CAP_L * BS + META, BS), jnp.bfloat16),
        in_specs=[
            pl.BlockSpec(memory_space=pltpu.SMEM),
        ]
        + [pl.BlockSpec(memory_space=pl.ANY)] * 3,
        out_specs=pl.BlockSpec(memory_space=pl.ANY),
        scratch_shapes=[pltpu.SemaphoreType.DMA],
        cost_estimate=CHEAP,
        name="pack_panel",
    )(left_mask, left_blocks, meta, after)


def cut_kernel(first, count, blocks_ref, part_ref, sem):
    copy = pltpu.make_async_copy(blocks_ref.at[pl.ds(first, count)], part_ref, sem)
    copy.start()
    copy.wait()


def cut(blocks, first, count):
    return pl.pallas_call(
        functools.partial(cut_kernel, first, count),
        out_shape=jax.ShapeDtypeStruct((count,) + blocks.shape[1:], blocks.dtype),
        in_specs=[pl.BlockSpec(memory_space=pl.ANY)],
        out_specs=pl.BlockSpec(memory_space=pl.ANY),
        scratch_shapes=[pltpu.SemaphoreType.DMA],
        cost_estimate=CHEAP,
        name="cut_right",
    )(blocks)


def mask_of(packed, panel):
    return packed[CAP_L * BS, :panel].astype(jnp.int32)


def step_kernel(has_acc, lists_ref, count_ref, mask_ref, left_ref, right_ref, *rest):
    if has_acc:
        acc_ref, out_ref, rank_ref, table_ref = rest
    else:
        out_ref, rank_ref, table_ref = rest
    panel = mask_ref.shape[0]
    run = jnp.int32(0)
    for q in range(panel):
        rank_ref[q] = run
        run = run + (mask_ref[q] != 0).astype(jnp.int32)
    for t in range(CAPM * BR):
        table_ref[t] = -1
    for p in range(lists_ref.shape[1]):

        @pl.when(p < count_ref[0])
        def _(p=p):
            at = lists_ref[0, p]
            place = lists_ref[1, p] * BR + lists_ref[2, p]
            table_ref[place] = jnp.where(mask_ref[at] != 0, rank_ref[at], -1)

    for o in range(BR):
        rows = pl.ds(o * BS, BS)
        total = acc_ref[rows, :] if has_acc else jnp.zeros((BS, BS), jnp.float32)
        for m in range(CAPM):
            rank = table_ref[m * BR + o]
            row = pl.multiple_of(jnp.clip(rank, 0, CAP_L - 1) * BS, BS)
            block = left_ref[pl.ds(row, BS), :]
            block = jnp.where(rank >= 0, block, jnp.zeros_like(block))
            total = total + jnp.dot(block, right_ref[m], preferred_element_type=jnp.float32)
        out_ref[rows, :] = total.astype(out_ref.dtype)


def step(lists, count, mask, left, right, acc, dtype, name, cost=CHEAP):
    smem = pl.BlockSpec(memory_space=pltpu.SMEM)
    vmem = pl.BlockSpec(memory_space=pltpu.VMEM)
    args = [lists, count, mask, left, right] + ([] if acc is None else [acc])
    return pl.pallas_call(
        functools.partial(step_kernel, acc is not None),
        out_shape=jax.ShapeDtypeStruct((BR * BS, BS), dtype),
        in_specs=[smem] * 3 + [vmem] * (len(args) - 3),
        out_specs=vmem,
        scratch_shapes=[
            pltpu.SMEM((mask.shape[0],), jnp.int32),
            pltpu.SMEM((CAPM * BR,), jnp.int32),
        ],
        cost_estimate=cost,
        name=name,
    )(*args)


def on_device(n_row, n_col, left_blocks, left_mask, right_blocks, pair_lists, pair_counts):
    panel = left_blocks.shape[0]
    lists, counts = pair_lists[0], pair_counts[0]

    def shift(rows, cols):
        return [
            (r * n_col + c, (r + rows) % n_row * n_col + (c + cols) % n_col)
            for r in range(n_row)
            for c in range(n_col)
        ]

    right = [right_blocks[m * CAPM : (m + 1) * CAPM] for m in range(4)]
    counts_at = [counts[u : u + 1] for u in range(4)]

    first_right = cut(right_blocks, 2 * CAPM, CAPM)
    right_2 = by_pairs(first_right, shift(1, -2))
    packed = pack(left_blocks, left_mask, first_right)
    left_below = by_pairs(packed, shift(0, 1))
    left_above = by_pairs(packed, shift(0, -1))
    ask = jnp.concatenate([lists[0].reshape(-1), counts[:1]])
    asked = by_pairs(ask, shift(0, -2))
    right_3 = by_pairs(right[3], shift(1, 0))

    own = step(lists[2], counts_at[2], left_mask, packed, right[0], None, jnp.float32, "own_step")
    sent = step(
        asked[:36].reshape(3, 12), asked[36:37], left_mask, packed, right_2, None,
        jnp.float32, "partial_for_two_above", DEAR,
    )
    from_two_below = by_pairs(sent, shift(0, 2))
    upper = step(
        lists[3], counts_at[3], mask_of(left_above, panel), left_above, right[1], own,
        jnp.float32, "step_above",
    )
    lower = step(
        lists[1], counts_at[1], mask_of(left_below, panel), left_below, right_3, upper,
        jnp.float32, "step_below",
    )
    return (lower + from_two_below).astype(jnp.bfloat16)


def solution(mesh):
    in_specs = (
        P(("prow", "pcol"), None, None),
        P(("prow", "pcol")),
        P(("prow", "pcol"), None, None),
        P(("prow", "pcol"), None, None, None),
        P(("prow", "pcol"), None),
    )
    return jax.shard_map(
        functools.partial(on_device, mesh.shape["prow"], mesh.shape["pcol"]),
        mesh=mesh,
        in_specs=in_specs,
        out_specs=P("prow", "pcol"),
        check_vma=False,
    )
```

time: 149 us -> 136 us (0.913)
  the two profiles are of different devices: /device:TPU:1 before, /device:TPU:13 now
where the time goes in v1:
time: 136 us
  starting transfers between devices  69 us (51%)
  Pallas kernels  39.1 us (29%)
  waiting for transfers between devices  16.4 us (12%)
  local copies, waits for them, and re-layouts  6.89 us (5%)
  other arithmetic  4.03 us (3%)
    ppermute x6, starting transfers between devices, by_pairs(): return lax.ppermute(array, ('prow', 'pcol'), pairs)  69 us
    pallas_call x1, Pallas kernels, pack(): pl.pallas_call(pack_kernel, out_shape=jax.ShapeDtypeStruct((CAP_L * BS +...  20.8 us
    ppermute x6, waiting for transfers between devices, by_pairs(): return lax.ppermute(array, ('prow', 'pcol'), pairs)  16.4 us
    pallas_call x4, Pallas kernels, step(): pl.pallas_call(functools.partial(step_kernel, acc is not None), out_shape...  11.3 us
    pallas_call x1, Pallas kernels, cut(): pl.pallas_call(functools.partial(cut_kernel, first, count), out_shape=jax...  7.06 us
    unnamed x17, local copies, waits for them, and re-layouts  3.42 us
  transfers between devices with their start and end apart: 6, of which 1 were waited for; matrix products, arithmetic and copies ran while one was open for 6% of the time, Pallas kernels for 24%

profile of v1, /device:TPU:13, one launch (start us, length us, event | category | flops | bytes accessed | tf_op | source)
XLA Modules:
  0.0 135.6 jit_solution(11571570315993189518)
XLA Ops:
  0.0 7.1 %cut_right.1.after_ref = bf16[6,128,128]{2,1,0:T(8,128)(2,1)} custom-call(bf16[24,128,128]{2,1,0:T(8,128)(2,1)} %blocks_ref.1), custom_call_target="tpu_custom_call" | custom-call | bytes 1024 | tf_op jit(solution)/shard_map/cut_right/pallas_call | solution.py:73
  7.1 0.0 copy-start.4
  7.1 0.0 copy-start.5
  7.1 0.0 copy-start
  7.1 20.8 %collective-permute-start.4 = (bf16[6,128,128]{2,1,0:T(8,128)(2,1)}, bf16[6,128,128]{2,1,0:T(8,128)(2,1)S(1)}, u32[]{:S(2)}, u32[]{:S(2)}) collective-permute-start(bf16[6,128,128]{2,1,0:T(8,128)(2,1)} %cut_right.1.after_ref), channel_id=1, source_target_pairs={{0,126},{1,127},{2,64},{3,65},{4,66},{5,67},{6,68},{7,69},{8,70},{... | collective-permute-start | bytes 589832 | tf_op jit(solution)/shard_map/ppermute | solution.py:21
  27.9 0.7 convert_element_type.18
  28.6 0.6 broadcast_in_dim.2.meta_ref
  29.2 20.8 %pack_panel.1.left_ref = bf16[2448,128]{1,0:T(8,128)(2,1)} custom-call(s32[38]{0:T(128)} %mask_ref.5, bf16[38,128,128]{2,1,0:T(8,128)(2,1)} %left_ref.1, bf16[16,128]{1,0:T(8,128)(2,1)} %broadcast_in_dim.2.meta_ref, bf16[6,128,128]{2,1,0:T(8,128)(2,1)} %cut_right.1.after_ref), custom_call_target="tpu_custom_call" | custom-call | bytes 1024 | tf_op jit(solution)/shard_map/pack_panel/pallas_call | solution.py:52
  50.0 3.0 %collective-permute-start.2 = (bf16[2448,128]{1,0:T(8,128)(2,1)}, bf16[2448,128]{1,0:T(8,128)(2,1)S(1)}, u32[]{:S(2)}, u32[]{:S(2)}) collective-permute-start(bf16[2448,128]{1,0:T(8,128)(2,1)} %pack_panel.1.left_ref), channel_id=1, source_target_pairs={{0,63},{1,0},{2,1},{3,2},{4,3},{5,4},{6,5},{7,6},{8,7},{9,8},{10,9... | collective-permute-start | bytes 1880072 | tf_op jit(solution)/shard_map/ppermute | solution.py:21
  53.0 10.5 %collective-permute-start = (bf16[2448,128]{1,0:T(8,128)(2,1)}, bf16[2448,128]{1,0:T(8,128)(2,1)S(1)}, u32[]{:S(2)}, u32[]{:S(2)}) collective-permute-start(bf16[2448,128]{1,0:T(8,128)(2,1)} %pack_panel.1.left_ref), channel_id=1, source_target_pairs={{0,1},{1,2},{2,3},{3,4},{4,5},{5,6},{6,7},{7,8},{8,9},{9,10},{10,1... | collective-permute-start | bytes 1880072 | tf_op jit(solution)/shard_map/ppermute | solution.py:21
  63.4 0.0 copy-done.4
  63.5 0.7 fusion.3
  64.1 0.0 copy-done.5
  64.1 0.1 reshape_squeeze.3
  64.2 0.7 pad_add_fusion
  64.9 30.1 %collective-permute-start.3 = (s32[37]{0:T(128)S(1)}, s32[37]{0:T(128)S(1)}, u32[]{:S(2)}, u32[]{:S(2)}) collective-permute-start(s32[37]{0:T(128)S(1)} %pad_add_fusion), channel_id=1, source_target_pairs={{0,62},{1,63},{2,0},{3,1},{4,2},{5,3},{6,4},{7,5},{8,6},{9,7},{10,... | collective-permute-start | bytes 452 | tf_op jit(solution)/shard_map/ppermute | solution.py:21
  95.1 0.0 copy-done
  95.1 0.8 fusion.2
  95.9 2.7 %collective-permute-start.1 = (bf16[6,128,128]{2,1,0:T(8,128)(2,1)S(1)}, bf16[6,128,128]{2,1,0:T(8,128)(2,1)S(1)}, u32[]{:S(2)}, u32[]{:S(2)}) collective-permute-start(bf16[6,128,128]{2,1,0:T(8,128)(2,1)S(1)} %get-tuple-element.6), channel_id=1, source_target_pairs={{0,64},{1,65},{2,66},{3,67},{4,68},{5,69},{6,70},{7,71},{8,72},{9,... | collective-permute-start | bytes 589832 | tf_op jit(solution)/shard_map/ppermute | solution.py:21
  98.6 0.6 copy.13
  99.2 0.6 copy.14
  99.8 0.6 copy.12
  100.4 2.8 %own_step.1.rest_0_ = f32[256,128]{1,0:T(8,128)} custom-call(s32[3,12]{1,0:T(4,128)} %bitcast.26, s32[1]{0:T(128)} %bitcast.4.count_ref, s32[38]{0:T(128)} %mask_ref.5, bf16[2448,128]{1,0:T(8,128)(2,1)} %pack_panel.1.left_ref, bf16[6,128,128]{2,1,0:T(8,128)(2,1)} %get-tuple-element.5.right_ref), custom_call_target="tpu_custom_call" | custom-call | bytes 1024 | tf_op jit(solution)/shard_map/own_step/pallas_call | solution.py:124
  103.2 0.0 collective-permute-done.3
  103.2 0.7 reshape.20.lists_ref
  103.8 0.6 slice.79.count_ref
  104.5 0.0 collective-permute-done.4.right_ref
  104.5 0.0 copy-start.6
  104.5 0.7 copy-done.6
  105.2 2.8 %partial_for_two_above.1 = f32[256,128]{1,0:T(8,128)} custom-call(s32[3,12]{1,0:T(4,128)} %reshape.20.lists_ref, s32[1]{0:T(128)} %slice.79.count_ref, s32[38]{0:T(128)} %mask_ref.5, bf16[2448,128]{1,0:T(8,128)(2,1)} %pack_panel.1.left_ref, bf16[6,128,128]{2,1,0:T(8,128)(2,1)} %copy-done.6), custom_call_target="tpu_custom_call" | custom-call | flops 68719476736 | bytes 268435456 | tf_op jit(solution)/shard_map/partial_for_two_above/pallas_call | solution.py:124
  107.9 1.9 %collective-permute-start.5 = (f32[256,128]{1,0:T(8,128)}, f32[256,128]{1,0:T(8,128)S(1)}, u32[]{:S(2)}, u32[]{:S(2)}) collective-permute-start(f32[256,128]{1,0:T(8,128)} %partial_for_two_above.1), channel_id=1, source_target_pairs={{0,2},{1,3},{2,4},{3,5},{4,6},{5,7},{6,8},{7,9},{8,10},{9,11},{10,... | collective-permute-start | bytes 393224 | tf_op jit(solution)/shard_map/ppermute | solution.py:21
  109.9 0.0 collective-permute-done.2.left_ref
  109.9 0.0 copy-start.2
  109.9 0.5 fusion.mask_ref
  110.4 0.3 copy-done.2
  110.7 2.9 %step_above.1.rest_0_ = f32[256,128]{1,0:T(8,128)} custom-call(s32[3,12]{1,0:T(4,128)} %bitcast.25, s32[1]{0:T(128)} %bitcast.2.count_ref, s32[38]{0:T(128)} %fusion.mask_ref, bf16[2448,128]{1,0:T(8,128)(2,1)} %copy-done.2, bf16[6,128,128]{2,1,0:T(8,128)(2,1)} %get-tuple-element.7.right_ref, f32[256,128]{1,0:T(8,128)} %own_step.1.rest_0_), custom_call_target="tpu_custom_call" | custom-call | bytes 1024 | tf_op jit(solution)/shard_map/step_above/pallas_call | solution.py:124
  113.6 0.0 collective-permute-done.left_ref
  113.6 0.0 copy-start.1
  113.6 0.6 fusion.1.mask_ref
  114.1 0.0 collective-permute-done.1.right_ref
  114.1 0.0 copy-start.3
  114.1 0.3 copy-done.1
  114.4 0.4 copy-done.3
  114.8 2.8 %step_below.1 = f32[256,128]{1,0:T(8,128)} custom-call(s32[3,12]{1,0:T(4,128)} %bitcast.24, s32[1]{0:T(128)} %bitcast.count_ref, s32[38]{0:T(128)} %fusion.1.mask_ref, bf16[2448,128]{1,0:T(8,128)(2,1)} %copy-done.1, bf16[6,128,128]{2,1,0:T(8,128)(2,1)} %copy-done.3, f32[256,128]{1,0:T(8,128)} %step_above.1.rest_0_), custom_call_target="tpu_custom_call" | custom-call | bytes 1024 | tf_op jit(solution)/shard_map/step_below/pallas_call | solution.py:124
  117.6 16.4 %collective-permute-done.5 = f32[256,128]{1,0:T(8,128)S(1)} collective-permute-done((f32[256,128]{1,0:T(8,128)}, f32[256,128]{1,0:T(8,128)S(1)}, u32[]{:S(2)}, u32[]{:S(2)}) %collective-permute-start.5) | collective-permute-done | bytes 131104 | tf_op jit(solution)/shard_map/ppermute | solution.py:21
  134.0 1.6 %add_convert_fusion = bf16[256,128]{1,0:T(8,128)(2,1)} fusion(f32[256,128]{1,0:T(8,128)} %step_below.1, f32[256,128]{1,0:T(8,128)S(1)} %collective-permute-done.5), kind=kLoop, calls=%fused_computation | loop fusion | flops 65536 | bytes 327680 | tf_op jit(solution)/shard_map/convert_element_type | solution.py:175
  (2 shorter events, 0.0 us)
Async XLA Ops:
  7.1 56.4 %copy-start.4 = (s32[1,4]{1,0:T(1,128)S(1)}, s32[1,4]{1,0:T(1,128)}, u32[]{:S(2)}) copy-start(s32[1,4]{1,0:T(1,128)} %param.9) | copy-start | bytes 52
  7.1 57.0 %copy-start.5 = (s32[1,4,3,12]{3,1,2,0:T(4,128)S(1)}, s32[1,4,3,12]{3,1,2,0:T(4,128)}, u32[]{:S(2)}) copy-start(s32[1,4,3,12]{3,1,2,0:T(4,128)} %param.8) | copy-start | bytes 1732
  7.1 88.0 %copy-start = (bf16[24,128,128]{2,1,0:T(8,128)(2,1)S(1)}, bf16[24,128,128]{2,1,0:T(8,128)(2,1)}, u32[]{:S(2)}) copy-start(bf16[24,128,128]{2,1,0:T(8,128)(2,1)} %blocks_ref.1) | copy-start | bytes 2359300
  7.1 97.4 %collective-permute-start.4 = (bf16[6,128,128]{2,1,0:T(8,128)(2,1)}, bf16[6,128,128]{2,1,0:T(8,128)(2,1)S(1)}, u32[]{:S(2)}, u32[]{:S(2)}) collective-permute-start(bf16[6,128,128]{2,1,0:T(8,128)(2,1)} %cut_right.1.after_ref), channel_id=1, source_target_pairs={{0,126},{1,127},{2,64},{3,65},{4,66},{5,67},{6,68},{7,69},{8,70},{... | collective-permute-start | bytes 589832 | tf_op jit(solution)/shard_map/ppermute | solution.py:21
  50.0 59.9 %collective-permute-start.2 = (bf16[2448,128]{1,0:T(8,128)(2,1)}, bf16[2448,128]{1,0:T(8,128)(2,1)S(1)}, u32[]{:S(2)}, u32[]{:S(2)}) collective-permute-start(bf16[2448,128]{1,0:T(8,128)(2,1)} %pack_panel.1.left_ref), channel_id=1, source_target_pairs={{0,63},{1,0},{2,1},{3,2},{4,3},{5,4},{6,5},{7,6},{8,7},{9,8},{10,9... | collective-permute-start | bytes 1880072 | tf_op jit(solution)/shard_map/ppermute | solution.py:21
  53.0 60.6 %collective-permute-start = (bf16[2448,128]{1,0:T(8,128)(2,1)}, bf16[2448,128]{1,0:T(8,128)(2,1)S(1)}, u32[]{:S(2)}, u32[]{:S(2)}) collective-permute-start(bf16[2448,128]{1,0:T(8,128)(2,1)} %pack_panel.1.left_ref), channel_id=1, source_target_pairs={{0,1},{1,2},{2,3},{3,4},{4,5},{5,6},{6,7},{7,8},{8,9},{9,10},{10,1... | collective-permute-start | bytes 1880072 | tf_op jit(solution)/shard_map/ppermute | solution.py:21
  64.9 38.2 %collective-permute-start.3 = (s32[37]{0:T(128)S(1)}, s32[37]{0:T(128)S(1)}, u32[]{:S(2)}, u32[]{:S(2)}) collective-permute-start(s32[37]{0:T(128)S(1)} %pad_add_fusion), channel_id=1, source_target_pairs={{0,62},{1,63},{2,0},{3,1},{4,2},{5,3},{6,4},{7,5},{8,6},{9,7},{10,... | collective-permute-start | bytes 452 | tf_op jit(solution)/shard_map/ppermute | solution.py:21
  95.9 18.3 %collective-permute-start.1 = (bf16[6,128,128]{2,1,0:T(8,128)(2,1)S(1)}, bf16[6,128,128]{2,1,0:T(8,128)(2,1)S(1)}, u32[]{:S(2)}, u32[]{:S(2)}) collective-permute-start(bf16[6,128,128]{2,1,0:T(8,128)(2,1)S(1)} %get-tuple-element.6), channel_id=1, source_target_pairs={{0,64},{1,65},{2,66},{3,67},{4,68},{5,69},{6,70},{7,71},{8,72},{9,... | collective-permute-start | bytes 589832 | tf_op jit(solution)/shard_map/ppermute | solution.py:21
  104.5 0.7 copy-start.6
  107.9 26.1 %collective-permute-start.5 = (f32[256,128]{1,0:T(8,128)}, f32[256,128]{1,0:T(8,128)S(1)}, u32[]{:S(2)}, u32[]{:S(2)}) collective-permute-start(f32[256,128]{1,0:T(8,128)} %partial_for_two_above.1), channel_id=1, source_target_pairs={{0,2},{1,3},{2,4},{3,5},{4,6},{5,7},{6,8},{7,9},{8,10},{9,11},{10,... | collective-permute-start | bytes 393224 | tf_op jit(solution)/shard_map/ppermute | solution.py:21
  109.9 0.8 copy-start.2
  113.6 0.8 copy-start.1
  114.1 0.7 copy-start.3

commit v2 on v1

v2 whole, which is shorter than its diff:
```python
import functools

import jax
import jax.numpy as jnp
from jax import lax
from jax.experimental import pallas as pl
from jax.experimental.pallas import tpu as pltpu
from jax.sharding import PartitionSpec as P

BR = 2
BS = 128
SUBS = 4
CAP_L = 19
CAPM = 6
META = 16
RING = 4
CHEAP = pl.CostEstimate(flops=0, bytes_accessed=1024, transcendentals=0)
SMEM = pl.BlockSpec(memory_space=pltpu.SMEM)
VMEM = pl.BlockSpec(memory_space=pltpu.VMEM)
ANY = pl.BlockSpec(memory_space=pl.ANY)


def by_pairs(array, pairs):
    return lax.ppermute(array, ("prow", "pcol"), pairs)


def cut_kernel(first, blocks_ref, part_ref, sem):
    copy = pltpu.make_async_copy(blocks_ref.at[pl.ds(first, part_ref.shape[0])], part_ref, sem)
    copy.start()
    copy.wait()


def cut(blocks, first, count):
    return pl.pallas_call(
        functools.partial(cut_kernel, first),
        out_shape=jax.ShapeDtypeStruct((count,) + blocks.shape[1:], blocks.dtype),
        in_specs=[ANY],
        out_specs=VMEM,
        scratch_shapes=[pltpu.SemaphoreType.DMA],
        cost_estimate=CHEAP,
        name="cut_right",
    )(blocks)


def pack_kernel(mask_ref, left_ref, after_ref, packed_ref, sem):
    del after_ref
    panel = left_ref.shape[0]
    slot = jnp.int32(0)
    for q in range(panel):
        taken = jnp.logical_and(mask_ref[q] != 0, slot < CAP_L)

        @pl.when(taken)
        def _(q=q, slot=slot):
            row = pl.multiple_of(slot * BS, BS)
            pltpu.make_async_copy(left_ref.at[q], packed_ref.at[pl.ds(row, BS)], sem).start()

        slot = slot + taken.astype(jnp.int32)

    @pl.loop(slot, CAP_L)
    def _(spare):
        row = pl.multiple_of(spare * BS, BS)
        pltpu.make_async_copy(left_ref.at[0], packed_ref.at[pl.ds(row, BS)], sem).start()

    lane = lax.broadcasted_iota(jnp.int32, (META, BS), 1)
    mask = jnp.zeros((META, BS), jnp.float32)
    for q in range(panel):
        mask = jnp.where(lane == q, (mask_ref[q] != 0).astype(jnp.float32), mask)
    packed_ref[pl.ds(CAP_L * BS, META), :] = mask.astype(packed_ref.dtype)
    blocks = packed_ref.at[pl.ds(0, CAP_L * BS)]
    pltpu.make_async_copy(blocks, blocks, sem).wait()


def pack(left_blocks, left_mask, after):
    return pl.pallas_call(
        pack_kernel,
        out_shape=jax.ShapeDtypeStruct((CAP_L * BS + META, BS), jnp.bfloat16),
        in_specs=[SMEM, ANY, ANY],
        out_specs=VMEM,
        scratch_shapes=[pltpu.SemaphoreType.DMA],
        cost_estimate=CHEAP,
        name="pack_panel",
    )(left_mask, left_blocks, after)


def mask_of(packed, panel):
    return packed[CAP_L * BS, :panel].astype(jnp.int32)


def lay_kernel(steps, flag_ref, lists_ref, counts_ref, *refs):
    masks, panels = refs[:2], refs[2 : 2 + 3]
    out_ref, rank_ref, sem = refs[5:]
    out_ref[...] = jnp.zeros_like(out_ref)
    second = flag_ref[0] != 0
    total = jnp.int32(0)
    for at, u in enumerate(steps):
        mask_ref = masks[at]
        run = jnp.int32(0)
        for q in range(mask_ref.shape[0]):
            rank_ref[q] = run
            run = run + (mask_ref[q] != 0).astype(jnp.int32)
        for p in range(lists_ref.shape[3]):
            block = lists_ref[0, u, 0, p]
            slot = lists_ref[0, u, 1, p]
            o = lists_ref[0, u, 2, p]
            live = jnp.logical_and(p < counts_ref[0, u], mask_ref[block] != 0)
            row = pl.multiple_of(jnp.minimum(rank_ref[block], CAP_L - 1) * BS, BS)
            down = pl.multiple_of(o * BS, BS)
            along = pl.multiple_of((at * CAPM + slot) * BS, BS)
            target = out_ref.at[pl.ds(down, BS), pl.ds(along, BS)]

            def fetch(panel_ref):
                pltpu.make_async_copy(panel_ref.at[pl.ds(row, BS)], target, sem).start()

            if at == 0:
                pl.when(live)(lambda: fetch(panels[0]))
            else:
                pl.when(jnp.logical_and(live, jnp.logical_not(second)))(lambda: fetch(panels[1]))
                pl.when(jnp.logical_and(live, second))(lambda: fetch(panels[2]))
            total = total + live.astype(jnp.int32)

    @pl.loop(0, total)
    def _(_):
        one = panels[0].at[pl.ds(0, BS)]
        pltpu.make_async_copy(one, out_ref.at[pl.ds(0, BS), pl.ds(0, BS)], sem).wait()


def lay(steps, flag, lists, counts, masks, panels, name):
    return pl.pallas_call(
        functools.partial(lay_kernel, steps),
        out_shape=jax.ShapeDtypeStruct((BR * BS, 2 * CAPM * BS), jnp.bfloat16),
        in_specs=[SMEM] * 5 + [ANY] * 3,
        out_specs=VMEM,
        scratch_shapes=[pltpu.SMEM((masks[0].shape[0],), jnp.int32), pltpu.SemaphoreType.DMA],
        cost_estimate=CHEAP,
        name=name,
    )(flag, lists, counts, *masks, *panels)


def on_device(n_row, n_col, left_blocks, left_mask, right_blocks, pair_lists, pair_counts):
    panel = left_blocks.shape[0]

    def shift(rows, cols, places=range(RING)):
        return [
            (r * n_col + c, (r + rows) % n_row * n_col + (c + cols) % n_col)
            for r in range(n_row)
            for c in range(n_col)
            if c % RING in places
        ]

    half = 2 * CAPM
    sent_right = cut(right_blocks, half, half)
    right_before = by_pairs(sent_right, shift(1, 0))
    packed = pack(left_blocks, left_mask, sent_right)
    two_below = by_pairs(packed, shift(0, 2))
    one_below = by_pairs(packed, shift(0, 1, range(RING - 1)))
    one_above = by_pairs(packed, shift(0, -1))
    handed = by_pairs(two_below, shift(0, -1, [1]))

    first = (lax.axis_index("pcol") % RING == 0).astype(jnp.int32).reshape(1)
    never = jnp.zeros((1,), jnp.int32)
    upper_left = lay(
        (2, 3), never, pair_lists, pair_counts,
        [left_mask, mask_of(one_above, panel)],
        [packed, one_above, one_above], "lay_upper",
    )
    mask_below = jnp.where(first != 0, mask_of(handed, panel), mask_of(one_below, panel))
    lower_left = lay(
        (0, 1), first, pair_lists, pair_counts,
        [mask_of(two_below, panel), mask_below],
        [two_below, one_below, handed], "lay_lower",
    )

    def times(left, right):
        return jnp.dot(left, right.reshape(half * BS, BS), preferred_element_type=jnp.float32)

    total = times(upper_left, right_blocks[:half]) + times(lower_left, right_before)
    return total.astype(jnp.bfloat16)


def solution(mesh):
    in_specs = (
        P(("prow", "pcol"), None, None),
        P(("prow", "pcol")),
        P(("prow", "pcol"), None, None),
        P(("prow", "pcol"), None, None, None),
        P(("prow", "pcol"), None),
    )
    return jax.shard_map(
        functools.partial(on_device, mesh.shape["prow"], mesh.shape["pcol"]),
        mesh=mesh,
        in_specs=in_specs,
        out_specs=P("prow", "pcol"),
        check_vma=False,
    )
```

time: 136 us -> 107 us (0.79)
  the two profiles are of different devices: /device:TPU:13 before, /device:TPU:2 now
where the time goes in v2:
time: 107 us; the launch traced here: 106 us
  waiting for transfers between devices  54 us (50%)
  starting transfers between devices  35.4 us (33%)
  Pallas kernels  10.1 us (9%)
  matrix products  3.72 us (3%)
  other arithmetic  1.82 us (2%)
  local copies, waits for them, and re-layouts  1.28 us (1%)
    ppermute x5, waiting for transfers between devices, by_pairs(): return lax.ppermute(array, ('prow', 'pcol'), pairs)  54 us
    ppermute x5, starting transfers between devices, by_pairs(): return lax.ppermute(array, ('prow', 'pcol'), pairs)  35.4 us
    pallas_call x2, Pallas kernels, lay(): pl.pallas_call(functools.partial(lay_kernel, steps), out_shape=jax.ShapeD...  5.56 us
    dot_general x2, matrix products, times(): jnp.dot(left, right.reshape(half * BS, BS), preferred_element_type=jnp.fl...  3.72 us
    pallas_call x1, Pallas kernels, pack(): pl.pallas_call(pack_kernel, out_shape=jax.ShapeDtypeStruct((CAP_L * BS +...  2.8 us
  transfers between devices with their start and end apart: 5, of which 3 were waited for; matrix products, arithmetic and copies ran while one was open for 4% of the time, Pallas kernels for 5%

profile of v2, /device:TPU:2, one launch (start us, length us, event | category | flops | bytes accessed | tf_op | source)
XLA Modules:
  0.0 106.4 jit_solution(704454430207165644)
XLA Ops:
  0.0 1.7 %cut_right.1.after_ref = bf16[12,128,128]{2,1,0:T(8,128)(2,1)} custom-call(bf16[24,128,128]{2,1,0:T(8,128)(2,1)} %blocks_ref.1), custom_call_target="tpu_custom_call" | custom-call | bytes 1024 | tf_op jit(solution)/shard_map/cut_right/pallas_call | solution.py:34
  1.8 0.0 copy-start.1
  1.8 0.0 copy-start.5
  1.8 2.8 %pack_panel.1.refs_2_ = bf16[2448,128]{1,0:T(8,128)(2,1)} custom-call(s32[38]{0:T(128)} %refs_0_.1, bf16[38,128,128]{2,1,0:T(8,128)(2,1)} %left_ref.1, bf16[12,128,128]{2,1,0:T(8,128)(2,1)} %cut_right.1.after_ref), custom_call_target="tpu_custom_call" | custom-call | bytes 1024 | tf_op jit(solution)/shard_map/pack_panel/pallas_call | solution.py:74
  4.6 5.1 %collective-permute-start.1 = (bf16[2448,128]{1,0:T(8,128)(2,1)}, bf16[2448,128]{1,0:T(8,128)(2,1)S(1)}, u32[]{:S(2)}, u32[]{:S(2)}) collective-permute-start(bf16[2448,128]{1,0:T(8,128)(2,1)} %pack_panel.1.refs_2_), channel_id=1, source_target_pairs={{0,2},{1,3},{2,4},{3,5},{4,6},{5,7},{6,8},{7,9},{8,10},{9,11},{10,... | collective-permute-start | bytes 1880072 | tf_op jit(solution)/shard_map/ppermute | solution.py:24
  9.7 25.8 %collective-permute-start = (bf16[2448,128]{1,0:T(8,128)(2,1)}, bf16[2448,128]{1,0:T(8,128)(2,1)S(1)}, u32[]{:S(2)}, u32[]{:S(2)}) collective-permute-start(bf16[2448,128]{1,0:T(8,128)(2,1)} %pack_panel.1.refs_2_), channel_id=1, source_target_pairs={{0,63},{1,0},{2,1},{3,2},{4,3},{5,4},{6,5},{7,6},{8,7},{9,8},{10,9... | collective-permute-start | bytes 1880072 | tf_op jit(solution)/shard_map/ppermute | solution.py:24
  35.4 1.3 %collective-permute-start.3 = (bf16[2448,128]{1,0:T(8,128)(2,1)}, bf16[2448,128]{1,0:T(8,128)(2,1)S(1)}, u32[]{:S(2)}, u32[]{:S(2)}) collective-permute-start(bf16[2448,128]{1,0:T(8,128)(2,1)} %pack_panel.1.refs_2_), channel_id=1, source_target_pairs={{0,1},{1,2},{2,3},{4,5},{5,6},{6,7},{8,9},{9,10},{10,11},{12,13},{... | collective-permute-start | bytes 1880072 | tf_op jit(solution)/shard_map/ppermute | solution.py:24
  36.8 0.0 copy-done.1
  36.8 1.9 %collective-permute-start.4 = (bf16[12,128,128]{2,1,0:T(8,128)(2,1)S(1)}, bf16[12,128,128]{2,1,0:T(8,128)(2,1)}, u32[]{:S(2)}, u32[]{:S(2)}) collective-permute-start(bf16[12,128,128]{2,1,0:T(8,128)(2,1)S(1)} %copy-done.1), channel_id=1, source_target_pairs={{0,64},{1,65},{2,66},{3,67},{4,68},{5,69},{6,70},{7,71},{8,72},{9,... | collective-permute-start | bytes 1179656 | tf_op jit(solution)/shard_map/ppermute | solution.py:24
  38.7 0.0 copy-done.5
  38.7 0.6 copy.6.lists_ref
  39.3 18.3 %collective-permute-done.1.refs_2_ = bf16[2448,128]{1,0:T(8,128)(2,1)S(1)} collective-permute-done((bf16[2448,128]{1,0:T(8,128)(2,1)}, bf16[2448,128]{1,0:T(8,128)(2,1)S(1)}, u32[]{:S(2)}, u32[]{:S(2)}) %collective-permute-start.1) | collective-permute-done | bytes 626720 | tf_op jit(solution)/shard_map/ppermute | solution.py:24
  57.7 0.0 copy-start.4
  57.7 1.3 %collective-permute-start.2 = (bf16[2448,128]{1,0:T(8,128)(2,1)S(1)}, bf16[2448,128]{1,0:T(8,128)(2,1)S(1)}, u32[]{:S(2)}, u32[]{:S(2)}) collective-permute-start(bf16[2448,128]{1,0:T(8,128)(2,1)S(1)} %collective-permute-done.1.refs_2_), channel_id=1, source_target_pairs={{1,0},{5,4},{9,8},{13,12},{17,16},{21,20},{25,24},{29,28},{33,32},... | collective-permute-start | bytes 1880072 | tf_op jit(solution)/shard_map/ppermute | solution.py:24
  59.0 20.8 %collective-permute-done.refs_3_.refs_4_ = bf16[2448,128]{1,0:T(8,128)(2,1)S(1)} collective-permute-done((bf16[2448,128]{1,0:T(8,128)(2,1)}, bf16[2448,128]{1,0:T(8,128)(2,1)S(1)}, u32[]{:S(2)}, u32[]{:S(2)}) %collective-permute-start) | collective-permute-done | bytes 626720 | tf_op jit(solution)/shard_map/ppermute | solution.py:24
  79.8 0.0 copy-start
  79.8 0.6 fusion.3.refs_1_
  80.4 0.2 copy-done
  80.6 0.0 slice-start
  80.6 2.9 %lay_upper.1 = bf16[256,1536]{1,0:T(8,128)(2,1)} custom-call(s32[1]{0:T(128)} %constant.15.clone.1.flag_ref, s32[1,4,3,12]{3,2,1,0:T(4,128)} %copy.6.lists_ref, s32[1,4]{1,0:T(1,128)} %counts_ref.3, s32[38]{0:T(128)} %refs_0_.1, s32[38]{0:T(128)} %fusion.3.refs_1_, bf16[2448,128]{1,0:T(8,128)(2,1)} %pack_panel.1.refs_2_, bf16[2448,128]{1,0:T(8,128)(2,1)} %copy-done, ...), custom_call_target="tpu_custom_call" | custom-call | bytes 1024 | tf_op jit(solution)/shard_map/lay_upper/pallas_call | solution.py:128
  83.5 0.0 slice-done
  83.5 1.5 %fusion.4 = f32[256,128]{1,0:T(8,128)S(1)} fusion(bf16[256,1536]{1,0:T(8,128)(2,1)} %lay_upper.1, bf16[1536,128]{1,0:T(8,128)(2,1)S(1)} %bitcast.20), kind=kOutput, calls=%fused_computation.10 | convolution fusion | flops 100663296 | bytes 1310720 | tf_op jit(solution)/shard_map/dot_general | solution.py:174
  85.0 0.6 fusion.2.refs_0_
  85.6 0.0 collective-permute-done.3.refs_3_
  85.6 0.0 copy-start.2
  85.6 0.0 collective-permute-done.2.refs_4_
  85.6 0.0 copy-start.3
  85.6 0.6 fusion.1.refs_1_
  86.2 0.0 copy-done.4
  86.2 0.2 copy-done.2
  86.4 0.2 copy-done.3
  86.7 2.7 %lay_lower.1 = bf16[256,1536]{1,0:T(8,128)(2,1)} custom-call(s32[1]{0:T(128)} %bitcast.2.flag_ref, s32[1,4,3,12]{3,2,1,0:T(4,128)} %copy.6.lists_ref, s32[1,4]{1,0:T(1,128)} %counts_ref.3, s32[38]{0:T(128)} %fusion.2.refs_0_, s32[38]{0:T(128)} %fusion.1.refs_1_, bf16[2448,128]{1,0:T(8,128)(2,1)} %copy-done.4, bf16[2448,128]{1,0:T(8,128)(2,1)} %copy-done.2, ...), custom_call_target="tpu_custom_call" | custom-call | bytes 1024 | tf_op jit(solution)/shard_map/lay_lower/pallas_call | solution.py:128
  89.4 14.8 %collective-permute-done.4 = bf16[12,128,128]{2,1,0:T(8,128)(2,1)} collective-permute-done((bf16[12,128,128]{2,1,0:T(8,128)(2,1)S(1)}, bf16[12,128,128]{2,1,0:T(8,128)(2,1)}, u32[]{:S(2)}, u32[]{:S(2)}) %collective-permute-start.4) | collective-permute-done | bytes 393248 | tf_op jit(solution)/shard_map/ppermute | solution.py:24
  104.2 2.2 %fusion = bf16[256,128]{1,0:T(8,128)(2,1)} fusion(f32[256,128]{1,0:T(8,128)S(1)} %fusion.4, bf16[256,1536]{1,0:T(8,128)(2,1)} %lay_lower.1, bf16[1536,128]{1,0:T(8,128)(2,1)} %bitcast.6), kind=kOutput, calls=%fused_computation.1 | convolution fusion | flops 100728832 | bytes 1376256 | tf_op jit(solution)/shard_map/dot_general | solution.py:174
Async XLA Ops:
  1.8 35.0 %copy-start.1 = (bf16[12,128,128]{2,1,0:T(8,128)(2,1)S(1)}, bf16[12,128,128]{2,1,0:T(8,128)(2,1)}, u32[]{:S(2)}) copy-start(bf16[12,128,128]{2,1,0:T(8,128)(2,1)} %cut_right.1.after_ref) | copy-start | bytes 1179652
  1.8 37.0 %copy-start.5 = (s32[1,4,3,12]{3,1,2,0:T(4,128)S(1)}, s32[1,4,3,12]{3,1,2,0:T(4,128)}, u32[]{:S(2)}) copy-start(s32[1,4,3,12]{3,1,2,0:T(4,128)} %param.8) | copy-start | bytes 1732
  4.6 53.1 %collective-permute-start.1 = (bf16[2448,128]{1,0:T(8,128)(2,1)}, bf16[2448,128]{1,0:T(8,128)(2,1)S(1)}, u32[]{:S(2)}, u32[]{:S(2)}) collective-permute-start(bf16[2448,128]{1,0:T(8,128)(2,1)} %pack_panel.1.refs_2_), channel_id=1, source_target_pairs={{0,2},{1,3},{2,4},{3,5},{4,6},{5,7},{6,8},{7,9},{8,10},{9,11},{10,... | collective-permute-start | bytes 1880072 | tf_op jit(solution)/shard_map/ppermute | solution.py:24
  9.7 70.1 %collective-permute-start = (bf16[2448,128]{1,0:T(8,128)(2,1)}, bf16[2448,128]{1,0:T(8,128)(2,1)S(1)}, u32[]{:S(2)}, u32[]{:S(2)}) collective-permute-start(bf16[2448,128]{1,0:T(8,128)(2,1)} %pack_panel.1.refs_2_), channel_id=1, source_target_pairs={{0,63},{1,0},{2,1},{3,2},{4,3},{5,4},{6,5},{7,6},{8,7},{9,8},{10,9... | collective-permute-start | bytes 1880072 | tf_op jit(solution)/shard_map/ppermute | solution.py:24
  35.4 50.2 %collective-permute-start.3 = (bf16[2448,128]{1,0:T(8,128)(2,1)}, bf16[2448,128]{1,0:T(8,128)(2,1)S(1)}, u32[]{:S(2)}, u32[]{:S(2)}) collective-permute-start(bf16[2448,128]{1,0:T(8,128)(2,1)} %pack_panel.1.refs_2_), channel_id=1, source_target_pairs={{0,1},{1,2},{2,3},{4,5},{5,6},{6,7},{8,9},{9,10},{10,11},{12,13},{... | collective-permute-start | bytes 1880072 | tf_op jit(solution)/shard_map/ppermute | solution.py:24
  36.8 67.4 %collective-permute-start.4 = (bf16[12,128,128]{2,1,0:T(8,128)(2,1)S(1)}, bf16[12,128,128]{2,1,0:T(8,128)(2,1)}, u32[]{:S(2)}, u32[]{:S(2)}) collective-permute-start(bf16[12,128,128]{2,1,0:T(8,128)(2,1)S(1)} %copy-done.1), channel_id=1, source_target_pairs={{0,64},{1,65},{2,66},{3,67},{4,68},{5,69},{6,70},{7,71},{8,72},{9,... | collective-permute-start | bytes 1179656 | tf_op jit(solution)/shard_map/ppermute | solution.py:24
  57.7 28.5 %copy-start.4 = (bf16[2448,128]{1,0:T(8,128)(2,1)}, bf16[2448,128]{1,0:T(8,128)(2,1)S(1)}, u32[]{:S(2)}) copy-start(bf16[2448,128]{1,0:T(8,128)(2,1)S(1)} %collective-permute-done.1.refs_2_) | copy-start | bytes 1880068
  57.7 27.9 %collective-permute-start.2 = (bf16[2448,128]{1,0:T(8,128)(2,1)S(1)}, bf16[2448,128]{1,0:T(8,128)(2,1)S(1)}, u32[]{:S(2)}, u32[]{:S(2)}) collective-permute-start(bf16[2448,128]{1,0:T(8,128)(2,1)S(1)} %collective-permute-done.1.refs_2_), channel_id=1, source_target_pairs={{1,0},{5,4},{9,8},{13,12},{17,16},{21,20},{25,24},{29,28},{33,32},... | collective-permute-start | bytes 1880072 | tf_op jit(solution)/shard_map/ppermute | solution.py:24
  79.8 0.9 copy-start
  80.6 2.9 %slice-start = ((bf16[24,128,128]{2,1,0:T(8,128)(2,1)}), bf16[12,128,128]{2,1,0:T(8,128)(2,1)S(1)}, s32[]{:S(2)}) async-start(bf16[24,128,128]{2,1,0:T(8,128)(2,1)} %blocks_ref.1), calls=%async_computation | async-start | bytes 786432 | tf_op jit(solution)/shard_map/slice | solution.py:176
  85.6 0.8 copy-start.2
  85.6 1.1 copy-start.3

commit v3 on v2

v3 whole, which is shorter than its diff:
```python
import functools

import jax
import jax.numpy as jnp
from jax import lax
from jax.experimental import pallas as pl
from jax.experimental.pallas import tpu as pltpu
from jax.sharding import PartitionSpec as P

BR = 2
BS = 128
SUBS = 4
CAP_L = 19
CAPM = 6
META = 16
RING = 4
CHEAP = pl.CostEstimate(flops=0, bytes_accessed=1024, transcendentals=0)
SMEM = pl.BlockSpec(memory_space=pltpu.SMEM)
VMEM = pl.BlockSpec(memory_space=pltpu.VMEM)
ANY = pl.BlockSpec(memory_space=pl.ANY)


def by_pairs(array, pairs):
    return lax.ppermute(array, ("prow", "pcol"), pairs)


def stage_kernel(mask_ref, left_ref, right_ref, packed_ref, part_ref, sem, part_sem):
    panel = left_ref.shape[0]
    half = part_ref.shape[0]
    part = pltpu.make_async_copy(right_ref.at[pl.ds(half, half)], part_ref, part_sem)
    part.start()
    slot = jnp.int32(0)
    for q in range(panel):
        taken = jnp.logical_and(mask_ref[q] != 0, slot < CAP_L)

        @pl.when(taken)
        def _(q=q, slot=slot):
            row = pl.multiple_of(slot * BS, BS)
            pltpu.make_async_copy(left_ref.at[q], packed_ref.at[pl.ds(row, BS)], sem).start()

        slot = slot + taken.astype(jnp.int32)

    @pl.loop(slot, CAP_L)
    def _(spare):
        row = pl.multiple_of(spare * BS, BS)
        pltpu.make_async_copy(left_ref.at[0], packed_ref.at[pl.ds(row, BS)], sem).start()

    lane = lax.broadcasted_iota(jnp.int32, (META, BS), 1)
    mask = jnp.zeros((META, BS), jnp.float32)
    for q in range(panel):
        mask = jnp.where(lane == q, (mask_ref[q] != 0).astype(jnp.float32), mask)
    packed_ref[pl.ds(CAP_L * BS, META), :] = mask.astype(packed_ref.dtype)
    blocks = packed_ref.at[pl.ds(0, CAP_L * BS)]
    pltpu.make_async_copy(blocks, blocks, sem).wait()
    part.wait()


def stage(left_mask, left_blocks, right_blocks):
    return pl.pallas_call(
        stage_kernel,
        out_shape=[
            jax.ShapeDtypeStruct((CAP_L * BS + META, BS), jnp.bfloat16),
            jax.ShapeDtypeStruct((2 * CAPM, BS, BS), jnp.bfloat16),
        ],
        in_specs=[SMEM, ANY, ANY],
        out_specs=[VMEM, VMEM],
        scratch_shapes=[pltpu.SemaphoreType.DMA, pltpu.SemaphoreType.DMA],
        cost_estimate=CHEAP,
        name="pack_and_cut",
    )(left_mask, left_blocks, right_blocks)


def mask_of(packed, panel):
    return packed[CAP_L * BS, :panel].astype(jnp.int32)


def lay_kernel(steps, lists_ref, counts_ref, *refs):
    masks, panels = refs[: len(steps)], refs[len(steps) : -3]
    out_ref, rank_ref, sem = refs[-3:]
    out_ref[...] = jnp.zeros_like(out_ref)
    column = lax.axis_index("pcol")
    total = jnp.int32(0)
    for at, (u, sources) in enumerate(steps):
        mask_ref = masks[at]
        run = jnp.int32(0)
        for q in range(mask_ref.shape[0]):
            rank_ref[q] = run
            run = run + (mask_ref[q] != 0).astype(jnp.int32)
        held = [(panels[i], where(column)) for i, where in sources]
        for p in range(lists_ref.shape[3]):
            block = lists_ref[0, u, 0, p]
            slot = lists_ref[0, u, 1, p]
            o = lists_ref[0, u, 2, p]
            live = jnp.logical_and(p < counts_ref[0, u], mask_ref[block] != 0)
            row = pl.multiple_of(jnp.minimum(rank_ref[block], CAP_L - 1) * BS, BS)
            down = pl.multiple_of(o * BS, BS)
            along = pl.multiple_of((at * CAPM + slot) * BS, BS)
            target = out_ref.at[pl.ds(down, BS), pl.ds(along, BS)]
            for panel_ref, here in held:
                taken = jnp.logical_and(live, here)

                @pl.when(taken)
                def _(panel_ref=panel_ref, row=row, target=target):
                    pltpu.make_async_copy(panel_ref.at[pl.ds(row, BS)], target, sem).start()

                total = total + taken.astype(jnp.int32)

    @pl.loop(0, total)
    def _(_):
        one = panels[0].at[pl.ds(0, BS)]
        pltpu.make_async_copy(one, out_ref.at[pl.ds(0, BS), pl.ds(0, BS)], sem).wait()


def lay(steps, lists, counts, masks, panels, name):
    return pl.pallas_call(
        functools.partial(lay_kernel, steps),
        out_shape=jax.ShapeDtypeStruct((BR * BS, len(steps) * CAPM * BS), jnp.bfloat16),
        in_specs=[SMEM] * (2 + len(masks)) + [ANY] * len(panels),
        out_specs=VMEM,
        scratch_shapes=[pltpu.SMEM((masks[0].shape[0],), jnp.int32), pltpu.SemaphoreType.DMA],
        cost_estimate=CHEAP,
        name=name,
    )(lists, counts, *masks, *panels)


def finish_kernel(steps, lists_ref, counts_ref, *refs):
    masks, panels, rights = refs[:2], refs[2:4], refs[4:6]
    known_ref, new_ref, out_ref, left_ref, right_ref, total_ref, rank_ref, sems = refs[6:]
    column = lax.axis_index("pcol")
    total_ref[...] = known_ref[...] + new_ref[...]
    for u, which, (side, first), here in steps:

        @pl.when(here(column))
        def _(u=u, which=which, side=side, first=first):
            part = rights[side].at[pl.ds(first * CAPM, CAPM)]
            fetch_right = pltpu.make_async_copy(part, right_ref, sems.at[0])
            fetch_right.start()
            left_ref[...] = jnp.zeros_like(left_ref)
            run = jnp.int32(0)
            for q in range(masks[which].shape[0]):
                rank_ref[q] = run
                run = run + (masks[which][q] != 0).astype(jnp.int32)
            count = jnp.int32(0)
            for p in range(lists_ref.shape[3]):
                block = lists_ref[0, u, 0, p]
                live = jnp.logical_and(p < counts_ref[0, u], masks[which][block] != 0)
                row = pl.multiple_of(jnp.minimum(rank_ref[block], CAP_L - 1) * BS, BS)
                along = pl.multiple_of(lists_ref[0, u, 1, p] * BS, BS)
                down = pl.multiple_of(lists_ref[0, u, 2, p] * BS, BS)

                @pl.when(live)
                def _(row=row, down=down, along=along):
                    target = left_ref.at[pl.ds(down, BS), pl.ds(along, BS)]
                    source = panels[which].at[pl.ds(row, BS)]
                    pltpu.make_async_copy(source, target, sems.at[1]).start()

                count = count + live.astype(jnp.int32)

            @pl.loop(0, count)
            def _(_):
                one = panels[which].at[pl.ds(0, BS)]
                target = left_ref.at[pl.ds(0, BS), pl.ds(0, BS)]
                pltpu.make_async_copy(one, target, sems.at[1]).wait()

            fetch_right.wait()
            for m in range(CAPM):
                total_ref[...] += jnp.dot(
                    left_ref[:, m * BS : (m + 1) * BS],
                    right_ref[m],
                    preferred_element_type=jnp.float32,
                )

    out_ref[...] = total_ref[...].astype(out_ref.dtype)


def finish(steps, lists, counts, masks, panels, rights, known, new):
    return pl.pallas_call(
        functools.partial(finish_kernel, steps),
        out_shape=jax.ShapeDtypeStruct(new.shape, jnp.bfloat16),
        in_specs=[SMEM] * 4 + [ANY] * 4 + [VMEM] * 2,
        out_specs=VMEM,
        scratch_shapes=[
            pltpu.VMEM((BR * BS, CAPM * BS), jnp.bfloat16),
            pltpu.VMEM((CAPM, BS, BS), jnp.bfloat16),
            pltpu.VMEM(new.shape, jnp.float32),
            pltpu.SMEM((masks[0].shape[0],), jnp.int32),
            pltpu.SemaphoreType.DMA((2,)),
        ],
        cost_estimate=CHEAP,
        name="finish",
    )(lists, counts, *masks, *panels, *rights, known, new)


def on_device(n_row, n_col, left_blocks, left_mask, right_blocks, pair_lists, pair_counts):
    panel = left_blocks.shape[0]
    last = n_col - 1
    half = 2 * CAPM

    def shift(rows, cols, chosen):
        return [
            (r * n_col + c, (r + rows) % n_row * n_col + (c + cols) % n_col)
            for r in range(n_row)
            for c in range(n_col)
            if chosen(c)
        ]

    packed, sent_right = stage(left_mask, left_blocks, right_blocks)
    two_below = by_pairs(packed, shift(0, 2, lambda c: c < last - 1))
    one_above = by_pairs(packed, shift(0, -1, lambda c: c > 0))
    one_below = by_pairs(packed, shift(0, 1, lambda c: c % RING < RING - 1))
    right_before = by_pairs(sent_right, shift(1, 0, lambda c: True))
    column = lax.axis_index("pcol")
    passed = jnp.where(jnp.logical_or(column % RING == 1, column == 2), two_below, packed)
    handed = by_pairs(
        passed,
        shift(0, -1, lambda c: c % RING == 1 and c != 1)
        + shift(0, 2, lambda c: c >= last - 1)
        + shift(0, -3, lambda c: c == 2),
    )
    around = by_pairs(passed, shift(0, 1, lambda c: c == last))

    laid = lay(
        (
            (0, ((0, lambda c: c >= 2),)),
            (1, ((1, lambda c: lax.rem(c, RING) != 0),)),
            (2, ((2, lambda c: c >= 0),)),
            (3, ((3, lambda c: c < last),)),
        ),
        pair_lists, pair_counts,
        [mask_of(two_below, panel), mask_of(one_below, panel), left_mask, mask_of(one_above, panel)],
        [two_below, one_below, packed, one_above], "lay_left",
    )

    def times(left, right):
        return jnp.dot(left, right.reshape(half * BS, BS), preferred_element_type=jnp.float32)

    known = times(laid[:, half * BS :], right_blocks[:half])
    new = times(laid[:, : half * BS], right_before)
    return finish(
        (
            (0, 1, (0, 0), lambda c: c < 2),
            (1, 1, (0, 1), lambda c: jnp.logical_and(lax.rem(c, RING) == 0, c != 0)),
            (1, 0, (0, 1), lambda c: c == 0),
            (3, 1, (1, 1), lambda c: c == last),
        ),
        pair_lists, pair_counts,
        [mask_of(around, panel), mask_of(handed, panel)],
        [around, handed], [right_before, right_blocks], known, new,
    )


def solution(mesh):
    in_specs = (
        P(("prow", "pcol"), None, None),
        P(("prow", "pcol")),
        P(("prow", "pcol"), None, None),
        P(("prow", "pcol"), None, None, None),
        P(("prow", "pcol"), None),
    )
    return jax.shard_map(
        functools.partial(on_device, mesh.shape["prow"], mesh.shape["pcol"]),
        mesh=mesh,
        in_specs=in_specs,
        out_specs=P("prow", "pcol"),
        check_vma=False,
    )
```

time: 107 us -> 111 us (1.037)
  the two profiles are of different devices: /device:TPU:2 before, /device:TPU:1 now
where the time goes in v3:
time: 111 us; the launch traced here: 109 us
  starting transfers between devices  44.6 us (40%)
  waiting for transfers between devices  43.9 us (40%)
  Pallas kernels  10.6 us (10%)
  other arithmetic  4.86 us (4%)
  matrix products  4.37 us (4%)
    ppermute x6, starting transfers between devices, by_pairs(): return lax.ppermute(array, ('prow', 'pcol'), pairs)  44.6 us
    ppermute x6, waiting for transfers between devices, by_pairs(): return lax.ppermute(array, ('prow', 'pcol'), pairs)  43.9 us
    dot_general x2, matrix products, times(): jnp.dot(left, right.reshape(half * BS, BS), preferred_element_type=jnp.fl...  4.37 us
    pallas_call x1, Pallas kernels, finish(): pl.pallas_call(functools.partial(finish_kernel, steps), out_shape=jax.Sha...  4 us
    pallas_call x1, Pallas kernels, lay(): pl.pallas_call(functools.partial(lay_kernel, steps), out_shape=jax.ShapeD...  3.52 us
    convert_element_type x5, other arithmetic, mask_of(): return packed[CAP_L * BS, :panel].astype(jnp.int32)  3.49 us
    pallas_call x1, Pallas kernels, stage(): pl.pallas_call(stage_kernel, out_shape=[jax.ShapeDtypeStruct((CAP_L * BS...  3.06 us
  transfers between devices with their start and end apart: 6, of which 3 were waited for; matrix products, arithmetic and copies ran while one was open for 8% of the time, Pallas kernels for 3%

profile of v3, /device:TPU:1, one launch (start us, length us, event | category | flops | bytes accessed | tf_op | source)
XLA Modules:
  0.0 109.3 jit_solution(5747941246380029729)
XLA Ops:
  0.0 0.0 copy-start.4
  0.0 3.1 %pack_and_cut.1 = (bf16[2448,128]{1,0:T(8,128)(2,1)}, bf16[12,128,128]{2,1,0:T(8,128)(2,1)}) custom-call(s32[38]{0:T(128)} %refs_2_.1, bf16[38,128,128]{2,1,0:T(8,128)(2,1)} %left_ref.1, bf16[24,128,128]{2,1,0:T(8,128)(2,1)} %refs_5_.1), custom_call_target="tpu_custom_call" | custom-call | bytes 1024 | tf_op jit(solution)/shard_map/pack_and_cut/pallas_call | solution.py:59
  3.1 5.8 %collective-permute-start = (bf16[2448,128]{1,0:T(8,128)(2,1)}, bf16[2448,128]{1,0:T(8,128)(2,1)S(1)}, u32[]{:S(2)}, u32[]{:S(2)}) collective-permute-start(bf16[2448,128]{1,0:T(8,128)(2,1)} %get-tuple-element.7.refs_6_), channel_id=1, source_target_pairs={{0,2},{1,3},{2,4},{3,5},{4,6},{5,7},{6,8},{7,9},{8,10},{9,11},{10,... | collective-permute-start | bytes 1880072 | tf_op jit(solution)/shard_map/ppermute | solution.py:24
  8.9 1.3 %collective-permute-start.5 = (bf16[2448,128]{1,0:T(8,128)(2,1)}, bf16[2448,128]{1,0:T(8,128)(2,1)S(1)}, u32[]{:S(2)}, u32[]{:S(2)}) collective-permute-start(bf16[2448,128]{1,0:T(8,128)(2,1)} %get-tuple-element.7.refs_6_), channel_id=1, source_target_pairs={{1,0},{2,1},{3,2},{4,3},{5,4},{6,5},{7,6},{8,7},{9,8},{10,9},{11,1... | collective-permute-start | bytes 1880072 | tf_op jit(solution)/shard_map/ppermute | solution.py:24
  10.2 4.8 %collective-permute-start.4 = (bf16[2448,128]{1,0:T(8,128)(2,1)}, bf16[2448,128]{1,0:T(8,128)(2,1)}, u32[]{:S(2)}, u32[]{:S(2)}) collective-permute-start(bf16[2448,128]{1,0:T(8,128)(2,1)} %get-tuple-element.7.refs_6_), channel_id=1, source_target_pairs={{0,1},{1,2},{2,3},{4,5},{5,6},{6,7},{8,9},{9,10},{10,11},{12,13},{... | collective-permute-start | bytes 1880072 | tf_op jit(solution)/shard_map/ppermute | solution.py:24
  15.0 30.1 %collective-permute-start.3 = (bf16[12,128,128]{2,1,0:T(8,128)(2,1)}, bf16[12,128,128]{2,1,0:T(8,128)(2,1)}, u32[]{:S(2)}, u32[]{:S(2)}) collective-permute-start(bf16[12,128,128]{2,1,0:T(8,128)(2,1)} %get-tuple-element.8), channel_id=1, source_target_pairs={{0,64},{1,65},{2,66},{3,67},{4,68},{5,69},{6,70},{7,71},{8,72},{9,... | collective-permute-start | bytes 1179656 | tf_op jit(solution)/shard_map/ppermute | solution.py:24
  45.2 0.0 copy-done.4
  45.2 0.6 copy.7.lists_ref
  45.8 0.0 collective-permute-done.refs_4_
  45.8 0.0 copy-start
  45.8 1.4 %broadcast_select_fusion = bf16[2448,128]{1,0:T(8,128)(2,1)S(1)} fusion(bf16[2448,128]{1,0:T(8,128)(2,1)S(1)} %collective-permute-done.refs_4_, bf16[2448,128]{1,0:T(8,128)(2,1)} %get-tuple-element.7.refs_6_, pred[]{:T(512)S(6)} %or.3), kind=kLoop, calls=%fused_computation.4 | loop fusion | flops 313344 | bytes 1880065 | tf_op jit(solution)/shard_map/jit(_where)/select_n | solution.py:213
  47.1 1.3 %collective-permute-start.2 = (bf16[2448,128]{1,0:T(8,128)(2,1)S(1)}, bf16[2448,128]{1,0:T(8,128)(2,1)S(1)}, u32[]{:S(2)}, u32[]{:S(2)}) collective-permute-start(bf16[2448,128]{1,0:T(8,128)(2,1)S(1)} %broadcast_select_fusion), channel_id=1, source_target_pairs={{5,4},{9,8},{13,12},{17,16},{21,20},{25,24},{29,28},{33,32},{37,36... | collective-permute-start | bytes 1880072 | tf_op jit(solution)/shard_map/ppermute | solution.py:24
  48.4 1.3 %collective-permute-start.1 = (bf16[2448,128]{1,0:T(8,128)(2,1)S(1)}, bf16[2448,128]{1,0:T(8,128)(2,1)S(1)}, u32[]{:S(2)}, u32[]{:S(2)}) collective-permute-start(bf16[2448,128]{1,0:T(8,128)(2,1)S(1)} %broadcast_select_fusion), channel_id=1, source_target_pairs={{63,0},{127,64},{191,128},{255,192},{319,256},{383,320},{447,384},... | collective-permute-start | bytes 1880072 | tf_op jit(solution)/shard_map/ppermute | solution.py:24
  49.7 0.5 fusion.6.refs_0_
  50.3 0.0 collective-permute-done.5.refs_7_
  50.3 0.0 copy-start.3
  50.3 0.6 fusion.4.refs_3_
  50.8 0.0 collective-permute-done.4.refs_5_
  50.8 1.2 %fusion.5.refs_1_ = s32[38]{0:T(128)} fusion(bf16[2448,128]{1,0:T(8,128)(2,1)} %collective-permute-done.4.refs_5_), kind=kLoop, calls=%fused_computation.8 | loop fusion | flops 38 | bytes 228 | tf_op jit(solution)/shard_map/convert_element_type | solution.py:74
  52.1 0.0 copy-done
  52.1 0.0 copy-done.3
  52.1 0.0 slice-start
  52.1 3.5 %lay_left.1 = bf16[256,3072]{1,0:T(8,128)(2,1)} custom-call(s32[1,4,3,12]{3,2,1,0:T(4,128)} %copy.7.lists_ref, s32[1,4]{1,0:T(1,128)} %counts_ref.3, s32[38]{0:T(128)} %fusion.6.refs_0_, s32[38]{0:T(128)} %fusion.5.refs_1_, s32[38]{0:T(128)} %refs_2_.1, s32[38]{0:T(128)} %fusion.4.refs_3_, bf16[2448,128]{1,0:T(8,128)(2,1)} %copy-done, ...), custom_call_target="tpu_custom_call" | custom-call | bytes 1024 | tf_op jit(solution)/shard_map/lay_left/pallas_call | solution.py:115
  55.6 0.0 slice-done
  55.6 2.1 %fusion.2.refs_6_ = f32[256,128]{1,0:T(8,128)} fusion(bf16[1536,128]{1,0:T(8,128)(2,1)S(1)} %bitcast.29, bf16[256,3072]{1,0:T(8,128)(2,1)} %lay_left.1), kind=kOutput, calls=%fused_computation.2 | convolution fusion | flops 100663296 | bytes 1310720 | tf_op jit(solution)/shard_map/dot_general | solution.py:235
  57.7 19.4 %collective-permute-done.3.refs_4_ = bf16[12,128,128]{2,1,0:T(8,128)(2,1)} collective-permute-done((bf16[12,128,128]{2,1,0:T(8,128)(2,1)}, bf16[12,128,128]{2,1,0:T(8,128)(2,1)}, u32[]{:S(2)}, u32[]{:S(2)}) %collective-permute-start.3) | collective-permute-done | bytes 393248 | tf_op jit(solution)/shard_map/ppermute | solution.py:24
  77.2 2.2 %fusion.refs_7_ = f32[256,128]{1,0:T(8,128)} fusion(bf16[1536,128]{1,0:T(8,128)(2,1)} %bitcast.6, bf16[256,3072]{1,0:T(8,128)(2,1)} %lay_left.1), kind=kOutput, calls=%fused_computation | convolution fusion | flops 100663296 | bytes 1310720 | tf_op jit(solution)/shard_map/dot_general | solution.py:235
  79.4 17.4 %collective-permute-done.2.refs_3_ = bf16[2448,128]{1,0:T(8,128)(2,1)S(1)} collective-permute-done((bf16[2448,128]{1,0:T(8,128)(2,1)S(1)}, bf16[2448,128]{1,0:T(8,128)(2,1)S(1)}, u32[]{:S(2)}, u32[]{:S(2)}) %collective-permute-start.2) | collective-permute-done | bytes 626720 | tf_op jit(solution)/shard_map/ppermute | solution.py:24
  96.8 0.0 copy-start.1
  96.8 0.6 fusion.7.refs_1_
  97.4 7.1 %collective-permute-done.1.refs_2_ = bf16[2448,128]{1,0:T(8,128)(2,1)S(1)} collective-permute-done((bf16[2448,128]{1,0:T(8,128)(2,1)S(1)}, bf16[2448,128]{1,0:T(8,128)(2,1)S(1)}, u32[]{:S(2)}, u32[]{:S(2)}) %collective-permute-start.1) | collective-permute-done | bytes 626720 | tf_op jit(solution)/shard_map/ppermute | solution.py:24
  104.5 0.0 copy-start.2
  104.5 0.6 fusion.8.refs_0_
  105.1 0.0 copy-done.1
  105.1 0.2 copy-done.2
  105.3 4.0 %finish.1 = bf16[256,128]{1,0:T(8,128)(2,1)} custom-call(s32[1,4,3,12]{3,2,1,0:T(4,128)} %copy.7.lists_ref, s32[1,4]{1,0:T(1,128)} %counts_ref.3, s32[38]{0:T(128)} %fusion.8.refs_0_, s32[38]{0:T(128)} %fusion.7.refs_1_, bf16[2448,128]{1,0:T(8,128)(2,1)} %copy-done.2, bf16[2448,128]{1,0:T(8,128)(2,1)} %copy-done.1, ...), custom_call_target="tpu_custom_call" | custom-call | bytes 1024 | tf_op jit(solution)/shard_map/finish/pallas_call | solution.py:177
Async XLA Ops:
  0.0 45.2 %copy-start.4 = (s32[1,4,3,12]{3,1,2,0:T(4,128)S(1)}, s32[1,4,3,12]{3,1,2,0:T(4,128)}, u32[]{:S(2)}) copy-start(s32[1,4,3,12]{3,1,2,0:T(4,128)} %param.8) | copy-start | bytes 1732
  3.1 42.7 %collective-permute-start = (bf16[2448,128]{1,0:T(8,128)(2,1)}, bf16[2448,128]{1,0:T(8,128)(2,1)S(1)}, u32[]{:S(2)}, u32[]{:S(2)}) collective-permute-start(bf16[2448,128]{1,0:T(8,128)(2,1)} %get-tuple-element.7.refs_6_), channel_id=1, source_target_pairs={{0,2},{1,3},{2,4},{3,5},{4,6},{5,7},{6,8},{7,9},{8,10},{9,11},{10,... | collective-permute-start | bytes 1880072 | tf_op jit(solution)/shard_map/ppermute | solution.py:24
  8.9 41.4 %collective-permute-start.5 = (bf16[2448,128]{1,0:T(8,128)(2,1)}, bf16[2448,128]{1,0:T(8,128)(2,1)S(1)}, u32[]{:S(2)}, u32[]{:S(2)}) collective-permute-start(bf16[2448,128]{1,0:T(8,128)(2,1)} %get-tuple-element.7.refs_6_), channel_id=1, source_target_pairs={{1,0},{2,1},{3,2},{4,3},{5,4},{6,5},{7,6},{8,7},{9,8},{10,9},{11,1... | collective-permute-start | bytes 1880072 | tf_op jit(solution)/shard_map/ppermute | solution.py:24
  10.2 40.7 %collective-permute-start.4 = (bf16[2448,128]{1,0:T(8,128)(2,1)}, bf16[2448,128]{1,0:T(8,128)(2,1)}, u32[]{:S(2)}, u32[]{:S(2)}) collective-permute-start(bf16[2448,128]{1,0:T(8,128)(2,1)} %get-tuple-element.7.refs_6_), channel_id=1, source_target_pairs={{0,1},{1,2},{2,3},{4,5},{5,6},{6,7},{8,9},{9,10},{10,11},{12,13},{... | collective-permute-start | bytes 1880072 | tf_op jit(solution)/shard_map/ppermute | solution.py:24
  15.0 62.2 %collective-permute-start.3 = (bf16[12,128,128]{2,1,0:T(8,128)(2,1)}, bf16[12,128,128]{2,1,0:T(8,128)(2,1)}, u32[]{:S(2)}, u32[]{:S(2)}) collective-permute-start(bf16[12,128,128]{2,1,0:T(8,128)(2,1)} %get-tuple-element.8), channel_id=1, source_target_pairs={{0,64},{1,65},{2,66},{3,67},{4,68},{5,69},{6,70},{7,71},{8,72},{9,... | collective-permute-start | bytes 1179656 | tf_op jit(solution)/shard_map/ppermute | solution.py:24
  45.8 6.3 %copy-start = (bf16[2448,128]{1,0:T(8,128)(2,1)}, bf16[2448,128]{1,0:T(8,128)(2,1)S(1)}, u32[]{:S(2)}) copy-start(bf16[2448,128]{1,0:T(8,128)(2,1)S(1)} %collective-permute-done.refs_4_) | copy-start | bytes 1880068
  47.1 49.6 %collective-permute-start.2 = (bf16[2448,128]{1,0:T(8,128)(2,1)S(1)}, bf16[2448,128]{1,0:T(8,128)(2,1)S(1)}, u32[]{:S(2)}, u32[]{:S(2)}) collective-permute-start(bf16[2448,128]{1,0:T(8,128)(2,1)S(1)} %broadcast_select_fusion), channel_id=1, source_target_pairs={{5,4},{9,8},{13,12},{17,16},{21,20},{25,24},{29,28},{33,32},{37,36... | collective-permute-start | bytes 1880072 | tf_op jit(solution)/shard_map/ppermute | solution.py:24
  48.4 56.1 %collective-permute-start.1 = (bf16[2448,128]{1,0:T(8,128)(2,1)S(1)}, bf16[2448,128]{1,0:T(8,128)(2,1)S(1)}, u32[]{:S(2)}, u32[]{:S(2)}) collective-permute-start(bf16[2448,128]{1,0:T(8,128)(2,1)S(1)} %broadcast_select_fusion), channel_id=1, source_target_pairs={{63,0},{127,64},{191,128},{255,192},{319,256},{383,320},{447,384},... | collective-permute-start | bytes 1880072 | tf_op jit(solution)/shard_map/ppermute | solution.py:24
  50.3 1.8 %copy-start.3 = (bf16[2448,128]{1,0:T(8,128)(2,1)}, bf16[2448,128]{1,0:T(8,128)(2,1)S(1)}, u32[]{:S(2)}) copy-start(bf16[2448,128]{1,0:T(8,128)(2,1)S(1)} %collective-permute-done.5.refs_7_) | copy-start | bytes 1880068
  52.1 3.5 %slice-start = ((bf16[24,128,128]{2,1,0:T(8,128)(2,1)}), bf16[12,128,128]{2,1,0:T(8,128)(2,1)S(1)}, s32[]{:S(2)}) async-start(bf16[24,128,128]{2,1,0:T(8,128)(2,1)} %refs_5_.1), calls=%async_computation | async-start | bytes 786432 | tf_op jit(solution)/shard_map/slice | solution.py:237
  96.8 8.3 %copy-start.1 = (bf16[2448,128]{1,0:T(8,128)(2,1)}, bf16[2448,128]{1,0:T(8,128)(2,1)S(1)}, u32[]{:S(2)}) copy-start(bf16[2448,128]{1,0:T(8,128)(2,1)S(1)} %collective-permute-done.2.refs_3_) | copy-start | bytes 1880068
  104.5 0.8 copy-start.2

commit v4 on v2

v4 whole, which is shorter than its diff:
```python
import functools

import jax
import jax.numpy as jnp
from jax import lax
from jax.experimental import pallas as pl
from jax.experimental.pallas import tpu as pltpu
from jax.sharding import PartitionSpec as P

BR = 2
BS = 128
SUBS = 4
CAP_L = 19
CAPM = 6
META = 16
RING = 4
CHEAP = pl.CostEstimate(flops=0, bytes_accessed=1024, transcendentals=0)
DEAR = pl.CostEstimate(flops=1 << 35, bytes_accessed=1 << 20, transcendentals=0)
ROOM = pltpu.CompilerParams(vmem_limit_bytes=16 << 20)
SMEM = pl.BlockSpec(memory_space=pltpu.SMEM)
VMEM = pl.BlockSpec(memory_space=pltpu.VMEM)
ANY = pl.BlockSpec(memory_space=pl.ANY)


def by_pairs(array, pairs):
    return lax.ppermute(array, ("prow", "pcol"), pairs)


def stage_kernel(mask_ref, left_ref, right_ref, packed_ref, part_ref, sem, part_sem):
    panel = left_ref.shape[0]
    half = part_ref.shape[0]
    part = pltpu.make_async_copy(right_ref.at[pl.ds(half, half)], part_ref, part_sem)
    part.start()
    slot = jnp.int32(0)
    for q in range(panel):
        taken = jnp.logical_and(mask_ref[q] != 0, slot < CAP_L)

        @pl.when(taken)
        def _(q=q, slot=slot):
            row = pl.multiple_of(slot * BS, BS)
            pltpu.make_async_copy(left_ref.at[q], packed_ref.at[pl.ds(row, BS)], sem).start()

        slot = slot + taken.astype(jnp.int32)

    @pl.loop(slot, CAP_L)
    def _(spare):
        row = pl.multiple_of(spare * BS, BS)
        pltpu.make_async_copy(left_ref.at[0], packed_ref.at[pl.ds(row, BS)], sem).start()

    lane = lax.broadcasted_iota(jnp.int32, (META, BS), 1)
    mask = jnp.zeros((META, BS), jnp.float32)
    for q in range(panel):
        mask = jnp.where(lane == q, (mask_ref[q] != 0).astype(jnp.float32), mask)
    packed_ref[pl.ds(CAP_L * BS, META), :] = mask.astype(packed_ref.dtype)
    blocks = packed_ref.at[pl.ds(0, CAP_L * BS)]
    pltpu.make_async_copy(blocks, blocks, sem).wait()
    part.wait()


def stage(left_mask, left_blocks, right_blocks):
    return pl.pallas_call(
        stage_kernel,
        out_shape=[
            jax.ShapeDtypeStruct((CAP_L * BS + META, BS), jnp.bfloat16),
            jax.ShapeDtypeStruct((2 * CAPM, BS, BS), jnp.bfloat16),
        ],
        in_specs=[SMEM, ANY, ANY],
        out_specs=[VMEM, VMEM],
        scratch_shapes=[pltpu.SemaphoreType.DMA, pltpu.SemaphoreType.DMA],
        compiler_params=ROOM,
        cost_estimate=CHEAP,
        name="pack_and_cut",
    )(left_mask, left_blocks, right_blocks)


def mask_of(packed, panel):
    return packed[CAP_L * BS, :panel].astype(jnp.int32)


def place(u, at, lists_ref, counts_ref, mask_ref, sources, into_ref, rank_ref, sem):
    column = lax.axis_index("pcol")
    run = jnp.int32(0)
    for q in range(mask_ref.shape[0]):
        rank_ref[q] = run
        run = run + (mask_ref[q] != 0).astype(jnp.int32)
    held = [(panel_ref, where(column)) for panel_ref, where in sources]
    total = jnp.int32(0)
    for p in range(lists_ref.shape[3]):
        block = lists_ref[0, u, 0, p]
        slot = lists_ref[0, u, 1, p]
        o = lists_ref[0, u, 2, p]
        live = jnp.logical_and(p < counts_ref[0, u], mask_ref[block] != 0)
        row = pl.multiple_of(jnp.minimum(rank_ref[block], CAP_L - 1) * BS, BS)
        down = pl.multiple_of(o * BS, BS)
        along = pl.multiple_of((at * CAPM + slot) * BS, BS)
        target = into_ref.at[pl.ds(down, BS), pl.ds(along, BS)]
        for panel_ref, here in held:
            taken = jnp.logical_and(live, here)

            @pl.when(taken)
            def _(panel_ref=panel_ref, row=row, target=target):
                pltpu.make_async_copy(panel_ref.at[pl.ds(row, BS)], target, sem).start()

            total = total + taken.astype(jnp.int32)
    return total


def drain(total, panel_ref, into_ref, sem):
    @pl.loop(0, total)
    def _(_):
        one = panel_ref.at[pl.ds(0, BS)]
        pltpu.make_async_copy(one, into_ref.at[pl.ds(0, BS), pl.ds(0, BS)], sem).wait()


def multiply(left_ref, right_ref, total_ref):
    for m in range(right_ref.shape[0]):
        total_ref[...] += jnp.dot(
            left_ref[:, m * BS : (m + 1) * BS], right_ref[m], preferred_element_type=jnp.float32
        )


def early_kernel(
    last, lists_ref, counts_ref, own_mask_ref, mask_ref, own_ref, above_ref, right_ref,
    known_ref, left_ref, held_ref, rank_ref, sem, right_sem,
):
    fetch_right = pltpu.make_async_copy(
        right_ref.at[pl.ds(0, held_ref.shape[0])], held_ref, right_sem
    )
    fetch_right.start()
    left_ref[...] = jnp.zeros_like(left_ref)
    own = ((own_ref, lambda c: c >= 0),)
    above = ((above_ref, lambda c: c < last),)
    total = place(2, 0, lists_ref, counts_ref, own_mask_ref, own, left_ref, rank_ref, sem)
    total += place(3, 1, lists_ref, counts_ref, mask_ref, above, left_ref, rank_ref, sem)
    drain(total, own_ref, left_ref, sem)
    fetch_right.wait()
    known_ref[...] = jnp.zeros_like(known_ref)
    multiply(left_ref, held_ref, known_ref)


def early(last, lists, counts, masks, panels, right):
    half = 2 * CAPM
    return pl.pallas_call(
        functools.partial(early_kernel, last),
        out_shape=jax.ShapeDtypeStruct((BR * BS, BS), jnp.float32),
        in_specs=[SMEM] * 4 + [ANY] * 3,
        out_specs=VMEM,
        scratch_shapes=[
            pltpu.VMEM((BR * BS, half * BS), jnp.bfloat16),
            pltpu.VMEM((half, BS, BS), jnp.bfloat16),
            pltpu.SMEM((masks[0].shape[0],), jnp.int32),
            pltpu.SemaphoreType.DMA,
            pltpu.SemaphoreType.DMA,
        ],
        compiler_params=ROOM,
        cost_estimate=DEAR,
        name="own_and_above",
    )(lists, counts, *masks, *panels, right)


def late_kernel(
    last, lists_ref, counts_ref, two_mask_ref, one_mask_ref, handed_mask_ref,
    two_ref, one_ref, handed_ref, right_ref, early_ref,
    laid_ref, known_ref, left_ref, held_ref, rank_ref, sem, right_sem,
):
    laid_ref[...] = jnp.zeros_like(laid_ref)
    two = ((two_ref, lambda c: c >= 0),)
    one = (
        (one_ref, lambda c: lax.rem(c, RING) != 0),
        (handed_ref, lambda c: lax.rem(c, RING) == 0),
    )
    total = place(0, 0, lists_ref, counts_ref, two_mask_ref, two, laid_ref, rank_ref, sem)
    total += place(1, 1, lists_ref, counts_ref, one_mask_ref, one, laid_ref, rank_ref, sem)
    known_ref[...] = early_ref[...]
    drain(total, two_ref, laid_ref, sem)

    @pl.when(lax.axis_index("pcol") == last)
    def _():
        fetch_right = pltpu.make_async_copy(
            right_ref.at[pl.ds(CAPM, CAPM)], held_ref, right_sem
        )
        fetch_right.start()
        left_ref[...] = jnp.zeros_like(left_ref)
        above = ((handed_ref, lambda c: c >= 0),)
        count = place(
            3, 0, lists_ref, counts_ref, handed_mask_ref, above, left_ref, rank_ref, sem
        )
        drain(count, handed_ref, left_ref, sem)
        fetch_right.wait()
        multiply(left_ref, held_ref, known_ref)


def late(last, lists, counts, masks, panels, right, known):
    return pl.pallas_call(
        functools.partial(late_kernel, last),
        out_shape=[
            jax.ShapeDtypeStruct((BR * BS, 2 * CAPM * BS), jnp.bfloat16),
            jax.ShapeDtypeStruct((BR * BS, BS), jnp.float32),
        ],
        in_specs=[SMEM] * 5 + [ANY] * 4 + [VMEM],
        out_specs=[VMEM, VMEM],
        scratch_shapes=[
            pltpu.VMEM((BR * BS, CAPM * BS), jnp.bfloat16),
            pltpu.VMEM((CAPM, BS, BS), jnp.bfloat16),
            pltpu.SMEM((masks[0].shape[0],), jnp.int32),
            pltpu.SemaphoreType.DMA,
            pltpu.SemaphoreType.DMA,
        ],
        compiler_params=ROOM,
        cost_estimate=CHEAP,
        name="lay_below",
    )(lists, counts, *masks, *panels, right, known)


def last_kernel(left_ref, right_ref, known_ref, out_ref):
    new = jnp.dot(left_ref[...], right_ref[...], preferred_element_type=jnp.float32)
    out_ref[...] = (known_ref[...] + new).astype(out_ref.dtype)


def last_product(left, right, known):
    return pl.pallas_call(
        last_kernel,
        out_shape=jax.ShapeDtypeStruct(known.shape, jnp.bfloat16),
        in_specs=[VMEM] * 3,
        out_specs=VMEM,
        compiler_params=ROOM,
        cost_estimate=CHEAP,
        name="last_product",
    )(left, right, known)


def on_device(n_row, n_col, left_blocks, left_mask, right_blocks, pair_lists, pair_counts):
    panel = left_blocks.shape[0]
    last = n_col - 1
    half = 2 * CAPM

    def shift(rows, cols, chosen):
        return [
            (r * n_col + c, (r + rows) % n_row * n_col + (c + cols) % n_col)
            for r in range(n_row)
            for c in range(n_col)
            if chosen(c)
        ]

    packed, sent_right = stage(left_mask, left_blocks, right_blocks)
    two_below = by_pairs(packed, shift(0, 2, lambda c: True))
    one_above = by_pairs(packed, shift(0, -1, lambda c: c > 0))
    one_below = by_pairs(packed, shift(0, 1, lambda c: c % RING < RING - 1))
    right_before = by_pairs(sent_right, shift(1, 0, lambda c: True))
    handed = by_pairs(
        two_below,
        shift(0, -1, lambda c: c % RING == 1) + shift(0, -3, lambda c: c == 2),
    )

    column = lax.axis_index("pcol")
    mask_handed = mask_of(handed, panel)
    known = early(
        last, pair_lists, pair_counts, [left_mask, mask_of(one_above, panel)],
        [packed, one_above], right_blocks,
    )
    mask_one = jnp.where(column % RING == 0, mask_handed, mask_of(one_below, panel))
    laid, known = late(
        last, pair_lists, pair_counts, [mask_of(two_below, panel), mask_one, mask_handed],
        [two_below, one_below, handed], right_blocks, known,
    )
    return last_product(laid, right_before.reshape(half * BS, BS), known)


def solution(mesh):
    in_specs = (
        P(("prow", "pcol"), None, None),
        P(("prow", "pcol")),
        P(("prow", "pcol"), None, None),
        P(("prow", "pcol"), None, None, None),
        P(("prow", "pcol"), None),
    )
    return jax.shard_map(
        functools.partial(on_device, mesh.shape["prow"], mesh.shape["pcol"]),
        mesh=mesh,
        in_specs=in_specs,
        out_specs=P("prow", "pcol"),
        check_vma=False,
    )
```

time: 107 us -> 103 us (0.963)
  the two profiles are of different devices: /device:TPU:2 before, /device:TPU:80 now
where the time goes in v4:
time: 103 us; the launch traced here: 102 us
  waiting for transfers between devices  79 us (77%)
  starting transfers between devices  12.6 us (12%)
  Pallas kernels  6.77 us (7%)
  local copies, waits for them, and re-layouts  3.1 us (3%)
    ppermute x5, waiting for transfers between devices, by_pairs(): return lax.ppermute(array, ('prow', 'pcol'), pairs)  79 us
    ppermute x5, starting transfers between devices, by_pairs(): return lax.ppermute(array, ('prow', 'pcol'), pairs)  12.6 us
    unnamed x15, local copies, waits for them, and re-layouts  3.1 us
    pallas_call x1, Pallas kernels, early(): pl.pallas_call(functools.partial(early_kernel, last), out_shape=jax.Shape...  2.38 us
  transfers between devices with their start and end apart: 5, of which 2 were waited for; matrix products, arithmetic and copies ran while one was open for 1% of the time, Pallas kernels for 4%

profile of v4, /device:TPU:80, one launch (start us, length us, event | category | flops | bytes accessed | tf_op | source)
XLA Modules:
  0.0 102.3 jit_solution(15247529615235254282)
XLA Ops:
  0.0 0.0 copy-start
  0.0 1.1 %copy-done = bf16[24,128,128]{2,1,0:T(8,128)(2,1)S(1)} copy-done((bf16[24,128,128]{2,1,0:T(8,128)(2,1)S(1)}, bf16[24,128,128]{2,1,0:T(8,128)(2,1)}, u32[]{:S(2)}) %copy-start) | copy-done | bytes 786456
  1.1 0.0 copy-start.2
  1.1 1.3 %copy-done.2 = bf16[38,128,128]{2,1,0:T(8,128)(2,1)S(1)} copy-done((bf16[38,128,128]{2,1,0:T(8,128)(2,1)S(1)}, bf16[38,128,128]{2,1,0:T(8,128)(2,1)}, u32[]{:S(2)}) %copy-start.2) | copy-done | bytes 1245208
  2.4 0.0 copy-start.3
  2.4 0.7 copy-done.3
  3.1 0.0 copy-start.6
  3.1 0.0 copy-start.1
  3.1 0.0 copy-start.4
  3.1 0.0 copy-start.5
  3.1 2.0 %pack_and_cut.1 = (bf16[2448,128]{1,0:T(8,128)(2,1)S(1)}, bf16[12,128,128]{2,1,0:T(8,128)(2,1)S(1)}) custom-call(s32[38]{0:T(128)S(1)} %copy-done.3, bf16[38,128,128]{2,1,0:T(8,128)(2,1)S(1)} %copy-done.2, bf16[24,128,128]{2,1,0:T(8,128)(2,1)S(1)} %copy-done), custom_call_target="tpu_custom_call" | custom-call | bytes 1024 | tf_op jit(solution)/shard_map/pack_and_cut/pallas_call | solution.py:61
  5.1 2.3 %collective-permute-start.3 = (bf16[2448,128]{1,0:T(8,128)(2,1)S(1)}, bf16[2448,128]{1,0:T(8,128)(2,1)}, u32[]{:S(2)}, u32[]{:S(2)}) collective-permute-start(bf16[2448,128]{1,0:T(8,128)(2,1)S(1)} %get-tuple-element.9.own_ref), channel_id=1, source_target_pairs={{1,0},{2,1},{3,2},{4,3},{5,4},{6,5},{7,6},{8,7},{9,8},{10,9},{11,1... | collective-permute-start | bytes 1880072 | tf_op jit(solution)/shard_map/ppermute | solution.py:26
  7.4 5.8 %collective-permute-start = (bf16[2448,128]{1,0:T(8,128)(2,1)S(1)}, bf16[2448,128]{1,0:T(8,128)(2,1)S(1)}, u32[]{:S(2)}, u32[]{:S(2)}) collective-permute-start(bf16[2448,128]{1,0:T(8,128)(2,1)S(1)} %get-tuple-element.9.own_ref), channel_id=1, source_target_pairs={{0,2},{1,3},{2,4},{3,5},{4,6},{5,7},{6,8},{7,9},{8,10},{9,11},{10,... | collective-permute-start | bytes 1880072 | tf_op jit(solution)/shard_map/ppermute | solution.py:26
  13.2 2.0 %collective-permute-start.2 = (bf16[2448,128]{1,0:T(8,128)(2,1)S(1)}, bf16[2448,128]{1,0:T(8,128)(2,1)S(1)}, u32[]{:S(2)}, u32[]{:S(2)}) collective-permute-start(bf16[2448,128]{1,0:T(8,128)(2,1)S(1)} %get-tuple-element.9.own_ref), channel_id=1, source_target_pairs={{0,1},{1,2},{2,3},{4,5},{5,6},{6,7},{8,9},{9,10},{10,11},{12,13},{... | collective-permute-start | bytes 1880072 | tf_op jit(solution)/shard_map/ppermute | solution.py:26
  15.1 1.9 %collective-permute-start.4 = (bf16[12,128,128]{2,1,0:T(8,128)(2,1)S(1)}, bf16[12,128,128]{2,1,0:T(8,128)(2,1)S(1)}, u32[]{:S(2)}, u32[]{:S(2)}) collective-permute-start(bf16[12,128,128]{2,1,0:T(8,128)(2,1)S(1)} %get-tuple-element.11), channel_id=1, source_target_pairs={{0,64},{1,65},{2,66},{3,67},{4,68},{5,69},{6,70},{7,71},{8,72},{9,... | collective-permute-start | bytes 1179656 | tf_op jit(solution)/shard_map/ppermute | solution.py:26
  17.1 0.0 copy-done.6
  17.1 19.3 %collective-permute-done.3.above_ref = bf16[2448,128]{1,0:T(8,128)(2,1)} collective-permute-done((bf16[2448,128]{1,0:T(8,128)(2,1)S(1)}, bf16[2448,128]{1,0:T(8,128)(2,1)}, u32[]{:S(2)}, u32[]{:S(2)}) %collective-permute-start.3) | collective-permute-done | bytes 626720 | tf_op jit(solution)/shard_map/ppermute | solution.py:26
  36.4 0.7 fusion.mask_ref
  37.1 0.0 collective-permute-done.two_ref
  37.1 0.7 collective-permute-start.1
  37.8 0.0 copy-done.1
  37.8 0.0 copy-done.4
  37.8 0.0 copy-done.5
  37.8 2.4 %own_and_above.1.early_ref = f32[256,128]{1,0:T(8,128)S(1)} custom-call(s32[1,4,3,12]{3,2,1,0:T(4,128)S(1)} %copy.7.lists_ref, s32[1,4]{1,0:T(1,128)S(1)} %copy-done.5, s32[38]{0:T(128)S(1)} %copy-done.4, s32[38]{0:T(128)S(1)} %fusion.mask_ref, bf16[2448,128]{1,0:T(8,128)(2,1)S(1)} %get-tuple-element.9.own_ref, ...), custom_call_target="tpu_custom_call" | custom-call | flops 34359738368 | bytes 1048576 | tf_op jit(solution)/shard_map/own_and_above/pallas_call | solution.py:143
  40.2 0.0 collective-permute-done.1.handed_ref
  40.2 0.0 collective-permute-done.2.one_ref
  40.2 1.4 %lay_below.1 = (bf16[256,1536]{1,0:T(8,128)(2,1)S(1)}, f32[256,128]{1,0:T(8,128)S(1)}) custom-call(s32[1,4,3,12]{3,2,1,0:T(4,128)S(1)} %copy.7.lists_ref, s32[1,4]{1,0:T(1,128)S(1)} %copy-done.5, s32[38]{0:T(128)S(1)} %fusion.3.two_mask_ref, s32[38]{0:T(128)S(1)} %broadcast_select_fusion.one_mask_ref, s32[38]{0:T(128)S(1)} %fusion.2.handed_mask_ref, ...), custom_call_target="tpu_custom_call" | custom-call | bytes 1024 | tf_op jit(solution)/shard_map/lay_below/pallas_call | solution.py:194
  41.6 59.7 %collective-permute-done.4 = bf16[12,128,128]{2,1,0:T(8,128)(2,1)S(1)} collective-permute-done((bf16[12,128,128]{2,1,0:T(8,128)(2,1)S(1)}, bf16[12,128,128]{2,1,0:T(8,128)(2,1)S(1)}, u32[]{:S(2)}, u32[]{:S(2)}) %collective-permute-start.4) | collective-permute-done | bytes 393248 | tf_op jit(solution)/shard_map/ppermute | solution.py:26
  101.3 1.0 last_product.1
  (4 shorter events, 0.0 us)
Async XLA Ops:
  0.0 1.1 %copy-start = (bf16[24,128,128]{2,1,0:T(8,128)(2,1)S(1)}, bf16[24,128,128]{2,1,0:T(8,128)(2,1)}, u32[]{:S(2)}) copy-start(bf16[24,128,128]{2,1,0:T(8,128)(2,1)} %right_ref.5) | copy-start | bytes 2359300
  1.1 1.3 %copy-start.2 = (bf16[38,128,128]{2,1,0:T(8,128)(2,1)S(1)}, bf16[38,128,128]{2,1,0:T(8,128)(2,1)}, u32[]{:S(2)}) copy-start(bf16[38,128,128]{2,1,0:T(8,128)(2,1)} %left_ref.1) | copy-start | bytes 3735556
  2.4 0.7 copy-start.3
  3.1 14.0 %copy-start.6 = (s32[1,4,3,12]{3,1,2,0:T(4,128)S(1)}, s32[1,4,3,12]{3,1,2,0:T(4,128)}, u32[]{:S(2)}) copy-start(s32[1,4,3,12]{3,1,2,0:T(4,128)} %param.8) | copy-start | bytes 1732
  3.1 34.7 %copy-start.1 = (bf16[24,128,128]{2,1,0:T(8,128)(2,1)S(1)}, bf16[24,128,128]{2,1,0:T(8,128)(2,1)}, u32[]{:S(2)}) copy-start(bf16[24,128,128]{2,1,0:T(8,128)(2,1)} %right_ref.5) | copy-start | bytes 2359300
  3.1 34.7 %copy-start.4 = (s32[38]{0:T(128)S(1)}, s32[38]{0:T(128)}, u32[]{:S(2)}) copy-start(s32[38]{0:T(128)} %own_mask_ref.1) | copy-start | bytes 460
  3.1 34.7 %copy-start.5 = (s32[1,4]{1,0:T(1,128)S(1)}, s32[1,4]{1,0:T(1,128)}, u32[]{:S(2)}) copy-start(s32[1,4]{1,0:T(1,128)} %counts_ref.3) | copy-start | bytes 52
  5.1 31.3 %collective-permute-start.3 = (bf16[2448,128]{1,0:T(8,128)(2,1)S(1)}, bf16[2448,128]{1,0:T(8,128)(2,1)}, u32[]{:S(2)}, u32[]{:S(2)}) collective-permute-start(bf16[2448,128]{1,0:T(8,128)(2,1)S(1)} %get-tuple-element.9.own_ref), channel_id=1, source_target_pairs={{1,0},{2,1},{3,2},{4,3},{5,4},{6,5},{7,6},{8,7},{9,8},{10,9},{11,1... | collective-permute-start | bytes 1880072 | tf_op jit(solution)/shard_map/ppermute | solution.py:26
  7.4 29.7 %collective-permute-start = (bf16[2448,128]{1,0:T(8,128)(2,1)S(1)}, bf16[2448,128]{1,0:T(8,128)(2,1)S(1)}, u32[]{:S(2)}, u32[]{:S(2)}) collective-permute-start(bf16[2448,128]{1,0:T(8,128)(2,1)S(1)} %get-tuple-element.9.own_ref), channel_id=1, source_target_pairs={{0,2},{1,3},{2,4},{3,5},{4,6},{5,7},{6,8},{7,9},{8,10},{9,11},{10,... | collective-permute-start | bytes 1880072 | tf_op jit(solution)/shard_map/ppermute | solution.py:26
  13.2 27.0 %collective-permute-start.2 = (bf16[2448,128]{1,0:T(8,128)(2,1)S(1)}, bf16[2448,128]{1,0:T(8,128)(2,1)S(1)}, u32[]{:S(2)}, u32[]{:S(2)}) collective-permute-start(bf16[2448,128]{1,0:T(8,128)(2,1)S(1)} %get-tuple-element.9.own_ref), channel_id=1, source_target_pairs={{0,1},{1,2},{2,3},{4,5},{5,6},{6,7},{8,9},{9,10},{10,11},{12,13},{... | collective-permute-start | bytes 1880072 | tf_op jit(solution)/shard_map/ppermute | solution.py:26
  15.1 86.2 %collective-permute-start.4 = (bf16[12,128,128]{2,1,0:T(8,128)(2,1)S(1)}, bf16[12,128,128]{2,1,0:T(8,128)(2,1)S(1)}, u32[]{:S(2)}, u32[]{:S(2)}) collective-permute-start(bf16[12,128,128]{2,1,0:T(8,128)(2,1)S(1)} %get-tuple-element.11), channel_id=1, source_target_pairs={{0,64},{1,65},{2,66},{3,67},{4,68},{5,69},{6,70},{7,71},{8,72},{9,... | collective-permute-start | bytes 1179656 | tf_op jit(solution)/shard_map/ppermute | solution.py:26
  37.1 3.1 %collective-permute-start.1 = (bf16[2448,128]{1,0:T(8,128)(2,1)S(1)}, bf16[2448,128]{1,0:T(8,128)(2,1)S(1)}, u32[]{:S(2)}, u32[]{:S(2)}) collective-permute-start(bf16[2448,128]{1,0:T(8,128)(2,1)S(1)} %collective-permute-done.two_ref), channel_id=1, source_target_pairs={{1,0},{5,4},{9,8},{13,12},{17,16},{21,20},{25,24},{29,28},{33,32},... | collective-permute-start | bytes 1880072 | tf_op jit(solution)/shard_map/ppermute | solution.py:26

commit v5 on v4

--- a/solution.py
+++ b/solution.py
@@ -67,7 +67,7 @@
         in_specs=[SMEM, ANY, ANY],
         out_specs=[VMEM, VMEM],
         scratch_shapes=[pltpu.SemaphoreType.DMA, pltpu.SemaphoreType.DMA],
-        compiler_params=ROOM,
+        compiler_params=pltpu.CompilerParams(vmem_limit_bytes=62 << 20),
         cost_estimate=CHEAP,
         name="pack_and_cut",
     )(left_mask, left_blocks, right_blocks)
@@ -119,43 +119,42 @@
         )
 
 
-def early_kernel(
-    last, lists_ref, counts_ref, own_mask_ref, mask_ref, own_ref, above_ref, right_ref,
-    known_ref, left_ref, held_ref, rank_ref, sem, right_sem,
+def one_kernel(
+    u, here, lists_ref, counts_ref, mask_ref, panel_ref, right_ref, *refs,
 ):
+    before_ref = refs[0] if len(refs) == 7 else None
+    known_ref, left_ref, held_ref, rank_ref, sem, right_sem = refs[-6:]
     fetch_right = pltpu.make_async_copy(
-        right_ref.at[pl.ds(0, held_ref.shape[0])], held_ref, right_sem
+        right_ref.at[pl.ds((u - 2) * CAPM, CAPM)], held_ref, right_sem
     )
     fetch_right.start()
     left_ref[...] = jnp.zeros_like(left_ref)
-    own = ((own_ref, lambda c: c >= 0),)
-    above = ((above_ref, lambda c: c < last),)
-    total = place(2, 0, lists_ref, counts_ref, own_mask_ref, own, left_ref, rank_ref, sem)
-    total += place(3, 1, lists_ref, counts_ref, mask_ref, above, left_ref, rank_ref, sem)
-    drain(total, own_ref, left_ref, sem)
+    source = ((panel_ref, here),)
+    total = place(u, 0, lists_ref, counts_ref, mask_ref, source, left_ref, rank_ref, sem)
+    drain(total, panel_ref, left_ref, sem)
     fetch_right.wait()
-    known_ref[...] = jnp.zeros_like(known_ref)
+    known_ref[...] = jnp.zeros_like(known_ref) if before_ref is None else before_ref[...]
     multiply(left_ref, held_ref, known_ref)
 
 
-def early(last, lists, counts, masks, panels, right):
-    half = 2 * CAPM
-    return pl.pallas_call(
-        functools.partial(early_kernel, last),
+def one_step(u, here, lists, counts, mask, panel, right, before, cost, name):
+    more = [] if before is None else [before]
+    return pl.pallas_call(
+        functools.partial(one_kernel, u, here),
         out_shape=jax.ShapeDtypeStruct((BR * BS, BS), jnp.float32),
-        in_specs=[SMEM] * 4 + [ANY] * 3,
+        in_specs=[SMEM] * 3 + [ANY] * 2 + [VMEM] * len(more),
         out_specs=VMEM,
         scratch_shapes=[
-            pltpu.VMEM((BR * BS, half * BS), jnp.bfloat16),
-            pltpu.VMEM((half, BS, BS), jnp.bfloat16),
-            pltpu.SMEM((masks[0].shape[0],), jnp.int32),
-            pltpu.SemaphoreType.DMA,
-            pltpu.SemaphoreType.DMA,
-        ],
-        compiler_params=ROOM,
-        cost_estimate=DEAR,
-        name="own_and_above",
-    )(lists, counts, *masks, *panels, right)
+            pltpu.VMEM((BR * BS, CAPM * BS), jnp.bfloat16),
+            pltpu.VMEM((CAPM, BS, BS), jnp.bfloat16),
+            pltpu.SMEM((mask.shape[0],), jnp.int32),
+            pltpu.SemaphoreType.DMA,
+            pltpu.SemaphoreType.DMA,
+        ],
+        compiler_params=ROOM,
+        cost_estimate=cost,
+        name=name,
+    )(lists, counts, mask, panel, right, *more)
 
 
 def late_kernel(
@@ -244,6 +243,180 @@
 
     packed, sent_right = stage(left_mask, left_blocks, right_blocks)
     two_below = by_pairs(packed, shift(0, 2, lambda c: True))
+    right_before = by_pairs(sent_right, shift(1, 0, lambda c: True))
+    one_above = by_pairs(packed, shift(0, -1, lambda c: c > 0))
+    one_below = by_pairs(packed, shift(0, 1, lambda c: c % RING < RING - 1))
+    passed = jnp.where(lax.axis_index("pcol") == 0, packed, two_below)
+    handed = by_pairs(
+        passed,
+        shift(0, -1, lambda c: c % RING == 1) + shift(0, -1, lambda c: c == 0),
+    )
+
+    column = lax.axis_index("pcol")
+    run = jnp.int32(0)
+    for q in range(mask_ref.shape[0]):
+        rank_ref[q] = run
+        run = run + (mask_ref[q] != 0).astype(jnp.int32)
+    held = [(panel_ref, where(column)) for panel_ref, where in sources]
+    total = jnp.int32(0)
+    for p in range(lists_ref.shape[3]):
+        block = lists_ref[0, u, 0, p]
+        slot = lists_ref[0, u, 1, p]
+        o = lists_ref[0, u, 2, p]
+        live = jnp.logical_and(p < counts_ref[0, u], mask_ref[block] != 0)
+        row = pl.multiple_of(jnp.minimum(rank_ref[block], CAP_L - 1) * BS, BS)
+        down = pl.multiple_of(o * BS, BS)
+        along = pl.multiple_of((at * CAPM + slot) * BS, BS)
+        target = into_ref.at[pl.ds(down, BS), pl.ds(along, BS)]
+        for panel_ref, here in held:
+            taken = jnp.logical_and(live, here)
+
+            @pl.when(taken)
+            def _(panel_ref=panel_ref, row=row, target=target):
+                pltpu.make_async_copy(panel_ref.at[pl.ds(row, BS)], target, sem).start()
+
+            total = total + taken.astype(jnp.int32)
+    return total
+
+
+def drain(total, panel_ref, into_ref, sem):
+    @pl.loop(0, total)
+    def _(_):
+        one = panel_ref.at[pl.ds(0, BS)]
+        pltpu.make_async_copy(one, into_ref.at[pl.ds(0, BS), pl.ds(0, BS)], sem).wait()
+
+
+def multiply(left_ref, right_ref, total_ref):
+    for m in range(right_ref.shape[0]):
+        total_ref[...] += jnp.dot(
+            left_ref[:, m * BS : (m + 1) * BS], right_ref[m], preferred_element_type=jnp.float32
+        )
+
+
+def one_kernel(
+    u, here, lists_ref, counts_ref, mask_ref, panel_ref, right_ref, *refs,
+):
+    before_ref = refs[0] if len(refs) == 7 else None
+    known_ref, left_ref, held_ref, rank_ref, sem, right_sem = refs[-6:]
+    fetch_right = pltpu.make_async_copy(
+        right_ref.at[pl.ds((u - 2) * CAPM, CAPM)], held_ref, right_sem
+    )
+    fetch_right.start()
+    left_ref[...] = jnp.zeros_like(left_ref)
+    source = ((panel_ref, here),)
+    total = place(u, 0, lists_ref, counts_ref, mask_ref, source, left_ref, rank_ref, sem)
+    drain(total, panel_ref, left_ref, sem)
+    fetch_right.wait()
+    known_ref[...] = jnp.zeros_like(known_ref) if before_ref is None else before_ref[...]
+    multiply(left_ref, held_ref, known_ref)
+
+
+def one_step(u, here, lists, counts, mask, panel, right, before, cost, name):
+    more = [] if before is None else [before]
+    return pl.pallas_call(
+        functools.partial(one_kernel, u, here),
+        out_shape=jax.ShapeDtypeStruct((BR * BS, BS), jnp.float32),
+        in_specs=[SMEM] * 3 + [ANY] * 2 + [VMEM] * len(more),
+        out_specs=VMEM,
+        scratch_shapes=[
+            pltpu.VMEM((BR * BS, CAPM * BS), jnp.bfloat16),
+            pltpu.VMEM((CAPM, BS, BS), jnp.bfloat16),
+            pltpu.SMEM((mask.shape[0],), jnp.int32),
+            pltpu.SemaphoreType.DMA,
+            pltpu.SemaphoreType.DMA,
+        ],
+        compiler_params=ROOM,
+        cost_estimate=cost,
+        name=name,
+    )(lists, counts, mask, panel, right, *more)
+
+
+def late_kernel(
+    last, lists_ref, counts_ref, two_mask_ref, one_mask_ref, handed_mask_ref,
+    two_ref, one_ref, handed_ref, right_ref, early_ref,
+    laid_ref, known_ref, left_ref, held_ref, rank_ref, sem, right_sem,
+):
+    laid_ref[...] = jnp.zeros_like(laid_ref)
+    two = ((two_ref, lambda c: c >= 0),)
+    one = (
+        (one_ref, lambda c: lax.rem(c, RING) != 0),
+        (handed_ref, lambda c: lax.rem(c, RING) == 0),
+    )
+    total = place(0, 0, lists_ref, counts_ref, two_mask_ref, two, laid_ref, rank_ref, sem)
+    total += place(1, 1, lists_ref, counts_ref, one_mask_ref, one, laid_ref, rank_ref, sem)
+    known_ref[...] = early_ref[...]
+    drain(total, two_ref, laid_ref, sem)
+
+    @pl.when(lax.axis_index("pcol") == last)
+    def _():
+        fetch_right = pltpu.make_async_copy(
+            right_ref.at[pl.ds(CAPM, CAPM)], held_ref, right_sem
+        )
+        fetch_right.start()
+        left_ref[...] = jnp.zeros_like(left_ref)
+        above = ((handed_ref, lambda c: c >= 0),)
+        count = place(
+            3, 0, lists_ref, counts_ref, handed_mask_ref, above, left_ref, rank_ref, sem
+        )
+        drain(count, handed_ref, left_ref, sem)
+        fetch_right.wait()
+        multiply(left_ref, held_ref, known_ref)
+
+
+def late(last, lists, counts, masks, panels, right, known):
+    return pl.pallas_call(
+        functools.partial(late_kernel, last),
+        out_shape=[
+            jax.ShapeDtypeStruct((BR * BS, 2 * CAPM * BS), jnp.bfloat16),
+            jax.ShapeDtypeStruct((BR * BS, BS), jnp.float32),
+        ],
+        in_specs=[SMEM] * 5 + [ANY] * 4 + [VMEM],
+        out_specs=[VMEM, VMEM],
+        scratch_shapes=[
+            pltpu.VMEM((BR * BS, CAPM * BS), jnp.bfloat16),
+            pltpu.VMEM((CAPM, BS, BS), jnp.bfloat16),
+            pltpu.SMEM((masks[0].shape[0],), jnp.int32),
+            pltpu.SemaphoreType.DMA,
+            pltpu.SemaphoreType.DMA,
+        ],
+        compiler_params=ROOM,
+        cost_estimate=CHEAP,
+        name="lay_below",
+    )(lists, counts, *masks, *panels, right, known)
+
+
+def last_kernel(left_ref, right_ref, known_ref, out_ref):
+    new = jnp.dot(left_ref[...], right_ref[...], preferred_element_type=jnp.float32)
+    out_ref[...] = (known_ref[...] + new).astype(out_ref.dtype)
+
+
+def last_product(left, right, known):
+    return pl.pallas_call(
+        last_kernel,
+        out_shape=jax.ShapeDtypeStruct(known.shape, jnp.bfloat16),
+        in_specs=[VMEM] * 3,
+        out_specs=VMEM,
+        compiler_params=ROOM,
+        cost_estimate=CHEAP,
+        name="last_product",
+    )(left, right, known)
+
+
+def on_device(n_row, n_col, left_blocks, left_mask, right_blocks, pair_lists, pair_counts):
+    panel = left_blocks.shape[0]
+    last = n_col - 1
+    half = 2 * CAPM
+
+    def shift(rows, cols, chosen):
+        return [
+            (r * n_col + c, (r + rows) % n_row * n_col + (c + cols) % n_col)
+            for r in range(n_row)
+            for c in range(n_col)
+            if chosen(c)
+        ]
+
+    packed, sent_right = stage(left_mask, left_blocks, right_blocks)
+    two_below = by_pairs(packed, shift(0, 2, lambda c: True))
     one_above = by_pairs(packed, shift(0, -1, lambda c: c > 0))
     one_below = by_pairs(packed, shift(0, 1, lambda c: c % RING < RING - 1))
     right_before = by_pairs(sent_right, shift(1, 0, lambda c: True))
@@ -254,9 +427,13 @@
 
     column = lax.axis_index("pcol")
     mask_handed = mask_of(handed, panel)
-    known = early(
-        last, pair_lists, pair_counts, [left_mask, mask_of(one_above, panel)],
-        [packed, one_above], right_blocks,
+    known = one_step(
+        2, lambda c: c >= 0, pair_lists, pair_counts, left_mask, packed, right_blocks, None,
+        DEAR, "own_step",
+    )
+    known = one_step(
+        3, lambda c: c < last, pair_lists, pair_counts, mask_of(one_above, panel), one_above,
+        right_blocks, known, CHEAP, "step_above",
     )
     mask_one = jnp.where(column % RING == 0, mask_handed, mask_of(one_below, panel))
     laid, known = late(

time: 103 us -> 93.8 us (0.911)
  the two profiles are of different devices: /device:TPU:80 before, /device:TPU:32 now
where the time goes in v5:
time: 93.8 us; the launch traced here: 93.4 us
  waiting for transfers between devices  68.3 us (73%)
  starting transfers between devices  14.2 us (15%)
  Pallas kernels  8.95 us (10%)
  local copies, waits for them, and re-layouts  1.09 us (1%)
    ppermute x5, waiting for transfers between devices, by_pairs(): return lax.ppermute(array, ('prow', 'pcol'), pairs)  68.3 us
    ppermute x5, starting transfers between devices, by_pairs(): return lax.ppermute(array, ('prow', 'pcol'), pairs)  14.2 us
    pallas_call x2, Pallas kernels, one_step(): pl.pallas_call(functools.partial(one_kernel, u, here), out_shape=jax.Shap...  3.59 us
    pallas_call x1, Pallas kernels, stage(): pl.pallas_call(stage_kernel, out_shape=[jax.ShapeDtypeStruct((CAP_L * BS...  2.97 us
  transfers between devices with their start and end apart: 5, of which 4 were waited for; matrix products, arithmetic and copies ran while one was open for 1% of the time, Pallas kernels for 5%

profile of v5, /device:TPU:32, one launch (start us, length us, event | category | flops | bytes accessed | tf_op | source)
XLA Modules:
  0.0 93.4 jit_solution(6201217500511457293)
XLA Ops:
  0.0 0.0 copy-start
  0.0 0.0 copy-start.2
  0.0 0.0 copy-start.4
  0.0 0.0 copy-start.1
  0.0 3.0 %pack_and_cut.1 = (bf16[2448,128]{1,0:T(8,128)(2,1)}, bf16[12,128,128]{2,1,0:T(8,128)(2,1)}) custom-call(s32[38]{0:T(128)} %mask_ref.3, bf16[38,128,128]{2,1,0:T(8,128)(2,1)} %left_ref.1, bf16[24,128,128]{2,1,0:T(8,128)(2,1)} %right_ref.7), custom_call_target="tpu_custom_call" | custom-call | bytes 1024 | tf_op jit(solution)/shard_map/pack_and_cut/pallas_call | solution.py:61
  3.0 5.2 %collective-permute-start = (bf16[2448,128]{1,0:T(8,128)(2,1)}, bf16[2448,128]{1,0:T(8,128)(2,1)S(1)}, u32[]{:S(2)}, u32[]{:S(2)}) collective-permute-start(bf16[2448,128]{1,0:T(8,128)(2,1)} %get-tuple-element.9.panel_ref), channel_id=1, source_target_pairs={{0,2},{1,3},{2,4},{3,5},{4,6},{5,7},{6,8},{7,9},{8,10},{9,11},{10,... | collective-permute-start | bytes 1880072 | tf_op jit(solution)/shard_map/ppermute | solution.py:26
  8.2 3.8 %collective-permute-start.3 = (bf16[2448,128]{1,0:T(8,128)(2,1)}, bf16[2448,128]{1,0:T(8,128)(2,1)}, u32[]{:S(2)}, u32[]{:S(2)}) collective-permute-start(bf16[2448,128]{1,0:T(8,128)(2,1)} %get-tuple-element.9.panel_ref), channel_id=1, source_target_pairs={{1,0},{2,1},{3,2},{4,3},{5,4},{6,5},{7,6},{8,7},{9,8},{10,9},{11,1... | collective-permute-start | bytes 1880072 | tf_op jit(solution)/shard_map/ppermute | solution.py:26
  12.0 2.1 %collective-permute-start.2 = (bf16[2448,128]{1,0:T(8,128)(2,1)}, bf16[2448,128]{1,0:T(8,128)(2,1)S(1)}, u32[]{:S(2)}, u32[]{:S(2)}) collective-permute-start(bf16[2448,128]{1,0:T(8,128)(2,1)} %get-tuple-element.9.panel_ref), channel_id=1, source_target_pairs={{0,1},{1,2},{2,3},{4,5},{5,6},{6,7},{8,9},{9,10},{10,11},{12,13},{... | collective-permute-start | bytes 1880072 | tf_op jit(solution)/shard_map/ppermute | solution.py:26
  14.1 1.9 %collective-permute-start.4 = (bf16[12,128,128]{2,1,0:T(8,128)(2,1)}, bf16[12,128,128]{2,1,0:T(8,128)(2,1)S(1)}, u32[]{:S(2)}, u32[]{:S(2)}) collective-permute-start(bf16[12,128,128]{2,1,0:T(8,128)(2,1)} %get-tuple-element.11), channel_id=1, source_target_pairs={{0,64},{1,65},{2,66},{3,67},{4,68},{5,69},{6,70},{7,71},{8,72},{9,... | collective-permute-start | bytes 1179656 | tf_op jit(solution)/shard_map/ppermute | solution.py:26
  16.0 0.0 copy-done.4
  16.0 7.5 %collective-permute-done.two_ref = bf16[2448,128]{1,0:T(8,128)(2,1)S(1)} collective-permute-done((bf16[2448,128]{1,0:T(8,128)(2,1)}, bf16[2448,128]{1,0:T(8,128)(2,1)S(1)}, u32[]{:S(2)}, u32[]{:S(2)}) %collective-permute-start) | collective-permute-done | bytes 626720 | tf_op jit(solution)/shard_map/ppermute | solution.py:26
  23.5 1.3 %collective-permute-start.1 = (bf16[2448,128]{1,0:T(8,128)(2,1)S(1)}, bf16[2448,128]{1,0:T(8,128)(2,1)S(1)}, u32[]{:S(2)}, u32[]{:S(2)}) collective-permute-start(bf16[2448,128]{1,0:T(8,128)(2,1)S(1)} %collective-permute-done.two_ref), channel_id=1, source_target_pairs={{1,0},{5,4},{9,8},{13,12},{17,16},{21,20},{25,24},{29,28},{33,32},... | collective-permute-start | bytes 1880072 | tf_op jit(solution)/shard_map/ppermute | solution.py:26
  24.8 0.0 copy-done
  24.8 0.0 copy-done.2
  24.8 0.0 copy-done.1
  24.8 0.0 copy-start.3
  24.9 1.1 %copy-done.3 = bf16[2448,128]{1,0:T(8,128)(2,1)S(1)} copy-done((bf16[2448,128]{1,0:T(8,128)(2,1)S(1)}, bf16[2448,128]{1,0:T(8,128)(2,1)}, u32[]{:S(2)}) %copy-start.3) | copy-done | bytes 626712
  25.9 1.5 %own_step.1.refs_0_ = f32[256,128]{1,0:T(8,128)S(1)} custom-call(s32[1,4,3,12]{3,2,1,0:T(4,128)S(1)} %copy.8.lists_ref, s32[1,4]{1,0:T(1,128)S(1)} %copy-done.1, s32[38]{0:T(128)S(1)} %copy-done.2, bf16[2448,128]{1,0:T(8,128)(2,1)S(1)} %copy-done.3, bf16[24,128,128]{2,1,0:T(8,128)(2,1)S(1)} %copy-done), custom_call_target="tpu_custom_call" | custom-call | flops 34359738368 | bytes 1048576 | tf_op jit(solution)/shard_map/own_step/pallas_call | solution.py:316
  27.4 15.3 %collective-permute-done.3.panel_ref = bf16[2448,128]{1,0:T(8,128)(2,1)} collective-permute-done((bf16[2448,128]{1,0:T(8,128)(2,1)}, bf16[2448,128]{1,0:T(8,128)(2,1)}, u32[]{:S(2)}, u32[]{:S(2)}) %collective-permute-start.3) | collective-permute-done | bytes 626720 | tf_op jit(solution)/shard_map/ppermute | solution.py:26
  42.7 0.7 fusion.mask_ref
  43.4 2.1 %step_above.1.early_ref = f32[256,128]{1,0:T(8,128)S(1)} custom-call(s32[1,4,3,12]{3,2,1,0:T(4,128)S(1)} %copy.8.lists_ref, s32[1,4]{1,0:T(1,128)S(1)} %copy-done.1, s32[38]{0:T(128)S(1)} %fusion.mask_ref, bf16[2448,128]{1,0:T(8,128)(2,1)} %collective-permute-done.3.panel_ref, bf16[24,128,128]{2,1,0:T(8,128)(2,1)S(1)} %copy-done, f32[256,128]{1,0:T(8,128)S(1)} %own_step.1.refs_0_), custom_call_target="tpu_custom_call" | custom-call | bytes 1024 | tf_op jit(solution)/shard_map/step_above/pallas_call | solution.py:316
  45.5 6.3 %collective-permute-done.1.handed_ref = bf16[2448,128]{1,0:T(8,128)(2,1)S(1)} collective-permute-done((bf16[2448,128]{1,0:T(8,128)(2,1)S(1)}, bf16[2448,128]{1,0:T(8,128)(2,1)S(1)}, u32[]{:S(2)}, u32[]{:S(2)}) %collective-permute-start.1) | collective-permute-done | bytes 626720 | tf_op jit(solution)/shard_map/ppermute | solution.py:26
  51.9 0.0 collective-permute-done.2.one_ref
  51.9 1.4 %lay_below.1 = (bf16[256,1536]{1,0:T(8,128)(2,1)S(1)}, f32[256,128]{1,0:T(8,128)S(1)}) custom-call(s32[1,4,3,12]{3,2,1,0:T(4,128)S(1)} %copy.8.lists_ref, s32[1,4]{1,0:T(1,128)S(1)} %copy-done.1, s32[38]{0:T(128)S(1)} %fusion.3.two_mask_ref, s32[38]{0:T(128)S(1)} %broadcast_select_fusion.one_mask_ref, s32[38]{0:T(128)S(1)} %fusion.2.handed_mask_ref, ...), custom_call_target="tpu_custom_call" | custom-call | bytes 1024 | tf_op jit(solution)/shard_map/lay_below/pallas_call | solution.py:367
  53.3 39.1 %collective-permute-done.4 = bf16[12,128,128]{2,1,0:T(8,128)(2,1)S(1)} collective-permute-done((bf16[12,128,128]{2,1,0:T(8,128)(2,1)}, bf16[12,128,128]{2,1,0:T(8,128)(2,1)S(1)}, u32[]{:S(2)}, u32[]{:S(2)}) %collective-permute-start.4) | collective-permute-done | bytes 393248 | tf_op jit(solution)/shard_map/ppermute | solution.py:26
  92.4 1.0 %last_product.1 = bf16[256,128]{1,0:T(8,128)(2,1)} custom-call(bf16[256,1536]{1,0:T(8,128)(2,1)S(1)} %get-tuple-element.10.left_ref, bf16[1536,128]{1,0:T(8,128)(2,1)S(1)} %bitcast.25, f32[256,128]{1,0:T(8,128)S(1)} %get-tuple-element.12.known_ref), custom_call_target="tpu_custom_call" | custom-call | bytes 1024 | tf_op jit(solution)/shard_map/last_product/pallas_call | solution.py:394
  (4 shorter events, 0.0 us)
Async XLA Ops:
  0.0 24.8 %copy-start = (bf16[24,128,128]{2,1,0:T(8,128)(2,1)S(1)}, bf16[24,128,128]{2,1,0:T(8,128)(2,1)}, u32[]{:S(2)}) copy-start(bf16[24,128,128]{2,1,0:T(8,128)(2,1)} %right_ref.7) | copy-start | bytes 2359300
  0.0 24.8 %copy-start.2 = (s32[38]{0:T(128)S(1)}, s32[38]{0:T(128)}, u32[]{:S(2)}) copy-start(s32[38]{0:T(128)} %mask_ref.3) | copy-start | bytes 460
  0.0 16.0 %copy-start.4 = (s32[1,4,3,12]{3,1,2,0:T(4,128)S(1)}, s32[1,4,3,12]{3,1,2,0:T(4,128)}, u32[]{:S(2)}) copy-start(s32[1,4,3,12]{3,1,2,0:T(4,128)} %param.8) | copy-start | bytes 1732
  0.0 24.8 %copy-start.1 = (s32[1,4]{1,0:T(1,128)S(1)}, s32[1,4]{1,0:T(1,128)}, u32[]{:S(2)}) copy-start(s32[1,4]{1,0:T(1,128)} %counts_ref.5) | copy-start | bytes 52
  3.0 20.5 %collective-permute-start = (bf16[2448,128]{1,0:T(8,128)(2,1)}, bf16[2448,128]{1,0:T(8,128)(2,1)S(1)}, u32[]{:S(2)}, u32[]{:S(2)}) collective-permute-start(bf16[2448,128]{1,0:T(8,128)(2,1)} %get-tuple-element.9.panel_ref), channel_id=1, source_target_pairs={{0,2},{1,3},{2,4},{3,5},{4,6},{5,7},{6,8},{7,9},{8,10},{9,11},{10,... | collective-permute-start | bytes 1880072 | tf_op jit(solution)/shard_map/ppermute | solution.py:26
  8.2 34.6 %collective-permute-start.3 = (bf16[2448,128]{1,0:T(8,128)(2,1)}, bf16[2448,128]{1,0:T(8,128)(2,1)}, u32[]{:S(2)}, u32[]{:S(2)}) collective-permute-start(bf16[2448,128]{1,0:T(8,128)(2,1)} %get-tuple-element.9.panel_ref), channel_id=1, source_target_pairs={{1,0},{2,1},{3,2},{4,3},{5,4},{6,5},{7,6},{8,7},{9,8},{10,9},{11,1... | collective-permute-start | bytes 1880072 | tf_op jit(solution)/shard_map/ppermute | solution.py:26
  12.0 39.9 %collective-permute-start.2 = (bf16[2448,128]{1,0:T(8,128)(2,1)}, bf16[2448,128]{1,0:T(8,128)(2,1)S(1)}, u32[]{:S(2)}, u32[]{:S(2)}) collective-permute-start(bf16[2448,128]{1,0:T(8,128)(2,1)} %get-tuple-element.9.panel_ref), channel_id=1, source_target_pairs={{0,1},{1,2},{2,3},{4,5},{5,6},{6,7},{8,9},{9,10},{10,11},{12,13},{... | collective-permute-start | bytes 1880072 | tf_op jit(solution)/shard_map/ppermute | solution.py:26
  14.1 78.4 %collective-permute-start.4 = (bf16[12,128,128]{2,1,0:T(8,128)(2,1)}, bf16[12,128,128]{2,1,0:T(8,128)(2,1)S(1)}, u32[]{:S(2)}, u32[]{:S(2)}) collective-permute-start(bf16[12,128,128]{2,1,0:T(8,128)(2,1)} %get-tuple-element.11), channel_id=1, source_target_pairs={{0,64},{1,65},{2,66},{3,67},{4,68},{5,69},{6,70},{7,71},{8,72},{9,... | collective-permute-start | bytes 1179656 | tf_op jit(solution)/shard_map/ppermute | solution.py:26
  23.5 28.3 %collective-permute-start.1 = (bf16[2448,128]{1,0:T(8,128)(2,1)S(1)}, bf16[2448,128]{1,0:T(8,128)(2,1)S(1)}, u32[]{:S(2)}, u32[]{:S(2)}) collective-permute-start(bf16[2448,128]{1,0:T(8,128)(2,1)S(1)} %collective-permute-done.two_ref), channel_id=1, source_target_pairs={{1,0},{5,4},{9,8},{13,12},{17,16},{21,20},{25,24},{29,28},{33,32},... | collective-permute-start | bytes 1880072 | tf_op jit(solution)/shard_map/ppermute | solution.py:26
  24.8 1.1 %copy-start.3 = (bf16[2448,128]{1,0:T(8,128)(2,1)S(1)}, bf16[2448,128]{1,0:T(8,128)(2,1)}, u32[]{:S(2)}) copy-start(bf16[2448,128]{1,0:T(8,128)(2,1)} %get-tuple-element.9.panel_ref) | copy-start | bytes 1880068

commit v6 on v4

--- a/solution.py
+++ b/solution.py
@@ -14,6 +14,7 @@
 CAPM = 6
 META = 16
 RING = 4
+ROWS = CAP_L * BS + META
 CHEAP = pl.CostEstimate(flops=0, bytes_accessed=1024, transcendentals=0)
 DEAR = pl.CostEstimate(flops=1 << 35, bytes_accessed=1 << 20, transcendentals=0)
 ROOM = pltpu.CompilerParams(vmem_limit_bytes=16 << 20)
@@ -67,7 +68,7 @@
         in_specs=[SMEM, ANY, ANY],
         out_specs=[VMEM, VMEM],
         scratch_shapes=[pltpu.SemaphoreType.DMA, pltpu.SemaphoreType.DMA],
-        compiler_params=ROOM,
+        compiler_params=pltpu.CompilerParams(vmem_limit_bytes=62 << 20),
         cost_estimate=CHEAP,
         name="pack_and_cut",
     )(left_mask, left_blocks, right_blocks)
@@ -83,23 +84,24 @@
     for q in range(mask_ref.shape[0]):
         rank_ref[q] = run
         run = run + (mask_ref[q] != 0).astype(jnp.int32)
-    held = [(panel_ref, where(column)) for panel_ref, where in sources]
+    held = [(panel_ref, where(column), base(column)) for panel_ref, where, base in sources]
     total = jnp.int32(0)
     for p in range(lists_ref.shape[3]):
         block = lists_ref[0, u, 0, p]
         slot = lists_ref[0, u, 1, p]
         o = lists_ref[0, u, 2, p]
         live = jnp.logical_and(p < counts_ref[0, u], mask_ref[block] != 0)
-        row = pl.multiple_of(jnp.minimum(rank_ref[block], CAP_L - 1) * BS, BS)
+        row = jnp.minimum(rank_ref[block], CAP_L - 1) * BS
         down = pl.multiple_of(o * BS, BS)
         along = pl.multiple_of((at * CAPM + slot) * BS, BS)
         target = into_ref.at[pl.ds(down, BS), pl.ds(along, BS)]
-        for panel_ref, here in held:
+        for panel_ref, here, base in held:
             taken = jnp.logical_and(live, here)
+            first = pl.multiple_of(row + base * ROWS, META)
 
             @pl.when(taken)
-            def _(panel_ref=panel_ref, row=row, target=target):
-                pltpu.make_async_copy(panel_ref.at[pl.ds(row, BS)], target, sem).start()
+            def _(panel_ref=panel_ref, first=first, target=target):
+                pltpu.make_async_copy(panel_ref.at[pl.ds(first, BS)], target, sem).start()
 
             total = total + taken.astype(jnp.int32)
     return total
@@ -119,75 +121,81 @@
         )
 
 
-def early_kernel(
-    last, lists_ref, counts_ref, own_mask_ref, mask_ref, own_ref, above_ref, right_ref,
+def zero(c):
+    return 0
+
+
+def own_kernel(
+    lists_ref, counts_ref, mask_ref, panel_ref, right_ref,
     known_ref, left_ref, held_ref, rank_ref, sem, right_sem,
 ):
-    fetch_right = pltpu.make_async_copy(
-        right_ref.at[pl.ds(0, held_ref.shape[0])], held_ref, right_sem
-    )
+    fetch_right = pltpu.make_async_copy(right_ref.at[pl.ds(0, CAPM)], held_ref, right_sem)
     fetch_right.start()
     left_ref[...] = jnp.zeros_like(left_ref)
-    own = ((own_ref, lambda c: c >= 0),)
-    above = ((above_ref, lambda c: c < last),)
-    total = place(2, 0, lists_ref, counts_ref, own_mask_ref, own, left_ref, rank_ref, sem)
-    total += place(3, 1, lists_ref, counts_ref, mask_ref, above, left_ref, rank_ref, sem)
-    drain(total, own_ref, left_ref, sem)
+    own = ((panel_ref, lambda c: c >= 0, zero),)
+    total = place(2, 0, lists_ref, counts_ref, mask_ref, own, left_ref, rank_ref, sem)
+    drain(total, panel_ref, left_ref, sem)
     fetch_right.wait()
     known_ref[...] = jnp.zeros_like(known_ref)
     multiply(left_ref, held_ref, known_ref)
 
 
-def early(last, lists, counts, masks, panels, right):
-    half = 2 * CAPM
-    return pl.pallas_call(
-        functools.partial(early_kernel, last),
+def scratch(panel):
+    return [
+        pltpu.VMEM((BR * BS, CAPM * BS), jnp.bfloat16),
+        pltpu.VMEM((CAPM, BS, BS), jnp.bfloat16),
+        pltpu.SMEM((panel,), jnp.int32),
+        pltpu.SemaphoreType.DMA,
+        pltpu.SemaphoreType.DMA,
+    ]
+
+
+def own_step(lists, counts, mask, packed, right):
+    return pl.pallas_call(
+        own_kernel,
         out_shape=jax.ShapeDtypeStruct((BR * BS, BS), jnp.float32),
-        in_specs=[SMEM] * 4 + [ANY] * 3,
+        in_specs=[SMEM] * 3 + [ANY] * 2,
         out_specs=VMEM,
-        scratch_shapes=[
-            pltpu.VMEM((BR * BS, half * BS), jnp.bfloat16),
-            pltpu.VMEM((half, BS, BS), jnp.bfloat16),
-            pltpu.SMEM((masks[0].shape[0],), jnp.int32),
-            pltpu.SemaphoreType.DMA,
-            pltpu.SemaphoreType.DMA,
-        ],
+        scratch_shapes=scratch(mask.shape[0]),
         compiler_params=ROOM,
         cost_estimate=DEAR,
-        name="own_and_above",
-    )(lists, counts, *masks, *panels, right)
+        name="own_step",
+    )(lists, counts, mask, packed, right)
 
 
 def late_kernel(
-    last, lists_ref, counts_ref, two_mask_ref, one_mask_ref, handed_mask_ref,
-    two_ref, one_ref, handed_ref, right_ref, early_ref,
+    last, lists_ref, counts_ref, two_mask_ref, one_mask_ref, above_mask_ref,
+    row_ref, crossed_ref, handed_ref, around_ref, right_ref, own_ref,
     laid_ref, known_ref, left_ref, held_ref, rank_ref, sem, right_sem,
 ):
+    fetch_right = pltpu.make_async_copy(right_ref.at[pl.ds(CAPM, CAPM)], held_ref, right_sem)
+    fetch_right.start()
     laid_ref[...] = jnp.zeros_like(laid_ref)
-    two = ((two_ref, lambda c: c >= 0),)
+    left_ref[...] = jnp.zeros_like(left_ref)
+
+    def at(c):
+        return lax.rem(c, RING)
+
+    two = (
+        (row_ref, lambda c: at(c) >= 2, lambda c: jnp.maximum(at(c) - 2, 0)),
+        (crossed_ref, lambda c: at(c) < 2, zero),
+    )
     one = (
-        (one_ref, lambda c: lax.rem(c, RING) != 0),
-        (handed_ref, lambda c: lax.rem(c, RING) == 0),
+        (row_ref, lambda c: at(c) >= 1, lambda c: jnp.maximum(at(c) - 1, 0)),
+        (handed_ref, lambda c: at(c) == 0, zero),
+    )
+    above = (
+        (row_ref, lambda c: at(c) < RING - 1, lambda c: jnp.minimum(at(c) + 1, RING - 1)),
+        (crossed_ref, lambda c: jnp.logical_and(at(c) == RING - 1, c != last), zero),
+        (around_ref, lambda c: c == last, zero),
     )
     total = place(0, 0, lists_ref, counts_ref, two_mask_ref, two, laid_ref, rank_ref, sem)
     total += place(1, 1, lists_ref, counts_ref, one_mask_ref, one, laid_ref, rank_ref, sem)
-    known_ref[...] = early_ref[...]
-    drain(total, two_ref, laid_ref, sem)
-
-    @pl.when(lax.axis_index("pcol") == last)
-    def _():
-        fetch_right = pltpu.make_async_copy(
-            right_ref.at[pl.ds(CAPM, CAPM)], held_ref, right_sem
-        )
-        fetch_right.start()
-        left_ref[...] = jnp.zeros_like(left_ref)
-        above = ((handed_ref, lambda c: c >= 0),)
-        count = place(
-            3, 0, lists_ref, counts_ref, handed_mask_ref, above, left_ref, rank_ref, sem
-        )
-        drain(count, handed_ref, left_ref, sem)
-        fetch_right.wait()
-        multiply(left_ref, held_ref, known_ref)
+    total += place(3, 0, lists_ref, counts_ref, above_mask_ref, above, left_ref, rank_ref, sem)
+    known_ref[...] = own_ref[...]
+    drain(total, crossed_ref, laid_ref, sem)
+    fetch_right.wait()
+    multiply(left_ref, held_ref, known_ref)
 
 
 def late(last, lists, counts, masks, panels, right, known):
@@ -197,18 +205,12 @@
             jax.ShapeDtypeStruct((BR * BS, 2 * CAPM * BS), jnp.bfloat16),
             jax.ShapeDtypeStruct((BR * BS, BS), jnp.float32),
         ],
-        in_specs=[SMEM] * 5 + [ANY] * 4 + [VMEM],
+        in_specs=[SMEM] * 5 + [ANY] * 5 + [VMEM],
         out_specs=[VMEM, VMEM],
-        scratch_shapes=[
-            pltpu.VMEM((BR * BS, CAPM * BS), jnp.bfloat16),
-            pltpu.VMEM((CAPM, BS, BS), jnp.bfloat16),
-            pltpu.SMEM((masks[0].shape[0],), jnp.int32),
-            pltpu.SemaphoreType.DMA,
-            pltpu.SemaphoreType.DMA,
-        ],
+        scratch_shapes=scratch(masks[0].shape[0]),
         compiler_params=ROOM,
         cost_estimate=CHEAP,
-        name="lay_below",
+        name="other_steps",
     )(lists, counts, *masks, *panels, right, known)
 
 
@@ -243,25 +245,38 @@
         ]
 
     packed, sent_right = stage(left_mask, left_blocks, right_blocks)
-    two_below = by_pairs(packed, shift(0, 2, lambda c: True))
-    one_above = by_pairs(packed, shift(0, -1, lambda c: c > 0))
-    one_below = by_pairs(packed, shift(0, 1, lambda c: c % RING < RING - 1))
+    crossed = by_pairs(
+        packed,
+        shift(0, 2, lambda c: c % RING >= 2)
+        + shift(0, -1, lambda c: c % RING == 0 and c != 0),
+    )
+    rings = [[first + at for at in range(RING)] for first in range(0, n_col, RING)]
+    row = lax.all_gather(packed, "pcol", axis_index_groups=rings)
     right_before = by_pairs(sent_right, shift(1, 0, lambda c: True))
-    handed = by_pairs(
-        two_below,
-        shift(0, -1, lambda c: c % RING == 1) + shift(0, -3, lambda c: c == 2),
-    )
+    handed = by_pairs(crossed, shift(0, -1, lambda c: c % RING == 1))
+    around = by_pairs(row[0], shift(0, -2, lambda c: c == 1))
 
     column = lax.axis_index("pcol")
-    mask_handed = mask_of(handed, panel)
-    known = early(
-        last, pair_lists, pair_counts, [left_mask, mask_of(one_above, panel)],
-        [packed, one_above], right_blocks,
-    )
-    mask_one = jnp.where(column % RING == 0, mask_handed, mask_of(one_below, panel))
+    place_in_row = column % RING
+    row_masks = row[:, CAP_L * BS, :panel].astype(jnp.int32)
+
+    def row_mask(step):
+        return row_masks[(place_in_row + step) % RING]
+
+    crossed_mask = mask_of(crossed, panel)
+    masks = [
+        jnp.where(place_in_row >= 2, row_mask(-2), crossed_mask),
+        jnp.where(place_in_row >= 1, row_mask(-1), mask_of(handed, panel)),
+        jnp.where(
+            column == last,
+            mask_of(around, panel),
+            jnp.where(place_in_row < RING - 1, row_mask(1), crossed_mask),
+        ),
+    ]
+    known = own_step(pair_lists, pair_counts, left_mask, packed, right_blocks)
     laid, known = late(
-        last, pair_lists, pair_counts, [mask_of(two_below, panel), mask_one, mask_handed],
-        [two_below, one_below, handed], right_blocks, known,
+        last, pair_lists, pair_counts, masks,
+        [row.reshape(RING * ROWS, BS), crossed, handed, around], right_blocks, known,
     )
     return last_product(laid, right_before.reshape(half * BS, BS), known)
 

time: 103 us -> 118 us (1.15)
  the two profiles are of different devices: /device:TPU:80 before, /device:TPU:8 now
where the time goes in v6:
time: 118 us
  waiting for transfers between devices  70.5 us (60%)
  starting transfers between devices  21.2 us (18%)
  between operations  13.6 us (12%)
  Pallas kernels  8.65 us (7%)
  local copies, waits for them, and re-layouts  3.05 us (3%)
    ppermute x4, waiting for transfers between devices, by_pairs(): return lax.ppermute(array, ('prow', 'pcol'), pairs)  70.5 us
    ppermute x4, starting transfers between devices, by_pairs(): return lax.ppermute(array, ('prow', 'pcol'), pairs)  21.2 us
    pallas_call x1, Pallas kernels, stage(): pl.pallas_call(stage_kernel, out_shape=[jax.ShapeDtypeStruct((CAP_L * BS...  3.01 us
  transfers between devices with their start and end apart: 5, of which 2 were waited for; matrix products, arithmetic and copies ran while one was open for 2% of the time, Pallas kernels for 3%

profile of v6, /device:TPU:8, one launch (start us, length us, event | category | flops | bytes accessed | tf_op | source)
XLA Modules:
  0.0 117.8 jit_solution(545125192376063003)
XLA Ops:
  6.5 0.0 copy-start.1
  6.5 0.0 copy-start.3
  6.5 0.0 copy-start.5
  6.5 0.0 copy-start.4
  6.5 0.0 all-gather.3.cloned.1.call-start
  6.6 3.0 %pack_and_cut.1 = (bf16[2448,128]{1,0:T(8,128)(2,1)}, bf16[12,128,128]{2,1,0:T(8,128)(2,1)}) custom-call(s32[38]{0:T(128)} %mask_ref.3, bf16[38,128,128]{2,1,0:T(8,128)(2,1)} %left_ref.1, bf16[24,128,128]{2,1,0:T(8,128)(2,1)} %right_ref.5), custom_call_target="tpu_custom_call" | custom-call | bytes 1024 | tf_op jit(solution)/shard_map/pack_and_cut/pallas_call | solution.py:62
  9.6 0.0 all-gather.3.cloned.1.call-update
  9.6 1.3 %collective-permute-start = (bf16[2448,128]{1,0:T(8,128)(2,1)}, bf16[2448,128]{1,0:T(8,128)(2,1)}, u32[]{:S(2)}, u32[]{:S(2)}) collective-permute-start(bf16[2448,128]{1,0:T(8,128)(2,1)} %get-tuple-element.9.panel_ref), channel_id=1, source_target_pairs={{2,4},{3,5},{6,8},{7,9},{10,12},{11,13},{14,16},{15,17},{18,20},{1... | collective-permute-start | bytes 1880072 | tf_op jit(solution)/shard_map/ppermute | solution.py:27
  10.9 1.9 %collective-permute-start.3 = (bf16[12,128,128]{2,1,0:T(8,128)(2,1)}, bf16[12,128,128]{2,1,0:T(8,128)(2,1)}, u32[]{:S(2)}, u32[]{:S(2)}) collective-permute-start(bf16[12,128,128]{2,1,0:T(8,128)(2,1)} %get-tuple-element.11), channel_id=1, source_target_pairs={{0,64},{1,65},{2,66},{3,67},{4,68},{5,69},{6,70},{7,71},{8,72},{9,... | collective-permute-start | bytes 1179656 | tf_op jit(solution)/shard_map/ppermute | solution.py:27
  12.9 0.0 copy-done.5
  12.9 60.4 %collective-permute-done.crossed_ref = bf16[2448,128]{1,0:T(8,128)(2,1)} collective-permute-done((bf16[2448,128]{1,0:T(8,128)(2,1)}, bf16[2448,128]{1,0:T(8,128)(2,1)}, u32[]{:S(2)}, u32[]{:S(2)}) %collective-permute-start) | collective-permute-done | bytes 626720 | tf_op jit(solution)/shard_map/ppermute | solution.py:27
  73.3 7.6 %collective-permute-start.1 = (bf16[2448,128]{1,0:T(8,128)(2,1)}, bf16[2448,128]{1,0:T(8,128)(2,1)}, u32[]{:S(2)}, u32[]{:S(2)}) collective-permute-start(bf16[2448,128]{1,0:T(8,128)(2,1)} %collective-permute-done.crossed_ref), channel_id=1, source_target_pairs={{1,0},{5,4},{9,8},{13,12},{17,16},{21,20},{25,24},{29,28},{33,32},... | collective-permute-start | bytes 1880072 | tf_op jit(solution)/shard_map/ppermute | solution.py:27
  80.9 0.0 all-gather.3.cloned.1.call-done.row_ref
  80.9 2.0 %slice.24 = bf16[2448,128]{1,0:T(8,128)(2,1)} slice(bf16[9792,128]{1,0:T(8,128)(2,1)} %all-gather.3.cloned.1.call-done.row_ref), slice={[0:2448], [0:128]} | slice | bytes 1253376 | tf_op jit(solution)/shard_map/slice | solution.py:257
  82.8 0.0 copy-start
  82.8 10.4 %collective-permute-start.2 = (bf16[2448,128]{1,0:T(8,128)(2,1)}, bf16[2448,128]{1,0:T(8,128)(2,1)}, u32[]{:S(2)}, u32[]{:S(2)}) collective-permute-start(bf16[2448,128]{1,0:T(8,128)(2,1)} %slice.24), channel_id=1, source_target_pairs={{1,63},{65,127},{129,191},{193,255},{257,319},{321,383},{385,447},... | collective-permute-start | bytes 1880072 | tf_op jit(solution)/shard_map/ppermute | solution.py:27
  93.2 0.0 copy-done.1
  93.2 0.0 copy-done.3
  93.2 0.0 copy-done.4
  93.3 0.0 copy-start.2
  93.3 1.1 copy-done.2
  94.3 1.5 %own_step.1.own_ref = f32[256,128]{1,0:T(8,128)S(1)} custom-call(s32[1,4,3,12]{3,2,1,0:T(4,128)S(1)} %copy.7.lists_ref, s32[1,4]{1,0:T(1,128)S(1)} %copy-done.4, s32[38]{0:T(128)S(1)} %copy-done.3, bf16[2448,128]{1,0:T(8,128)(2,1)S(1)} %copy-done.2, bf16[24,128,128]{2,1,0:T(8,128)(2,1)S(1)} %copy-done.1), custom_call_target="tpu_custom_call" | custom-call | flops 34359738368 | bytes 1048576 | tf_op jit(solution)/shard_map/own_step/pallas_call | solution.py:154
  95.9 0.0 copy-done
  95.9 0.0 collective-permute-done.1.handed_ref
  95.9 10.1 %collective-permute-done.2.around_ref = bf16[2448,128]{1,0:T(8,128)(2,1)} collective-permute-done((bf16[2448,128]{1,0:T(8,128)(2,1)}, bf16[2448,128]{1,0:T(8,128)(2,1)}, u32[]{:S(2)}, u32[]{:S(2)}) %collective-permute-start.2) | collective-permute-done | bytes 626720 | tf_op jit(solution)/shard_map/ppermute | solution.py:27
  106.0 0.7 broadcast_select_fusion.1
  106.7 2.2 %other_steps.1 = (bf16[256,1536]{1,0:T(8,128)(2,1)S(1)}, f32[256,128]{1,0:T(8,128)S(1)}) custom-call(s32[1,4,3,12]{3,2,1,0:T(4,128)S(1)} %copy.7.lists_ref, s32[1,4]{1,0:T(1,128)S(1)} %copy-done.4, s32[38]{0:T(128)S(1)} %get-tuple-element.14.two_mask_ref, s32[38]{0:T(128)S(1)} %get-tuple-element.15.one_mask_ref, s32[38]{0:T(128)S(1)} %get-tuple-element.13.above_mask_ref, ...), custom_call_target="tpu_custom_call" | custom-call | bytes 1024 | tf_op jit(solution)/shard_map/other_steps/pallas_call | solution.py:202
  108.9 0.0 collective-permute-done.3
  108.9 2.0 %last_product.1 = bf16[256,128]{1,0:T(8,128)(2,1)} custom-call(bf16[256,1536]{1,0:T(8,128)(2,1)S(1)} %get-tuple-element.10.left_ref, bf16[1536,128]{1,0:T(8,128)(2,1)} %bitcast.8.right_ref, f32[256,128]{1,0:T(8,128)S(1)} %get-tuple-element.12.known_ref), custom_call_target="tpu_custom_call" | custom-call | bytes 1024 | tf_op jit(solution)/shard_map/last_product/pallas_call | solution.py:223
  (2 shorter events, 0.0 us)
Async XLA Ops:
  6.5 86.7 %copy-start.1 = (bf16[24,128,128]{2,1,0:T(8,128)(2,1)S(1)}, bf16[24,128,128]{2,1,0:T(8,128)(2,1)}, u32[]{:S(2)}) copy-start(bf16[24,128,128]{2,1,0:T(8,128)(2,1)} %right_ref.5) | copy-start | bytes 2359300
  6.5 86.7 %copy-start.3 = (s32[38]{0:T(128)S(1)}, s32[38]{0:T(128)}, u32[]{:S(2)}) copy-start(s32[38]{0:T(128)} %mask_ref.3) | copy-start | bytes 460
  6.5 6.3 %copy-start.5 = (s32[1,4,3,12]{3,1,2,0:T(4,128)S(1)}, s32[1,4,3,12]{3,1,2,0:T(4,128)}, u32[]{:S(2)}) copy-start(s32[1,4,3,12]{3,1,2,0:T(4,128)} %param.8) | copy-start | bytes 1732
  6.5 86.7 %copy-start.4 = (s32[1,4]{1,0:T(1,128)S(1)}, s32[1,4]{1,0:T(1,128)}, u32[]{:S(2)}) copy-start(s32[1,4]{1,0:T(1,128)} %counts_ref.3) | copy-start | bytes 52
  6.5 74.3 %all-gather.3.cloned.1.call-start = ((), (), s32[]{:S(2)}) async-start(), calls=%async_computation | async-start | bytes 3133440 | tf_op jit(solution)/shard_map/all_gather | solution.py:254
  9.6 63.7 %collective-permute-start = (bf16[2448,128]{1,0:T(8,128)(2,1)}, bf16[2448,128]{1,0:T(8,128)(2,1)}, u32[]{:S(2)}, u32[]{:S(2)}) collective-permute-start(bf16[2448,128]{1,0:T(8,128)(2,1)} %get-tuple-element.9.panel_ref), channel_id=1, source_target_pairs={{2,4},{3,5},{6,8},{7,9},{10,12},{11,13},{14,16},{15,17},{18,20},{1... | collective-permute-start | bytes 1880072 | tf_op jit(solution)/shard_map/ppermute | solution.py:27
  10.9 98.0 %collective-permute-start.3 = (bf16[12,128,128]{2,1,0:T(8,128)(2,1)}, bf16[12,128,128]{2,1,0:T(8,128)(2,1)}, u32[]{:S(2)}, u32[]{:S(2)}) collective-permute-start(bf16[12,128,128]{2,1,0:T(8,128)(2,1)} %get-tuple-element.11), channel_id=1, source_target_pairs={{0,64},{1,65},{2,66},{3,67},{4,68},{5,69},{6,70},{7,71},{8,72},{9,... | collective-permute-start | bytes 1179656 | tf_op jit(solution)/shard_map/ppermute | solution.py:27
  73.3 22.6 %collective-permute-start.1 = (bf16[2448,128]{1,0:T(8,128)(2,1)}, bf16[2448,128]{1,0:T(8,128)(2,1)}, u32[]{:S(2)}, u32[]{:S(2)}) collective-permute-start(bf16[2448,128]{1,0:T(8,128)(2,1)} %collective-permute-done.crossed_ref), channel_id=1, source_target_pairs={{1,0},{5,4},{9,8},{13,12},{17,16},{21,20},{25,24},{29,28},{33,32},... | collective-permute-start | bytes 1880072 | tf_op jit(solution)/shard_map/ppermute | solution.py:27
  82.8 13.1 %copy-start = (bf16[9792,128]{1,0:T(8,128)(2,1)S(1)}, bf16[9792,128]{1,0:T(8,128)(2,1)}, u32[]{:S(2)}) copy-start(bf16[9792,128]{1,0:T(8,128)(2,1)} %all-gather.3.cloned.1.call-done.row_ref) | copy-start | bytes 7520260
  82.8 23.2 %collective-permute-start.2 = (bf16[2448,128]{1,0:T(8,128)(2,1)}, bf16[2448,128]{1,0:T(8,128)(2,1)}, u32[]{:S(2)}, u32[]{:S(2)}) collective-permute-start(bf16[2448,128]{1,0:T(8,128)(2,1)} %slice.24), channel_id=1, source_target_pairs={{1,63},{65,127},{129,191},{193,255},{257,319},{321,383},{385,447},... | collective-permute-start | bytes 1880072 | tf_op jit(solution)/shard_map/ppermute | solution.py:27
  93.3 1.1 copy-start.2
Sparse Core Ops, SparseCore 0:
  10.1 64.9 all-gather.2

commit v7 on v4

v7 whole, which is shorter than its diff:
```python
import functools

import jax
import jax.numpy as jnp
from jax import lax
from jax.experimental import pallas as pl
from jax.experimental.pallas import tpu as pltpu
from jax.sharding import PartitionSpec as P

BR = 2
BS = 128
CAP_L = 19
CAPM = 6
PCAP = 12
META = 16
RING = 4
CHEAP = pl.CostEstimate(flops=0, bytes_accessed=1024, transcendentals=0)
DEAR = pl.CostEstimate(flops=1 << 35, bytes_accessed=1 << 20, transcendentals=0)
ROOM = pltpu.CompilerParams(vmem_limit_bytes=16 << 20)
WIDE = pltpu.CompilerParams(vmem_limit_bytes=62 << 20)
SMEM = pl.BlockSpec(memory_space=pltpu.SMEM)
VMEM = pl.BlockSpec(memory_space=pltpu.VMEM)
ANY = pl.BlockSpec(memory_space=pl.ANY)


def by_pairs(array, pairs):
    return lax.ppermute(array, ("prow", "pcol"), pairs)


def pack_into(mask_ref, left_ref, packed_ref, sem):
    panel = left_ref.shape[0]
    slot = jnp.int32(0)
    for q in range(panel):
        taken = jnp.logical_and(mask_ref[q] != 0, slot < CAP_L)

        @pl.when(taken)
        def _(q=q, slot=slot):
            row = pl.multiple_of(slot * BS, BS)
            pltpu.make_async_copy(left_ref.at[q], packed_ref.at[pl.ds(row, BS)], sem).start()

        slot = slot + taken.astype(jnp.int32)

    @pl.loop(slot, CAP_L)
    def _(spare):
        row = pl.multiple_of(spare * BS, BS)
        pltpu.make_async_copy(left_ref.at[0], packed_ref.at[pl.ds(row, BS)], sem).start()

    lane = lax.broadcasted_iota(jnp.int32, (META, BS), 1)
    mask = jnp.zeros((META, BS), jnp.float32)
    for q in range(panel):
        mask = jnp.where(lane == q, (mask_ref[q] != 0).astype(jnp.float32), mask)
    packed_ref[pl.ds(CAP_L * BS, META), :] = mask.astype(packed_ref.dtype)


def wait_packed(packed_ref, sem):
    blocks = packed_ref.at[pl.ds(0, CAP_L * BS)]
    pltpu.make_async_copy(blocks, blocks, sem).wait()


def first_kernel(
    mask_ref, lists_ref, counts_ref, left_ref, right_ref,
    packed_ref, part_ref, ask_ref, sem, part_sem, ask_sem,
):
    half = part_ref.shape[0]
    part = pltpu.make_async_copy(right_ref.at[pl.ds(half, half)], part_ref, part_sem)
    part.start()
    pack_into(mask_ref, left_ref, packed_ref, sem)
    copies = []
    for m in range(CAPM):
        target = ask_ref.at[pl.ds(m * BS, BS)]
        copies.append(pltpu.make_async_copy(right_ref.at[CAPM + m], target, ask_sem.at[m]))
        copies[-1].start()
    lane = lax.broadcasted_iota(jnp.int32, (META, BS), 1)
    pairs = lists_ref.shape[3]
    row = jnp.where(lane == 3 * pairs, counts_ref[0, 3].astype(jnp.float32), 0.0)
    for q in range(3 * pairs):
        row = jnp.where(lane == q, lists_ref[0, 3, q // pairs, q % pairs].astype(jnp.float32), row)
    ask_ref[pl.ds(CAPM * BS, META), :] = row.astype(ask_ref.dtype)
    wait_packed(packed_ref, sem)
    part.wait()
    for copy in copies:
        copy.wait()


def second_kernel(mask_ref, left_ref, after_ref, packed_ref, sem):
    del after_ref
    pack_into(mask_ref, left_ref, packed_ref, sem)
    wait_packed(packed_ref, sem)


def first_stage(left_mask, lists, counts, left_blocks, right_blocks):
    return pl.pallas_call(
        first_kernel,
        out_shape=[
            jax.ShapeDtypeStruct((CAP_L * BS + META, BS), jnp.bfloat16),
            jax.ShapeDtypeStruct((2 * CAPM, BS, BS), jnp.bfloat16),
            jax.ShapeDtypeStruct((CAPM * BS + META, BS), jnp.bfloat16),
        ],
        in_specs=[SMEM] * 3 + [ANY] * 2,
        out_specs=[VMEM] * 3,
        scratch_shapes=[
            pltpu.SemaphoreType.DMA, pltpu.SemaphoreType.DMA, pltpu.SemaphoreType.DMA((CAPM,))
        ],
        compiler_params=WIDE,
        cost_estimate=CHEAP,
        name="pack_and_cut",
    )(left_mask, lists, counts, left_blocks, right_blocks)


def second_stage(left_mask, left_blocks, after):
    return pl.pallas_call(
        second_kernel,
        out_shape=jax.ShapeDtypeStruct((CAP_L * BS + META, BS), jnp.bfloat16),
        in_specs=[SMEM, ANY, ANY],
        out_specs=VMEM,
        scratch_shapes=[pltpu.SemaphoreType.DMA],
        compiler_params=WIDE,
        cost_estimate=CHEAP,
        name="pack_again",
    )(left_mask, left_blocks, after)


def mask_of(packed, panel):
    return packed[CAP_L * BS, :panel].astype(jnp.int32)


def place(u, at, lists_ref, counts_ref, mask_ref, sources, into_ref, rank_ref, sem):
    column = lax.axis_index("pcol")
    run = jnp.int32(0)
    for q in range(mask_ref.shape[0]):
        rank_ref[q] = run
        run = run + (mask_ref[q] != 0).astype(jnp.int32)
    held = [(panel_ref, where(column)) for panel_ref, where in sources]
    total = jnp.int32(0)
    for p in range(lists_ref.shape[3]):
        block = lists_ref[0, u, 0, p]
        slot = lists_ref[0, u, 1, p]
        o = lists_ref[0, u, 2, p]
        live = jnp.logical_and(p < counts_ref[0, u], mask_ref[block] != 0)
        row = pl.multiple_of(jnp.minimum(rank_ref[block], CAP_L - 1) * BS, BS)
        down = pl.multiple_of(o * BS, BS)
        along = pl.multiple_of((at * CAPM + slot) * BS, BS)
        target = into_ref.at[pl.ds(down, BS), pl.ds(along, BS)]
        for panel_ref, here in held:
            taken = jnp.logical_and(live, here)

            @pl.when(taken)
            def _(panel_ref=panel_ref, row=row, target=target):
                pltpu.make_async_copy(panel_ref.at[pl.ds(row, BS)], target, sem).start()

            total = total + taken.astype(jnp.int32)
    return total


def drain(total, panel_ref, into_ref, sem):
    @pl.loop(0, total)
    def _(_):
        one = panel_ref.at[pl.ds(0, BS)]
        pltpu.make_async_copy(one, into_ref.at[pl.ds(0, BS), pl.ds(0, BS)], sem).wait()


def multiply(left_ref, right_ref, total_ref):
    for m in range(right_ref.shape[0]):
        total_ref[...] += jnp.dot(
            left_ref[:, m * BS : (m + 1) * BS], right_ref[m], preferred_element_type=jnp.float32
        )


def one_kernel(
    u, first, here, lists_ref, counts_ref, mask_ref, panel_ref, right_ref, *refs,
):
    before_ref = refs[0] if len(refs) == 7 else None
    known_ref, left_ref, held_ref, rank_ref, sem, right_sem = refs[-6:]
    fetch_right = pltpu.make_async_copy(
        right_ref.at[pl.ds(first, CAPM)], held_ref, right_sem
    )
    fetch_right.start()
    left_ref[...] = jnp.zeros_like(left_ref)
    source = ((panel_ref, here),)
    total = place(u, 0, lists_ref, counts_ref, mask_ref, source, left_ref, rank_ref, sem)
    drain(total, panel_ref, left_ref, sem)
    fetch_right.wait()
    known_ref[...] = jnp.zeros_like(known_ref) if before_ref is None else before_ref[...]
    multiply(left_ref, held_ref, known_ref)


def one_step(u, first, here, lists, counts, mask, panel, right, before, cost, name):
    more = [] if before is None else [before]
    return pl.pallas_call(
        functools.partial(one_kernel, u, first, here),
        out_shape=jax.ShapeDtypeStruct((BR * BS, BS), jnp.float32),
        in_specs=[SMEM] * 3 + [ANY] * 2 + [VMEM] * len(more),
        out_specs=VMEM,
        scratch_shapes=[
            pltpu.VMEM((BR * BS, CAPM * BS), jnp.bfloat16),
            pltpu.VMEM((CAPM, BS, BS), jnp.bfloat16),
            pltpu.SMEM((mask.shape[0],), jnp.int32),
            pltpu.SemaphoreType.DMA,
            pltpu.SemaphoreType.DMA,
        ],
        compiler_params=ROOM,
        cost_estimate=cost,
        name=name,
    )(lists, counts, mask, panel, right, *more)


def late_kernel(
    lists_ref, counts_ref, two_mask_ref, one_mask_ref, two_ref, one_ref, handed_ref,
    early_ref, answer_ref, laid_ref, known_ref, rank_ref, sem,
):
    laid_ref[...] = jnp.zeros_like(laid_ref)
    two = ((two_ref, lambda c: c >= 0),)
    one = (
        (one_ref, lambda c: lax.rem(c, RING) != 0),
        (handed_ref, lambda c: lax.rem(c, RING) == 0),
    )
    total = place(0, 0, lists_ref, counts_ref, two_mask_ref, two, laid_ref, rank_ref, sem)
    total += place(1, 1, lists_ref, counts_ref, one_mask_ref, one, laid_ref, rank_ref, sem)
    known_ref[...] = early_ref[...] + answer_ref[...]
    drain(total, two_ref, laid_ref, sem)


def late(lists, counts, masks, panels, known, answer):
    return pl.pallas_call(
        late_kernel,
        out_shape=[
            jax.ShapeDtypeStruct((BR * BS, 2 * CAPM * BS), jnp.bfloat16),
            jax.ShapeDtypeStruct((BR * BS, BS), jnp.float32),
        ],
        in_specs=[SMEM] * 4 + [ANY] * 3 + [VMEM] * 2,
        out_specs=[VMEM, VMEM],
        scratch_shapes=[pltpu.SMEM((masks[0].shape[0],), jnp.int32), pltpu.SemaphoreType.DMA],
        compiler_params=ROOM,
        cost_estimate=CHEAP,
        name="lay_below",
    )(lists, counts, *masks, *panels, known, answer)


def last_kernel(left_ref, right_ref, known_ref, out_ref):
    new = jnp.dot(left_ref[...], right_ref[...], preferred_element_type=jnp.float32)
    out_ref[...] = (known_ref[...] + new).astype(out_ref.dtype)


def last_product(left, right, known):
    return pl.pallas_call(
        last_kernel,
        out_shape=jax.ShapeDtypeStruct(known.shape, jnp.bfloat16),
        in_specs=[VMEM] * 3,
        out_specs=VMEM,
        compiler_params=ROOM,
        cost_estimate=CHEAP,
        name="last_product",
    )(left, right, known)


def on_device(n_row, n_col, left_blocks, left_mask, right_blocks, pair_lists, pair_counts):
    panel = left_blocks.shape[0]
    last = n_col - 1
    half = 2 * CAPM

    def shift(rows, cols, chosen):
        return [
            (r * n_col + c, (r + rows) % n_row * n_col + (c + cols) % n_col)
            for r in range(n_row)
            for c in range(n_col)
            if chosen(c)
        ]

    def always(c):
        return c >= 0

    packed, sent_right, ask = first_stage(
        left_mask, pair_lists, pair_counts, left_blocks, right_blocks
    )
    two_below = by_pairs(packed, shift(0, 2, always))
    right_before = by_pairs(sent_right, shift(1, 0, always))
    mark = by_pairs(packed[:META], [(0, 1)])
    again = second_stage(left_mask, left_blocks, mark)
    one_above = by_pairs(again, shift(0, -1, lambda c: c > 0))
    one_below = by_pairs(again, shift(0, 1, lambda c: c % RING < RING - 1))
    asked = by_pairs(ask, shift(0, 1, lambda c: c == last))
    handed = by_pairs(two_below, shift(0, -1, lambda c: c % RING == 1))

    listed = asked[CAPM * BS, : 3 * PCAP + 1].astype(jnp.int32)
    answer = one_step(
        0, 0, always, listed[: 3 * PCAP].reshape(1, 1, 3, PCAP), listed[3 * PCAP :].reshape(1, 1),
        left_mask, packed, asked[: CAPM * BS].reshape(CAPM, BS, BS), None, CHEAP, "answer",
    )
    answer = by_pairs(answer, shift(0, -1, lambda c: c == 0))

    known = one_step(
        2, 0, always, pair_lists, pair_counts, left_mask, packed, right_blocks, None,
        DEAR, "own_step",
    )
    known = one_step(
        3, CAPM, lambda c: c < last, pair_lists, pair_counts, mask_of(one_above, panel),
        one_above, right_blocks, known, CHEAP, "step_above",
    )
    first = lax.axis_index("pcol") % RING == 0
    mask_one = jnp.where(first, mask_of(handed, panel), mask_of(one_below, panel))
    laid, known = late(
        pair_lists, pair_counts, [mask_of(two_below, panel), mask_one],
        [two_below, one_below, handed], known, answer,
    )
    return last_product(laid, right_before.reshape(half * BS, BS), known)


def solution(mesh):
    in_specs = (
        P(("prow", "pcol"), None, None),
        P(("prow", "pcol")),
        P(("prow", "pcol"), None, None),
        P(("prow", "pcol"), None, None, None),
        P(("prow", "pcol"), None),
    )
    return jax.shard_map(
        functools.partial(on_device, mesh.shape["prow"], mesh.shape["pcol"]),
        mesh=mesh,
        in_specs=in_specs,
        out_specs=P("prow", "pcol"),
        check_vma=False,
    )
```

time: 103 us -> 92.5 us (0.90)
  the two profiles are of different devices: /device:TPU:80 before, /device:TPU:1022 now
where the time goes in v7:
time: 92.5 us; the launch traced here: 91.8 us
  waiting for transfers between devices  48 us (52%)
  starting transfers between devices  25.5 us (28%)
  Pallas kernels  13.3 us (14%)
  local copies, waits for them, and re-layouts  3.39 us (4%)
  other arithmetic  1.36 us (1%)
    ppermute x8, waiting for transfers between devices, by_pairs(): return lax.ppermute(array, ('prow', 'pcol'), pairs)  48 us
    ppermute x8, starting transfers between devices, by_pairs(): return lax.ppermute(array, ('prow', 'pcol'), pairs)  25.5 us
    pallas_call x3, Pallas kernels, one_step(): pl.pallas_call(functools.partial(one_kernel, u, first, here), out_shape=j...  4.82 us
    pallas_call x1, Pallas kernels, first_stage(): pl.pallas_call(first_kernel, out_shape=[jax.ShapeDtypeStruct((CAP_L * BS...  3.19 us
    pallas_call x1, Pallas kernels, second_stage(): pl.pallas_call(second_kernel, out_shape=jax.ShapeDtypeStruct((CAP_L * BS...  2.71 us
    unnamed x13, local copies, waits for them, and re-layouts  1.9 us
  transfers between devices with their start and end apart: 8, of which 3 were waited for; matrix products, arithmetic and copies ran while one was open for 2% of the time, Pallas kernels for 10%

profile of v7, /device:TPU:1022, one launch (start us, length us, event | category | flops | bytes accessed | tf_op | source)
XLA Modules:
  0.0 91.8 jit_solution(15289225647772530345)
XLA Ops:
  0.0 1.3 %copy.13.lists_ref = s32[1,4,3,12]{3,2,1,0:T(4,128)} copy(s32[1,4,3,12]{3,1,2,0:T(4,128)} %param.8) | data formatting | bytes 1152 | tf_op args[3]
  1.3 3.2 %pack_and_cut.1 = (bf16[2448,128]{1,0:T(8,128)(2,1)}, bf16[12,128,128]{2,1,0:T(8,128)(2,1)}, bf16[784,128]{1,0:T(8,128)(2,1)}) custom-call(s32[38]{0:T(128)} %mask_ref.7, s32[1,4,3,12]{3,2,1,0:T(4,128)} %copy.13.lists_ref, s32[1,4]{1,0:T(1,128)} %counts_ref.7, bf16[38,128,128]{2,1,0:T(8,128)(2,1)} %left_ref.3, bf16[24,128,128]{2,1,0:T(8,128)(2,1)} %right_ref.5), custom_call_target="tpu_custom_call" | custom-call | bytes 1024 | tf_op jit(solution)/shard_map/pack_and_cut/pallas_call | solution.py:92
  4.5 0.0 copy-start
  4.5 0.0 copy-start.1
  4.5 0.0 copy-start.2
  4.5 0.0 copy-start.3
  4.5 0.0 copy-start.4
  4.5 0.8 slice.31
  5.3 0.6 collective-permute-start.2
  6.0 13.4 %collective-permute-start = (bf16[2448,128]{1,0:T(8,128)(2,1)}, bf16[2448,128]{1,0:T(8,128)(2,1)}, u32[]{:S(2)}, u32[]{:S(2)}) collective-permute-start(bf16[2448,128]{1,0:T(8,128)(2,1)} %get-tuple-element.10.panel_ref), channel_id=1, source_target_pairs={{0,2},{1,3},{2,4},{3,5},{4,6},{5,7},{6,8},{7,9},{8,10},{9,11},{10,... | collective-permute-start | bytes 1880072 | tf_op jit(solution)/shard_map/ppermute | solution.py:27
  19.4 4.1 %collective-permute-start.5 = (bf16[784,128]{1,0:T(8,128)(2,1)}, bf16[784,128]{1,0:T(8,128)(2,1)S(1)}, u32[]{:S(2)}, u32[]{:S(2)}) collective-permute-start(bf16[784,128]{1,0:T(8,128)(2,1)} %get-tuple-element.11), channel_id=1, source_target_pairs={{63,0},{127,64},{191,128},{255,192},{319,256},{383,320},{447,384},... | collective-permute-start | bytes 602120 | tf_op jit(solution)/shard_map/ppermute | solution.py:27
  23.5 1.9 %collective-permute-start.7 = (bf16[12,128,128]{2,1,0:T(8,128)(2,1)}, bf16[12,128,128]{2,1,0:T(8,128)(2,1)S(1)}, u32[]{:S(2)}, u32[]{:S(2)}) collective-permute-start(bf16[12,128,128]{2,1,0:T(8,128)(2,1)} %get-tuple-element.13), channel_id=1, source_target_pairs={{0,64},{1,65},{2,66},{3,67},{4,68},{5,69},{6,70},{7,71},{8,72},{9,... | collective-permute-start | bytes 1179656 | tf_op jit(solution)/shard_map/ppermute | solution.py:27
  25.4 0.0 collective-permute-done.2.after_ref
  25.5 0.0 copy-start.5
  25.5 0.6 copy-done.5
  26.0 2.7 %pack_again.1 = bf16[2448,128]{1,0:T(8,128)(2,1)} custom-call(s32[38]{0:T(128)} %mask_ref.7, bf16[38,128,128]{2,1,0:T(8,128)(2,1)} %left_ref.3, bf16[16,128]{1,0:T(8,128)(2,1)} %copy-done.5), custom_call_target="tpu_custom_call" | custom-call | bytes 1024 | tf_op jit(solution)/shard_map/pack_again/pallas_call | solution.py:111
  28.8 2.1 %collective-permute-start.4 = (bf16[2448,128]{1,0:T(8,128)(2,1)}, bf16[2448,128]{1,0:T(8,128)(2,1)}, u32[]{:S(2)}, u32[]{:S(2)}) collective-permute-start(bf16[2448,128]{1,0:T(8,128)(2,1)} %pack_again.1), channel_id=1, source_target_pairs={{1,0},{2,1},{3,2},{4,3},{5,4},{6,5},{7,6},{8,7},{9,8},{10,9},{11,1... | collective-permute-start | bytes 1880072 | tf_op jit(solution)/shard_map/ppermute | solution.py:27
  30.9 0.0 copy-done
  30.9 0.0 copy-done.1
  30.9 0.0 copy-done.2
  30.9 0.0 copy-done.3
  30.9 0.0 copy-done.4
  30.9 1.5 %own_step.1.refs_0_ = f32[256,128]{1,0:T(8,128)S(1)} custom-call(s32[1,4,3,12]{3,2,1,0:T(4,128)S(1)} %copy-done.2, s32[1,4]{1,0:T(1,128)S(1)} %copy-done.3, s32[38]{0:T(128)S(1)} %copy-done.4, bf16[2448,128]{1,0:T(8,128)(2,1)S(1)} %copy-done.1, bf16[24,128,128]{2,1,0:T(8,128)(2,1)S(1)} %copy-done), custom_call_target="tpu_custom_call" | custom-call | flops 34359738368 | bytes 1048576 | tf_op jit(solution)/shard_map/own_step/pallas_call | solution.py:189
  32.4 1.3 %collective-permute-start.3 = (bf16[2448,128]{1,0:T(8,128)(2,1)}, bf16[2448,128]{1,0:T(8,128)(2,1)S(1)}, u32[]{:S(2)}, u32[]{:S(2)}) collective-permute-start(bf16[2448,128]{1,0:T(8,128)(2,1)} %pack_again.1), channel_id=1, source_target_pairs={{0,1},{1,2},{2,3},{4,5},{5,6},{6,7},{8,9},{9,10},{10,11},{12,13},{... | collective-permute-start | bytes 1880072 | tf_op jit(solution)/shard_map/ppermute | solution.py:27
  33.7 21.9 %collective-permute-done.two_ref = bf16[2448,128]{1,0:T(8,128)(2,1)} collective-permute-done((bf16[2448,128]{1,0:T(8,128)(2,1)}, bf16[2448,128]{1,0:T(8,128)(2,1)}, u32[]{:S(2)}, u32[]{:S(2)}) %collective-permute-start) | collective-permute-done | bytes 626720 | tf_op jit(solution)/shard_map/ppermute | solution.py:27
  55.7 0.7 collective-permute-start.1
  56.4 4.8 %collective-permute-done.5 = bf16[784,128]{1,0:T(8,128)(2,1)S(1)} collective-permute-done((bf16[784,128]{1,0:T(8,128)(2,1)}, bf16[784,128]{1,0:T(8,128)(2,1)S(1)}, u32[]{:S(2)}, u32[]{:S(2)}) %collective-permute-start.5) | collective-permute-done | bytes 200736 | tf_op jit(solution)/shard_map/ppermute | solution.py:27
  61.1 0.6 slice.36.counts_ref
  61.7 0.1 reshape.23.lists_ref
  61.8 2.0 %answer.1 = f32[256,128]{1,0:T(8,128)S(1)} custom-call(s32[1,1,3,12]{3,2,1,0:T(4,128)S(1)} %reshape.23.lists_ref, s32[1,1]{1,0:T(1,128)} %slice.36.counts_ref, s32[38]{0:T(128)S(1)} %copy-done.4, bf16[2448,128]{1,0:T(8,128)(2,1)S(1)} %copy-done.1, bf16[6,128,128]{2,1,0:T(8,128)(2,1)S(1)} %bitcast.14), custom_call_target="tpu_custom_call" | custom-call | bytes 1024 | tf_op jit(solution)/shard_map/answer/pallas_call | solution.py:189
  63.8 1.3 %collective-permute-start.6 = (f32[256,128]{1,0:T(8,128)S(1)}, f32[256,128]{1,0:T(8,128)S(1)}, u32[]{:S(2)}, u32[]{:S(2)}) collective-permute-start(f32[256,128]{1,0:T(8,128)S(1)} %answer.1), channel_id=1, source_target_pairs={{0,63},{64,127},{128,191},{192,255},{256,319},{320,383},{384,447},... | collective-permute-start | bytes 393224 | tf_op jit(solution)/shard_map/ppermute | solution.py:27
  65.1 0.7 fusion.2.two_mask_ref
  65.8 0.0 collective-permute-done.4.panel_ref
  65.8 0.7 fusion.1.mask_ref
  66.5 1.4 %step_above.1.early_ref = f32[256,128]{1,0:T(8,128)S(1)} custom-call(s32[1,4,3,12]{3,2,1,0:T(4,128)S(1)} %copy-done.2, s32[1,4]{1,0:T(1,128)S(1)} %copy-done.3, s32[38]{0:T(128)S(1)} %fusion.1.mask_ref, bf16[2448,128]{1,0:T(8,128)(2,1)} %collective-permute-done.4.panel_ref, bf16[24,128,128]{2,1,0:T(8,128)(2,1)S(1)} %copy-done, f32[256,128]{1,0:T(8,128)S(1)} %own_step.1.refs_0_), custom_call_target="tpu_custom_call" | custom-call | bytes 1024 | tf_op jit(solution)/shard_map/step_above/pallas_call | solution.py:189
  67.8 0.0 collective-permute-done.3.one_ref
  67.9 0.0 collective-permute-done.1.handed_ref
  67.9 21.3 %collective-permute-done.6.answer_ref = f32[256,128]{1,0:T(8,128)S(1)} collective-permute-done((f32[256,128]{1,0:T(8,128)S(1)}, f32[256,128]{1,0:T(8,128)S(1)}, u32[]{:S(2)}, u32[]{:S(2)}) %collective-permute-start.6) | collective-permute-done | bytes 131104 | tf_op jit(solution)/shard_map/ppermute | solution.py:27
  89.2 1.6 %lay_below.1 = (bf16[256,1536]{1,0:T(8,128)(2,1)S(1)}, f32[256,128]{1,0:T(8,128)S(1)}) custom-call(s32[1,4,3,12]{3,2,1,0:T(4,128)S(1)} %copy-done.2, s32[1,4]{1,0:T(1,128)S(1)} %copy-done.3, s32[38]{0:T(128)S(1)} %fusion.2.two_mask_ref, s32[38]{0:T(128)S(1)} %fusion.one_mask_ref, bf16[2448,128]{1,0:T(8,128)(2,1)} %collective-permute-done.two_ref, ...), custom_call_target="tpu_custom_call" | custom-call | bytes 1024 | tf_op jit(solution)/shard_map/lay_below/pallas_call | solution.py:224
  90.8 0.0 collective-permute-done.7
  90.8 1.0 %last_product.1 = bf16[256,128]{1,0:T(8,128)(2,1)} custom-call(bf16[256,1536]{1,0:T(8,128)(2,1)S(1)} %get-tuple-element.12.left_ref, bf16[1536,128]{1,0:T(8,128)(2,1)S(1)} %bitcast.15, f32[256,128]{1,0:T(8,128)S(1)} %get-tuple-element.14.known_ref), custom_call_target="tpu_custom_call" | custom-call | bytes 1024 | tf_op jit(solution)/shard_map/last_product/pallas_call | solution.py:245
  (4 shorter events, 0.0 us)
Async XLA Ops:
  4.5 26.4 %copy-start = (bf16[24,128,128]{2,1,0:T(8,128)(2,1)S(1)}, bf16[24,128,128]{2,1,0:T(8,128)(2,1)}, u32[]{:S(2)}) copy-start(bf16[24,128,128]{2,1,0:T(8,128)(2,1)} %right_ref.5) | copy-start | bytes 2359300
  4.5 26.4 %copy-start.1 = (bf16[2448,128]{1,0:T(8,128)(2,1)S(1)}, bf16[2448,128]{1,0:T(8,128)(2,1)}, u32[]{:S(2)}) copy-start(bf16[2448,128]{1,0:T(8,128)(2,1)} %get-tuple-element.10.panel_ref) | copy-start | bytes 1880068
  4.5 26.4 %copy-start.2 = (s32[1,4,3,12]{3,2,1,0:T(4,128)S(1)}, s32[1,4,3,12]{3,2,1,0:T(4,128)}, u32[]{:S(2)}) copy-start(s32[1,4,3,12]{3,2,1,0:T(4,128)} %copy.13.lists_ref) | copy-start | bytes 1732
  4.5 26.4 %copy-start.3 = (s32[1,4]{1,0:T(1,128)S(1)}, s32[1,4]{1,0:T(1,128)}, u32[]{:S(2)}) copy-start(s32[1,4]{1,0:T(1,128)} %counts_ref.7) | copy-start | bytes 52
  4.5 26.4 %copy-start.4 = (s32[38]{0:T(128)S(1)}, s32[38]{0:T(128)}, u32[]{:S(2)}) copy-start(s32[38]{0:T(128)} %mask_ref.7) | copy-start | bytes 460
  5.3 20.1 %collective-permute-start.2 = (bf16[16,128]{1,0:T(8,128)(2,1)S(1)}, bf16[16,128]{1,0:T(8,128)(2,1)S(1)}, u32[]{:S(2)}, u32[]{:S(2)}) collective-permute-start(bf16[16,128]{1,0:T(8,128)(2,1)S(1)} %slice.31), channel_id=1, source_target_pairs={{0,1}} | collective-permute-start | bytes 12296 | tf_op jit(solution)/shard_map/ppermute | solution.py:27
  6.0 49.7 %collective-permute-start = (bf16[2448,128]{1,0:T(8,128)(2,1)}, bf16[2448,128]{1,0:T(8,128)(2,1)}, u32[]{:S(2)}, u32[]{:S(2)}) collective-permute-start(bf16[2448,128]{1,0:T(8,128)(2,1)} %get-tuple-element.10.panel_ref), channel_id=1, source_target_pairs={{0,2},{1,3},{2,4},{3,5},{4,6},{5,7},{6,8},{7,9},{8,10},{9,11},{10,... | collective-permute-start | bytes 1880072 | tf_op jit(solution)/shard_map/ppermute | solution.py:27
  19.4 41.7 %collective-permute-start.5 = (bf16[784,128]{1,0:T(8,128)(2,1)}, bf16[784,128]{1,0:T(8,128)(2,1)S(1)}, u32[]{:S(2)}, u32[]{:S(2)}) collective-permute-start(bf16[784,128]{1,0:T(8,128)(2,1)} %get-tuple-element.11), channel_id=1, source_target_pairs={{63,0},{127,64},{191,128},{255,192},{319,256},{383,320},{447,384},... | collective-permute-start | bytes 602120 | tf_op jit(solution)/shard_map/ppermute | solution.py:27
  23.5 67.3 %collective-permute-start.7 = (bf16[12,128,128]{2,1,0:T(8,128)(2,1)}, bf16[12,128,128]{2,1,0:T(8,128)(2,1)S(1)}, u32[]{:S(2)}, u32[]{:S(2)}) collective-permute-start(bf16[12,128,128]{2,1,0:T(8,128)(2,1)} %get-tuple-element.13), channel_id=1, source_target_pairs={{0,64},{1,65},{2,66},{3,67},{4,68},{5,69},{6,70},{7,71},{8,72},{9,... | collective-permute-start | bytes 1179656 | tf_op jit(solution)/shard_map/ppermute | solution.py:27
  25.5 0.6 copy-start.5
  28.8 37.0 %collective-permute-start.4 = (bf16[2448,128]{1,0:T(8,128)(2,1)}, bf16[2448,128]{1,0:T(8,128)(2,1)}, u32[]{:S(2)}, u32[]{:S(2)}) collective-permute-start(bf16[2448,128]{1,0:T(8,128)(2,1)} %pack_again.1), channel_id=1, source_target_pairs={{1,0},{2,1},{3,2},{4,3},{5,4},{6,5},{7,6},{8,7},{9,8},{10,9},{11,1... | collective-permute-start | bytes 1880072 | tf_op jit(solution)/shard_map/ppermute | solution.py:27
  32.4 35.4 %collective-permute-start.3 = (bf16[2448,128]{1,0:T(8,128)(2,1)}, bf16[2448,128]{1,0:T(8,128)(2,1)S(1)}, u32[]{:S(2)}, u32[]{:S(2)}) collective-permute-start(bf16[2448,128]{1,0:T(8,128)(2,1)} %pack_again.1), channel_id=1, source_target_pairs={{0,1},{1,2},{2,3},{4,5},{5,6},{6,7},{8,9},{9,10},{10,11},{12,13},{... | collective-permute-start | bytes 1880072 | tf_op jit(solution)/shard_map/ppermute | solution.py:27
  55.7 12.2 %collective-permute-start.1 = (bf16[2448,128]{1,0:T(8,128)(2,1)}, bf16[2448,128]{1,0:T(8,128)(2,1)S(1)}, u32[]{:S(2)}, u32[]{:S(2)}) collective-permute-start(bf16[2448,128]{1,0:T(8,128)(2,1)} %collective-permute-done.two_ref), channel_id=1, source_target_pairs={{1,0},{5,4},{9,8},{13,12},{17,16},{21,20},{25,24},{29,28},{33,32},... | collective-permute-start | bytes 1880072 | tf_op jit(solution)/shard_map/ppermute | solution.py:27
  63.8 25.4 %collective-permute-start.6 = (f32[256,128]{1,0:T(8,128)S(1)}, f32[256,128]{1,0:T(8,128)S(1)}, u32[]{:S(2)}, u32[]{:S(2)}) collective-permute-start(f32[256,128]{1,0:T(8,128)S(1)} %answer.1), channel_id=1, source_target_pairs={{0,63},{64,127},{128,191},{192,255},{256,319},{320,383},{384,447},... | collective-permute-start | bytes 393224 | tf_op jit(solution)/shard_map/ppermute | solution.py:27

commit v8 on v7

--- a/solution.py
+++ b/solution.py
@@ -11,7 +11,6 @@
 BS = 128
 CAP_L = 19
 CAPM = 6
-PCAP = 12
 META = 16
 RING = 4
 CHEAP = pl.CostEstimate(flops=0, bytes_accessed=1024, transcendentals=0)
@@ -57,66 +56,43 @@
     pltpu.make_async_copy(blocks, blocks, sem).wait()
 
 
-def first_kernel(
-    mask_ref, lists_ref, counts_ref, left_ref, right_ref,
-    packed_ref, part_ref, ask_ref, sem, part_sem, ask_sem,
-):
+def cut_kernel(right_ref, after_ref, part_ref, sem):
+    del after_ref
     half = part_ref.shape[0]
-    part = pltpu.make_async_copy(right_ref.at[pl.ds(half, half)], part_ref, part_sem)
+    part = pltpu.make_async_copy(right_ref.at[pl.ds(half, half)], part_ref, sem)
     part.start()
-    pack_into(mask_ref, left_ref, packed_ref, sem)
-    copies = []
-    for m in range(CAPM):
-        target = ask_ref.at[pl.ds(m * BS, BS)]
-        copies.append(pltpu.make_async_copy(right_ref.at[CAPM + m], target, ask_sem.at[m]))
-        copies[-1].start()
-    lane = lax.broadcasted_iota(jnp.int32, (META, BS), 1)
-    pairs = lists_ref.shape[3]
-    row = jnp.where(lane == 3 * pairs, counts_ref[0, 3].astype(jnp.float32), 0.0)
-    for q in range(3 * pairs):
-        row = jnp.where(lane == q, lists_ref[0, 3, q // pairs, q % pairs].astype(jnp.float32), row)
-    ask_ref[pl.ds(CAPM * BS, META), :] = row.astype(ask_ref.dtype)
-    wait_packed(packed_ref, sem)
     part.wait()
-    for copy in copies:
-        copy.wait()
-
-
-def second_kernel(mask_ref, left_ref, after_ref, packed_ref, sem):
+
+
+def cut(right_blocks, after):
+    return pl.pallas_call(
+        cut_kernel,
+        out_shape=jax.ShapeDtypeStruct((2 * CAPM, BS, BS), jnp.bfloat16),
+        in_specs=[ANY, ANY],
+        out_specs=VMEM,
+        scratch_shapes=[pltpu.SemaphoreType.DMA],
+        compiler_params=WIDE,
+        cost_estimate=CHEAP,
+        name="cut_right",
+    )(right_blocks, after)
+
+
+def pack_kernel(mask_ref, left_ref, after_ref, packed_ref, sem):
     del after_ref
     pack_into(mask_ref, left_ref, packed_ref, sem)
     wait_packed(packed_ref, sem)
 
 
-def first_stage(left_mask, lists, counts, left_blocks, right_blocks):
-    return pl.pallas_call(
-        first_kernel,
-        out_shape=[
-            jax.ShapeDtypeStruct((CAP_L * BS + META, BS), jnp.bfloat16),
-            jax.ShapeDtypeStruct((2 * CAPM, BS, BS), jnp.bfloat16),
-            jax.ShapeDtypeStruct((CAPM * BS + META, BS), jnp.bfloat16),
-        ],
-        in_specs=[SMEM] * 3 + [ANY] * 2,
-        out_specs=[VMEM] * 3,
-        scratch_shapes=[
-            pltpu.SemaphoreType.DMA, pltpu.SemaphoreType.DMA, pltpu.SemaphoreType.DMA((CAPM,))
-        ],
-        compiler_params=WIDE,
-        cost_estimate=CHEAP,
-        name="pack_and_cut",
-    )(left_mask, lists, counts, left_blocks, right_blocks)
-
-
-def second_stage(left_mask, left_blocks, after):
-    return pl.pallas_call(
-        second_kernel,
+def pack(left_mask, left_blocks, after, name):
+    return pl.pallas_call(
+        pack_kernel,
         out_shape=jax.ShapeDtypeStruct((CAP_L * BS + META, BS), jnp.bfloat16),
         in_specs=[SMEM, ANY, ANY],
         out_specs=VMEM,
         scratch_shapes=[pltpu.SemaphoreType.DMA],
         compiler_params=WIDE,
         cost_estimate=CHEAP,
-        name="pack_again",
+        name=name,
     )(left_mask, left_blocks, after)
 
 
@@ -205,43 +181,69 @@
 
 
 def late_kernel(
-    lists_ref, counts_ref, two_mask_ref, one_mask_ref, two_ref, one_ref, handed_ref,
-    early_ref, answer_ref, laid_ref, known_ref, rank_ref, sem,
+    lists_ref, counts_ref, one_mask_ref, two_mask_ref,
+    two_ref, wrapped_ref, one_ref, handed_ref, laid_ref, rank_ref, sem,
 ):
     laid_ref[...] = jnp.zeros_like(laid_ref)
-    two = ((two_ref, lambda c: c >= 0),)
+    two = ((two_ref, lambda c: c >= 2), (wrapped_ref, lambda c: c < 2))
     one = (
         (one_ref, lambda c: lax.rem(c, RING) != 0),
         (handed_ref, lambda c: lax.rem(c, RING) == 0),
     )
     total = place(0, 0, lists_ref, counts_ref, two_mask_ref, two, laid_ref, rank_ref, sem)
     total += place(1, 1, lists_ref, counts_ref, one_mask_ref, one, laid_ref, rank_ref, sem)
-    known_ref[...] = early_ref[...] + answer_ref[...]
     drain(total, two_ref, laid_ref, sem)
 
 
-def late(lists, counts, masks, panels, known, answer):
+def late(lists, counts, masks, panels):
     return pl.pallas_call(
         late_kernel,
-        out_shape=[
-            jax.ShapeDtypeStruct((BR * BS, 2 * CAPM * BS), jnp.bfloat16),
-            jax.ShapeDtypeStruct((BR * BS, BS), jnp.float32),
-        ],
-        in_specs=[SMEM] * 4 + [ANY] * 3 + [VMEM] * 2,
-        out_specs=[VMEM, VMEM],
+        out_shape=jax.ShapeDtypeStruct((BR * BS, 2 * CAPM * BS), jnp.bfloat16),
+        in_specs=[SMEM] * 4 + [ANY] * 4,
+        out_specs=VMEM,
         scratch_shapes=[pltpu.SMEM((masks[0].shape[0],), jnp.int32), pltpu.SemaphoreType.DMA],
         compiler_params=ROOM,
         cost_estimate=CHEAP,
         name="lay_below",
-    )(lists, counts, *masks, *panels, known, answer)
-
-
-def last_kernel(left_ref, right_ref, known_ref, out_ref):
+    )(lists, counts, *masks, *panels)
+
+
+def pass_kernel(two_ref, wrapped_ref, after_ref, passed_ref, sem):
+    del after_ref
+    column = lax.axis_index("pcol")
+
+    @pl.when(column == 1)
+    def _():
+        copy = pltpu.make_async_copy(wrapped_ref, passed_ref, sem)
+        copy.start()
+        copy.wait()
+
+    @pl.when(jnp.logical_and(column != 1, lax.rem(column, RING) == 1))
+    def _():
+        copy = pltpu.make_async_copy(two_ref, passed_ref, sem)
+        copy.start()
+        copy.wait()
+
+
+def pass_on(two_below, wrapped, after):
+    return pl.pallas_call(
+        pass_kernel,
+        out_shape=jax.ShapeDtypeStruct(two_below.shape, two_below.dtype),
+        in_specs=[ANY] * 3,
+        out_specs=VMEM,
+        scratch_shapes=[pltpu.SemaphoreType.DMA],
+        compiler_params=ROOM,
+        cost_estimate=CHEAP,
+        name="pass_on",
+    )(two_below, wrapped, after)
+
+
+def last_kernel(known_ref, left_ref, right_ref, out_ref):
     new = jnp.dot(left_ref[...], right_ref[...], preferred_element_type=jnp.float32)
     out_ref[...] = (known_ref[...] + new).astype(out_ref.dtype)
 
 
-def last_product(left, right, known):
+def last_product(known, left, right):
     return pl.pallas_call(
         last_kernel,
         out_shape=jax.ShapeDtypeStruct(known.shape, jnp.bfloat16),
@@ -250,7 +252,7 @@
         compiler_params=ROOM,
         cost_estimate=CHEAP,
         name="last_product",
-    )(left, right, known)
+    )(known, left, right)
 
 
 def on_device(n_row, n_col, left_blocks, left_mask, right_blocks, pair_lists, pair_counts):
@@ -269,40 +271,35 @@
     def always(c):
         return c >= 0
 
-    packed, sent_right, ask = first_stage(
-        left_mask, pair_lists, pair_counts, left_blocks, right_blocks
-    )
-    two_below = by_pairs(packed, shift(0, 2, always))
-    right_before = by_pairs(sent_right, shift(1, 0, always))
-    mark = by_pairs(packed[:META], [(0, 1)])
-    again = second_stage(left_mask, left_blocks, mark)
-    one_above = by_pairs(again, shift(0, -1, lambda c: c > 0))
+    column = lax.axis_index("pcol")
+    mark = by_pairs(left_mask, [(0, 1)])
+    mark_again = by_pairs(mark, [(1, 0)])
+    packed = pack(left_mask, left_blocks, left_mask, "pack_panel")
+    wrapped = by_pairs(packed, shift(0, 2, lambda c: c >= last - 1))
+    right_before = by_pairs(cut(right_blocks, mark), shift(1, 0, always))
+    again = pack(left_mask, left_blocks, mark_again, "pack_again")
+    two_below = by_pairs(again, shift(0, 2, lambda c: c < last - 1))
+    one_above = by_pairs(again, shift(0, -1, always))
     one_below = by_pairs(again, shift(0, 1, lambda c: c % RING < RING - 1))
-    asked = by_pairs(ask, shift(0, 1, lambda c: c == last))
-    handed = by_pairs(two_below, shift(0, -1, lambda c: c % RING == 1))
-
-    listed = asked[CAPM * BS, : 3 * PCAP + 1].astype(jnp.int32)
-    answer = one_step(
-        0, 0, always, listed[: 3 * PCAP].reshape(1, 1, 3, PCAP), listed[3 * PCAP :].reshape(1, 1),
-        left_mask, packed, asked[: CAPM * BS].reshape(CAPM, BS, BS), None, CHEAP, "answer",
-    )
-    answer = by_pairs(answer, shift(0, -1, lambda c: c == 0))
-
     known = one_step(
-        2, 0, always, pair_lists, pair_counts, left_mask, packed, right_blocks, None,
+        2, 0, always, pair_lists, pair_counts, left_mask, again, right_blocks, None,
         DEAR, "own_step",
     )
+    passed = pass_on(two_below, wrapped, known)
+    handed = by_pairs(passed, shift(0, -1, lambda c: c % RING == 1))
     known = one_step(
-        3, CAPM, lambda c: c < last, pair_lists, pair_counts, mask_of(one_above, panel),
-        one_above, right_blocks, known, CHEAP, "step_above",
-    )
-    first = lax.axis_index("pcol") % RING == 0
-    mask_one = jnp.where(first, mask_of(handed, panel), mask_of(one_below, panel))
-    laid, known = late(
-        pair_lists, pair_counts, [mask_of(two_below, panel), mask_one],
-        [two_below, one_below, handed], known, answer,
-    )
-    return last_product(laid, right_before.reshape(half * BS, BS), known)
+        3, CAPM, always, pair_lists, pair_counts, mask_of(one_above, panel),
+        one_above, right_blocks, known, DEAR, "step_above",
+    )
+    mask_two = jnp.where(column < 2, mask_of(wrapped, panel), mask_of(two_below, panel))
+    mask_one = jnp.where(
+        column % RING != 0, mask_of(one_below, panel), mask_of(handed, panel)
+    )
+    laid = late(
+        pair_lists, pair_counts, [mask_one, mask_two],
+        [two_below, wrapped, one_below, handed],
+    )
+    return last_product(known, laid, right_before.reshape(half * BS, BS))
 
 
 def solution(mesh):

time: 92.5 us -> 100 us (1.081)
  the two profiles are of different devices: /device:TPU:1022 before, /device:TPU:33 now
where the time goes in v8:
time: 100 us; the launch traced here: 99.8 us
  waiting for transfers between devices  43.8 us (44%)
  starting transfers between devices  41.5 us (42%)
  Pallas kernels  12.6 us (13%)
  local copies, waits for them, and re-layouts  1.61 us (2%)
    ppermute x8, waiting for transfers between devices, by_pairs(): return lax.ppermute(array, ('prow', 'pcol'), pairs)  43.8 us
    ppermute x8, starting transfers between devices, by_pairs(): return lax.ppermute(array, ('prow', 'pcol'), pairs)  41.5 us
    pallas_call x2, Pallas kernels, pack(): pl.pallas_call(pack_kernel, out_shape=jax.ShapeDtypeStruct((CAP_L * BS +...  5.47 us
    pallas_call x2, Pallas kernels, one_step(): pl.pallas_call(functools.partial(one_kernel, u, first, here), out_shape=j...  2.98 us
  transfers between devices with their start and end apart: 8, of which 2 were waited for; matrix products, arithmetic and copies ran while one was open for 0% of the time, Pallas kernels for 12%

profile of v8, /device:TPU:33, one launch (start us, length us, event | category | flops | bytes accessed | tf_op | source)
XLA Modules:
  0.0 99.8 jit_solution(16940959125933608312)
XLA Ops:
  0.0 0.0 copy-start.4
  0.0 0.8 collective-permute-start
  0.8 2.7 %pack_panel.1 = bf16[2448,128]{1,0:T(8,128)(2,1)} custom-call(s32[38]{0:T(128)} %after_ref.1, bf16[38,128,128]{2,1,0:T(8,128)(2,1)} %left_ref.3, s32[38]{0:T(128)} %after_ref.1), custom_call_target="tpu_custom_call" | custom-call | bytes 1024 | tf_op jit(solution)/shard_map/pack_panel/pallas_call | solution.py:87
  3.5 0.7 collective-permute-start.5
  4.2 0.0 copy-done.4
  4.3 0.0 copy-start
  4.3 0.0 copy-start.2
  4.3 0.0 copy-start.3
  4.3 0.0 collective-permute-done.after_ref
  4.3 0.0 copy-start.5
  4.3 0.8 collective-permute-start.1
  5.1 0.0 copy-done.5
  5.2 1.7 %cut_right.1 = bf16[12,128,128]{2,1,0:T(8,128)(2,1)} custom-call(bf16[24,128,128]{2,1,0:T(8,128)(2,1)} %right_ref.5, s32[38]{0:T(128)} %copy-done.5), custom_call_target="tpu_custom_call" | custom-call | bytes 1024 | tf_op jit(solution)/shard_map/cut_right/pallas_call | solution.py:68
  6.9 28.2 %collective-permute-start.7 = (bf16[12,128,128]{2,1,0:T(8,128)(2,1)}, bf16[12,128,128]{2,1,0:T(8,128)(2,1)S(1)}, u32[]{:S(2)}, u32[]{:S(2)}) collective-permute-start(bf16[12,128,128]{2,1,0:T(8,128)(2,1)} %cut_right.1), channel_id=1, source_target_pairs={{0,64},{1,65},{2,66},{3,67},{4,68},{5,69},{6,70},{7,71},{8,72},{9,... | collective-permute-start | bytes 1179656 | tf_op jit(solution)/shard_map/ppermute | solution.py:26
  35.1 0.0 collective-permute-done.1.after_ref
  35.2 0.0 copy-start.6
  35.2 0.5 copy-done.6
  35.7 2.7 %pack_again.1.panel_ref = bf16[2448,128]{1,0:T(8,128)(2,1)} custom-call(s32[38]{0:T(128)} %after_ref.1, bf16[38,128,128]{2,1,0:T(8,128)(2,1)} %left_ref.3, s32[38]{0:T(128)} %copy-done.6), custom_call_target="tpu_custom_call" | custom-call | bytes 1024 | tf_op jit(solution)/shard_map/pack_again/pallas_call | solution.py:87
  38.4 5.0 %collective-permute-start.2 = (bf16[2448,128]{1,0:T(8,128)(2,1)}, bf16[2448,128]{1,0:T(8,128)(2,1)S(1)}, u32[]{:S(2)}, u32[]{:S(2)}) collective-permute-start(bf16[2448,128]{1,0:T(8,128)(2,1)} %pack_again.1.panel_ref), channel_id=1, source_target_pairs={{0,63},{1,0},{2,1},{3,2},{4,3},{5,4},{6,5},{7,6},{8,7},{9,8},{10,9... | collective-permute-start | bytes 1880072 | tf_op jit(solution)/shard_map/ppermute | solution.py:26
  43.4 2.0 %collective-permute-start.4 = (bf16[2448,128]{1,0:T(8,128)(2,1)}, bf16[2448,128]{1,0:T(8,128)(2,1)S(1)}, u32[]{:S(2)}, u32[]{:S(2)}) collective-permute-start(bf16[2448,128]{1,0:T(8,128)(2,1)} %pack_again.1.panel_ref), channel_id=1, source_target_pairs={{0,2},{1,3},{2,4},{3,5},{4,6},{5,7},{6,8},{7,9},{8,10},{9,11},{10,... | collective-permute-start | bytes 1880072 | tf_op jit(solution)/shard_map/ppermute | solution.py:26
  45.5 2.7 %collective-permute-start.3 = (bf16[2448,128]{1,0:T(8,128)(2,1)}, bf16[2448,128]{1,0:T(8,128)(2,1)S(1)}, u32[]{:S(2)}, u32[]{:S(2)}) collective-permute-start(bf16[2448,128]{1,0:T(8,128)(2,1)} %pack_again.1.panel_ref), channel_id=1, source_target_pairs={{0,1},{1,2},{2,3},{4,5},{5,6},{6,7},{8,9},{9,10},{10,11},{12,13},{... | collective-permute-start | bytes 1880072 | tf_op jit(solution)/shard_map/ppermute | solution.py:26
  48.2 0.0 copy-done
  48.2 0.0 copy-done.2
  48.2 0.0 copy-done.3
  48.2 0.0 copy-start.1
  48.2 1.1 %copy-done.1 = bf16[2448,128]{1,0:T(8,128)(2,1)S(1)} copy-done((bf16[2448,128]{1,0:T(8,128)(2,1)S(1)}, bf16[2448,128]{1,0:T(8,128)(2,1)}, u32[]{:S(2)}) %copy-start.1) | copy-done | bytes 626712
  49.3 1.5 %own_step.1.refs_0_.after_ref = f32[256,128]{1,0:T(8,128)S(1)} custom-call(s32[1,4,3,12]{3,2,1,0:T(4,128)S(1)} %copy.7.lists_ref, s32[1,4]{1,0:T(1,128)S(1)} %copy-done.3, s32[38]{0:T(128)S(1)} %copy-done.2, bf16[2448,128]{1,0:T(8,128)(2,1)S(1)} %copy-done.1, bf16[24,128,128]{2,1,0:T(8,128)(2,1)S(1)} %copy-done), custom_call_target="tpu_custom_call" | custom-call | flops 34359738368 | bytes 1048576 | tf_op jit(solution)/shard_map/own_step/pallas_call | solution.py:165
  50.8 0.0 collective-permute-done.5.wrapped_ref
  50.8 32.2 %collective-permute-done.4.two_ref = bf16[2448,128]{1,0:T(8,128)(2,1)S(1)} collective-permute-done((bf16[2448,128]{1,0:T(8,128)(2,1)}, bf16[2448,128]{1,0:T(8,128)(2,1)S(1)}, u32[]{:S(2)}, u32[]{:S(2)}) %collective-permute-start.4) | collective-permute-done | bytes 626720 | tf_op jit(solution)/shard_map/ppermute | solution.py:26
  83.0 1.3 %collective-permute-start.6 = (bf16[2448,128]{1,0:T(8,128)(2,1)S(1)}, bf16[2448,128]{1,0:T(8,128)(2,1)S(1)}, u32[]{:S(2)}, u32[]{:S(2)}) collective-permute-start(bf16[2448,128]{1,0:T(8,128)(2,1)S(1)} %pass_on.1), channel_id=1, source_target_pairs={{1,0},{5,4},{9,8},{13,12},{17,16},{21,20},{25,24},{29,28},{33,32},... | collective-permute-start | bytes 1880072 | tf_op jit(solution)/shard_map/ppermute | solution.py:26
  84.3 0.0 collective-permute-done.2.panel_ref
  84.3 1.5 %step_above.1.known_ref = f32[256,128]{1,0:T(8,128)S(1)} custom-call(s32[1,4,3,12]{3,2,1,0:T(4,128)S(1)} %copy.7.lists_ref, s32[1,4]{1,0:T(1,128)S(1)} %copy-done.3, s32[38]{0:T(128)S(1)} %fusion.2.mask_ref, bf16[2448,128]{1,0:T(8,128)(2,1)S(1)} %collective-permute-done.2.panel_ref, bf16[24,128,128]{2,1,0:T(8,128)(2,1)S(1)} %copy-done, ...), custom_call_target="tpu_custom_call" | custom-call | flops 34359738368 | bytes 1048576 | tf_op jit(solution)/shard_map/step_above/pallas_call | solution.py:165
  85.8 0.0 collective-permute-done.3.one_ref
  85.8 11.6 %collective-permute-done.6.handed_ref = bf16[2448,128]{1,0:T(8,128)(2,1)S(1)} collective-permute-done((bf16[2448,128]{1,0:T(8,128)(2,1)S(1)}, bf16[2448,128]{1,0:T(8,128)(2,1)S(1)}, u32[]{:S(2)}, u32[]{:S(2)}) %collective-permute-start.6) | collective-permute-done | bytes 626720 | tf_op jit(solution)/shard_map/ppermute | solution.py:26
  97.4 1.4 %lay_below.1.left_ref = bf16[256,1536]{1,0:T(8,128)(2,1)S(1)} custom-call(s32[1,4,3,12]{3,2,1,0:T(4,128)S(1)} %copy.7.lists_ref, s32[1,4]{1,0:T(1,128)S(1)} %copy-done.3, s32[38]{0:T(128)S(1)} %fusion.one_mask_ref, s32[38]{0:T(128)S(1)} %fusion.1.two_mask_ref, bf16[2448,128]{1,0:T(8,128)(2,1)S(1)} %collective-permute-done.4.two_ref, ...), custom_call_target="tpu_custom_call" | custom-call | bytes 1024 | tf_op jit(solution)/shard_map/lay_below/pallas_call | solution.py:199
  98.8 0.0 collective-permute-done.7
  98.8 1.0 last_product.1
  (5 shorter events, 0.0 us)
Async XLA Ops:
  0.0 4.2 %copy-start.4 = (s32[1,4,3,12]{3,1,2,0:T(4,128)S(1)}, s32[1,4,3,12]{3,1,2,0:T(4,128)}, u32[]{:S(2)}) copy-start(s32[1,4,3,12]{3,1,2,0:T(4,128)} %param.8) | copy-start | bytes 1732
  0.0 4.3 %collective-permute-start = (s32[38]{0:T(128)}, s32[38]{0:T(128)S(1)}, u32[]{:S(2)}, u32[]{:S(2)}) collective-permute-start(s32[38]{0:T(128)} %after_ref.1), channel_id=1, source_target_pairs={{0,1}} | collective-permute-start | bytes 464 | tf_op jit(solution)/shard_map/ppermute | solution.py:26
  3.5 47.2 %collective-permute-start.5 = (bf16[2448,128]{1,0:T(8,128)(2,1)}, bf16[2448,128]{1,0:T(8,128)(2,1)S(1)}, u32[]{:S(2)}, u32[]{:S(2)}) collective-permute-start(bf16[2448,128]{1,0:T(8,128)(2,1)} %pack_panel.1), channel_id=1, source_target_pairs={{62,0},{63,1},{126,64},{127,65},{190,128},{191,129},{254,192},{255... | collective-permute-start | bytes 1880072 | tf_op jit(solution)/shard_map/ppermute | solution.py:26
  4.3 43.9 %copy-start = (bf16[24,128,128]{2,1,0:T(8,128)(2,1)S(1)}, bf16[24,128,128]{2,1,0:T(8,128)(2,1)}, u32[]{:S(2)}) copy-start(bf16[24,128,128]{2,1,0:T(8,128)(2,1)} %right_ref.5) | copy-start | bytes 2359300
  4.3 43.9 %copy-start.2 = (s32[38]{0:T(128)S(1)}, s32[38]{0:T(128)}, u32[]{:S(2)}) copy-start(s32[38]{0:T(128)} %after_ref.1) | copy-start | bytes 460
  4.3 43.9 %copy-start.3 = (s32[1,4]{1,0:T(1,128)S(1)}, s32[1,4]{1,0:T(1,128)}, u32[]{:S(2)}) copy-start(s32[1,4]{1,0:T(1,128)} %counts_ref.5) | copy-start | bytes 52
  4.3 0.8 copy-start.5
  4.3 30.8 %collective-permute-start.1 = (s32[38]{0:T(128)S(1)}, s32[38]{0:T(128)S(1)}, u32[]{:S(2)}, u32[]{:S(2)}) collective-permute-start(s32[38]{0:T(128)S(1)} %collective-permute-done.after_ref), channel_id=1, source_target_pairs={{1,0}} | collective-permute-start | bytes 464 | tf_op jit(solution)/shard_map/ppermute | solution.py:26
  6.9 91.9 %collective-permute-start.7 = (bf16[12,128,128]{2,1,0:T(8,128)(2,1)}, bf16[12,128,128]{2,1,0:T(8,128)(2,1)S(1)}, u32[]{:S(2)}, u32[]{:S(2)}) collective-permute-start(bf16[12,128,128]{2,1,0:T(8,128)(2,1)} %cut_right.1), channel_id=1, source_target_pairs={{0,64},{1,65},{2,66},{3,67},{4,68},{5,69},{6,70},{7,71},{8,72},{9,... | collective-permute-start | bytes 1179656 | tf_op jit(solution)/shard_map/ppermute | solution.py:26
  35.2 0.5 copy-start.6
  38.4 45.9 %collective-permute-start.2 = (bf16[2448,128]{1,0:T(8,128)(2,1)}, bf16[2448,128]{1,0:T(8,128)(2,1)S(1)}, u32[]{:S(2)}, u32[]{:S(2)}) collective-permute-start(bf16[2448,128]{1,0:T(8,128)(2,1)} %pack_again.1.panel_ref), channel_id=1, source_target_pairs={{0,63},{1,0},{2,1},{3,2},{4,3},{5,4},{6,5},{7,6},{8,7},{9,8},{10,9... | collective-permute-start | bytes 1880072 | tf_op jit(solution)/shard_map/ppermute | solution.py:26
  43.4 39.5 %collective-permute-start.4 = (bf16[2448,128]{1,0:T(8,128)(2,1)}, bf16[2448,128]{1,0:T(8,128)(2,1)S(1)}, u32[]{:S(2)}, u32[]{:S(2)}) collective-permute-start(bf16[2448,128]{1,0:T(8,128)(2,1)} %pack_again.1.panel_ref), channel_id=1, source_target_pairs={{0,2},{1,3},{2,4},{3,5},{4,6},{5,7},{6,8},{7,9},{8,10},{9,11},{10,... | collective-permute-start | bytes 1880072 | tf_op jit(solution)/shard_map/ppermute | solution.py:26
  45.5 40.4 %collective-permute-start.3 = (bf16[2448,128]{1,0:T(8,128)(2,1)}, bf16[2448,128]{1,0:T(8,128)(2,1)S(1)}, u32[]{:S(2)}, u32[]{:S(2)}) collective-permute-start(bf16[2448,128]{1,0:T(8,128)(2,1)} %pack_again.1.panel_ref), channel_id=1, source_target_pairs={{0,1},{1,2},{2,3},{4,5},{5,6},{6,7},{8,9},{9,10},{10,11},{12,13},{... | collective-permute-start | bytes 1880072 | tf_op jit(solution)/shard_map/ppermute | solution.py:26
  48.2 1.1 %copy-start.1 = (bf16[2448,128]{1,0:T(8,128)(2,1)S(1)}, bf16[2448,128]{1,0:T(8,128)(2,1)}, u32[]{:S(2)}) copy-start(bf16[2448,128]{1,0:T(8,128)(2,1)} %pack_again.1.panel_ref) | copy-start | bytes 1880068
  83.0 14.4 %collective-permute-start.6 = (bf16[2448,128]{1,0:T(8,128)(2,1)S(1)}, bf16[2448,128]{1,0:T(8,128)(2,1)S(1)}, u32[]{:S(2)}, u32[]{:S(2)}) collective-permute-start(bf16[2448,128]{1,0:T(8,128)(2,1)S(1)} %pass_on.1), channel_id=1, source_target_pairs={{1,0},{5,4},{9,8},{13,12},{17,16},{21,20},{25,24},{29,28},{33,32},... | collective-permute-start | bytes 1880072 | tf_op jit(solution)/shard_map/ppermute | solution.py:26

commit v9 on v4

--- a/solution.py
+++ b/solution.py
@@ -67,7 +67,7 @@
         in_specs=[SMEM, ANY, ANY],
         out_specs=[VMEM, VMEM],
         scratch_shapes=[pltpu.SemaphoreType.DMA, pltpu.SemaphoreType.DMA],
-        compiler_params=ROOM,
+        compiler_params=pltpu.CompilerParams(vmem_limit_bytes=62 << 20),
         cost_estimate=CHEAP,
         name="pack_and_cut",
     )(left_mask, left_blocks, right_blocks)
@@ -119,48 +119,47 @@
         )
 
 
-def early_kernel(
-    last, lists_ref, counts_ref, own_mask_ref, mask_ref, own_ref, above_ref, right_ref,
-    known_ref, left_ref, held_ref, rank_ref, sem, right_sem,
+def one_kernel(
+    u, here, lists_ref, counts_ref, mask_ref, panel_ref, right_ref, *refs,
 ):
+    before_ref = refs[0] if len(refs) == 7 else None
+    known_ref, left_ref, held_ref, rank_ref, sem, right_sem = refs[-6:]
     fetch_right = pltpu.make_async_copy(
-        right_ref.at[pl.ds(0, held_ref.shape[0])], held_ref, right_sem
+        right_ref.at[pl.ds((u - 2) * CAPM, CAPM)], held_ref, right_sem
     )
     fetch_right.start()
     left_ref[...] = jnp.zeros_like(left_ref)
-    own = ((own_ref, lambda c: c >= 0),)
-    above = ((above_ref, lambda c: c < last),)
-    total = place(2, 0, lists_ref, counts_ref, own_mask_ref, own, left_ref, rank_ref, sem)
-    total += place(3, 1, lists_ref, counts_ref, mask_ref, above, left_ref, rank_ref, sem)
-    drain(total, own_ref, left_ref, sem)
+    source = ((panel_ref, here),)
+    total = place(u, 0, lists_ref, counts_ref, mask_ref, source, left_ref, rank_ref, sem)
+    drain(total, panel_ref, left_ref, sem)
     fetch_right.wait()
-    known_ref[...] = jnp.zeros_like(known_ref)
+    known_ref[...] = jnp.zeros_like(known_ref) if before_ref is None else before_ref[...]
     multiply(left_ref, held_ref, known_ref)
 
 
-def early(last, lists, counts, masks, panels, right):
-    half = 2 * CAPM
-    return pl.pallas_call(
-        functools.partial(early_kernel, last),
+def one_step(u, here, lists, counts, mask, panel, right, before, cost, name):
+    more = [] if before is None else [before]
+    return pl.pallas_call(
+        functools.partial(one_kernel, u, here),
         out_shape=jax.ShapeDtypeStruct((BR * BS, BS), jnp.float32),
-        in_specs=[SMEM] * 4 + [ANY] * 3,
+        in_specs=[SMEM] * 3 + [ANY] * 2 + [VMEM] * len(more),
         out_specs=VMEM,
         scratch_shapes=[
-            pltpu.VMEM((BR * BS, half * BS), jnp.bfloat16),
-            pltpu.VMEM((half, BS, BS), jnp.bfloat16),
-            pltpu.SMEM((masks[0].shape[0],), jnp.int32),
+            pltpu.VMEM((BR * BS, CAPM * BS), jnp.bfloat16),
+            pltpu.VMEM((CAPM, BS, BS), jnp.bfloat16),
+            pltpu.SMEM((mask.shape[0],), jnp.int32),
             pltpu.SemaphoreType.DMA,
             pltpu.SemaphoreType.DMA,
         ],
         compiler_params=ROOM,
-        cost_estimate=DEAR,
-        name="own_and_above",
-    )(lists, counts, *masks, *panels, right)
+        cost_estimate=cost,
+        name=name,
+    )(lists, counts, mask, panel, right, *more)
 
 
 def late_kernel(
-    last, lists_ref, counts_ref, two_mask_ref, one_mask_ref, handed_mask_ref,
-    two_ref, one_ref, handed_ref, right_ref, early_ref,
+    last, lists_ref, counts_ref, two_mask_ref, one_mask_ref, around_mask_ref,
+    two_ref, one_ref, handed_ref, around_ref, right_ref, early_ref,
     laid_ref, known_ref, left_ref, held_ref, rank_ref, sem, right_sem,
 ):
     laid_ref[...] = jnp.zeros_like(laid_ref)
@@ -181,11 +180,11 @@
         )
         fetch_right.start()
         left_ref[...] = jnp.zeros_like(left_ref)
-        above = ((handed_ref, lambda c: c >= 0),)
+        above = ((around_ref, lambda c: c >= 0),)
         count = place(
-            3, 0, lists_ref, counts_ref, handed_mask_ref, above, left_ref, rank_ref, sem
+            3, 0, lists_ref, counts_ref, around_mask_ref, above, left_ref, rank_ref, sem
         )
-        drain(count, handed_ref, left_ref, sem)
+        drain(count, around_ref, left_ref, sem)
         fetch_right.wait()
         multiply(left_ref, held_ref, known_ref)
 
@@ -197,7 +196,7 @@
             jax.ShapeDtypeStruct((BR * BS, 2 * CAPM * BS), jnp.bfloat16),
             jax.ShapeDtypeStruct((BR * BS, BS), jnp.float32),
         ],
-        in_specs=[SMEM] * 5 + [ANY] * 4 + [VMEM],
+        in_specs=[SMEM] * 5 + [ANY] * 5 + [VMEM],
         out_specs=[VMEM, VMEM],
         scratch_shapes=[
             pltpu.VMEM((BR * BS, CAPM * BS), jnp.bfloat16),
@@ -244,24 +243,28 @@
 
     packed, sent_right = stage(left_mask, left_blocks, right_blocks)
     two_below = by_pairs(packed, shift(0, 2, lambda c: True))
+    right_before = by_pairs(sent_right, shift(1, 0, lambda c: True))
     one_above = by_pairs(packed, shift(0, -1, lambda c: c > 0))
     one_below = by_pairs(packed, shift(0, 1, lambda c: c % RING < RING - 1))
-    right_before = by_pairs(sent_right, shift(1, 0, lambda c: True))
-    handed = by_pairs(
-        two_below,
-        shift(0, -1, lambda c: c % RING == 1) + shift(0, -3, lambda c: c == 2),
-    )
+    handed = by_pairs(two_below, shift(0, -1, lambda c: c % RING == 1))
+    halfway = by_pairs(one_below, shift(0, -4, lambda c: c == 1))
+    around = by_pairs(halfway, shift(0, 2, lambda c: c == last - 2))
 
     column = lax.axis_index("pcol")
-    mask_handed = mask_of(handed, panel)
-    known = early(
-        last, pair_lists, pair_counts, [left_mask, mask_of(one_above, panel)],
-        [packed, one_above], right_blocks,
-    )
-    mask_one = jnp.where(column % RING == 0, mask_handed, mask_of(one_below, panel))
+    known = one_step(
+        2, lambda c: c >= 0, pair_lists, pair_counts, left_mask, packed, right_blocks, None,
+        DEAR, "own_step",
+    )
+    known = one_step(
+        3, lambda c: c < last, pair_lists, pair_counts, mask_of(one_above, panel), one_above,
+        right_blocks, known, CHEAP, "step_above",
+    )
+    mask_one = jnp.where(
+        column % RING == 0, mask_of(handed, panel), mask_of(one_below, panel)
+    )
     laid, known = late(
-        last, pair_lists, pair_counts, [mask_of(two_below, panel), mask_one, mask_handed],
-        [two_below, one_below, handed], right_blocks, known,
+        last, pair_lists, pair_counts, [mask_of(two_below, panel), mask_one, mask_of(around, panel)],
+        [two_below, one_below, handed, around], right_blocks, known,
     )
     return last_product(laid, right_before.reshape(half * BS, BS), known)
 

time: 103 us -> 102 us (level)
  the two profiles are of different devices: /device:TPU:80 before, /device:TPU:509 now
where the time goes in v9:
time: 102 us
  waiting for transfers between devices  55.6 us (55%)
  starting transfers between devices  35.1 us (34%)
  Pallas kernels  9.16 us (9%)
  local copies, waits for them, and re-layouts  1.09 us (1%)
    ppermute x7, waiting for transfers between devices, by_pairs(): return lax.ppermute(array, ('prow', 'pcol'), pairs)  55.6 us
    ppermute x7, starting transfers between devices, by_pairs(): return lax.ppermute(array, ('prow', 'pcol'), pairs)  35.1 us
    pallas_call x1, Pallas kernels, stage(): pl.pallas_call(stage_kernel, out_shape=[jax.ShapeDtypeStruct((CAP_L * BS...  3.08 us
    pallas_call x2, Pallas kernels, one_step(): pl.pallas_call(functools.partial(one_kernel, u, here), out_shape=jax.Shap...  2.85 us
    pallas_call x1, Pallas kernels, late(): pl.pallas_call(functools.partial(late_kernel, last), out_shape=[jax.Shape...  2.23 us
  transfers between devices with their start and end apart: 7, of which 1 were waited for; matrix products, arithmetic and copies ran while one was open for 1% of the time, Pallas kernels for 5%

profile of v9, /device:TPU:509, one launch (start us, length us, event | category | flops | bytes accessed | tf_op | source)
XLA Modules:
  0.0 101.8 jit_solution(3923640268734897442)
XLA Ops:
  0.0 0.0 copy-start
  0.0 0.0 copy-start.2
  0.0 0.0 copy-start.4
  0.0 0.0 copy-start.1
  0.0 3.1 %pack_and_cut.1 = (bf16[2448,128]{1,0:T(8,128)(2,1)}, bf16[12,128,128]{2,1,0:T(8,128)(2,1)}) custom-call(s32[38]{0:T(128)} %mask_ref.3, bf16[38,128,128]{2,1,0:T(8,128)(2,1)} %left_ref.1, bf16[24,128,128]{2,1,0:T(8,128)(2,1)} %right_ref.7), custom_call_target="tpu_custom_call" | custom-call | bytes 1024 | tf_op jit(solution)/shard_map/pack_and_cut/pallas_call | solution.py:61
  3.1 1.3 %collective-permute-start.2 = (bf16[2448,128]{1,0:T(8,128)(2,1)}, bf16[2448,128]{1,0:T(8,128)(2,1)S(1)}, u32[]{:S(2)}, u32[]{:S(2)}) collective-permute-start(bf16[2448,128]{1,0:T(8,128)(2,1)} %get-tuple-element.9.panel_ref), channel_id=1, source_target_pairs={{0,1},{1,2},{2,3},{4,5},{5,6},{6,7},{8,9},{9,10},{10,11},{12,13},{... | collective-permute-start | bytes 1880072 | tf_op jit(solution)/shard_map/ppermute | solution.py:26
  4.4 1.9 %collective-permute-start = (bf16[2448,128]{1,0:T(8,128)(2,1)}, bf16[2448,128]{1,0:T(8,128)(2,1)S(1)}, u32[]{:S(2)}, u32[]{:S(2)}) collective-permute-start(bf16[2448,128]{1,0:T(8,128)(2,1)} %get-tuple-element.9.panel_ref), channel_id=1, source_target_pairs={{0,2},{1,3},{2,4},{3,5},{4,6},{5,7},{6,8},{7,9},{8,10},{9,11},{10,... | collective-permute-start | bytes 1880072 | tf_op jit(solution)/shard_map/ppermute | solution.py:26
  6.3 4.8 %collective-permute-start.5 = (bf16[2448,128]{1,0:T(8,128)(2,1)}, bf16[2448,128]{1,0:T(8,128)(2,1)}, u32[]{:S(2)}, u32[]{:S(2)}) collective-permute-start(bf16[2448,128]{1,0:T(8,128)(2,1)} %get-tuple-element.9.panel_ref), channel_id=1, source_target_pairs={{1,0},{2,1},{3,2},{4,3},{5,4},{6,5},{7,6},{8,7},{9,8},{10,9},{11,1... | collective-permute-start | bytes 1880072 | tf_op jit(solution)/shard_map/ppermute | solution.py:26
  11.2 23.6 %collective-permute-start.6 = (bf16[12,128,128]{2,1,0:T(8,128)(2,1)}, bf16[12,128,128]{2,1,0:T(8,128)(2,1)S(1)}, u32[]{:S(2)}, u32[]{:S(2)}) collective-permute-start(bf16[12,128,128]{2,1,0:T(8,128)(2,1)} %get-tuple-element.11), channel_id=1, source_target_pairs={{0,64},{1,65},{2,66},{3,67},{4,68},{5,69},{6,70},{7,71},{8,72},{9,... | collective-permute-start | bytes 1179656 | tf_op jit(solution)/shard_map/ppermute | solution.py:26
  34.7 0.0 copy-done.4
  34.8 0.0 collective-permute-done.2.one_ref
  34.8 1.5 %collective-permute-start.3 = (bf16[2448,128]{1,0:T(8,128)(2,1)S(1)}, bf16[2448,128]{1,0:T(8,128)(2,1)}, u32[]{:S(2)}, u32[]{:S(2)}) collective-permute-start(bf16[2448,128]{1,0:T(8,128)(2,1)S(1)} %collective-permute-done.2.one_ref), channel_id=1, source_target_pairs={{1,61},{65,125},{129,189},{193,253},{257,317},{321,381},{385,445},... | collective-permute-start | bytes 1880072 | tf_op jit(solution)/shard_map/ppermute | solution.py:26
  36.3 0.0 collective-permute-done.two_ref
  36.3 0.7 collective-permute-start.1
  37.0 0.0 copy-done
  37.0 0.0 copy-done.2
  37.0 0.0 copy-done.1
  37.0 0.0 copy-start.3
  37.0 1.1 %copy-done.3 = bf16[2448,128]{1,0:T(8,128)(2,1)S(1)} copy-done((bf16[2448,128]{1,0:T(8,128)(2,1)S(1)}, bf16[2448,128]{1,0:T(8,128)(2,1)}, u32[]{:S(2)}) %copy-start.3) | copy-done | bytes 626712
  38.1 1.5 %own_step.1.refs_0_ = f32[256,128]{1,0:T(8,128)S(1)} custom-call(s32[1,4,3,12]{3,2,1,0:T(4,128)S(1)} %copy.8.lists_ref, s32[1,4]{1,0:T(1,128)S(1)} %copy-done.1, s32[38]{0:T(128)S(1)} %copy-done.2, bf16[2448,128]{1,0:T(8,128)(2,1)S(1)} %copy-done.3, bf16[24,128,128]{2,1,0:T(8,128)(2,1)S(1)} %copy-done), custom_call_target="tpu_custom_call" | custom-call | flops 34359738368 | bytes 1048576 | tf_op jit(solution)/shard_map/own_step/pallas_call | solution.py:142
  39.6 0.0 collective-permute-done.3
  39.6 1.3 %collective-permute-start.4 = (bf16[2448,128]{1,0:T(8,128)(2,1)}, bf16[2448,128]{1,0:T(8,128)(2,1)S(1)}, u32[]{:S(2)}, u32[]{:S(2)}) collective-permute-start(bf16[2448,128]{1,0:T(8,128)(2,1)} %collective-permute-done.3), channel_id=1, source_target_pairs={{61,63},{125,127},{189,191},{253,255},{317,319},{381,383},{445,447... | collective-permute-start | bytes 1880072 | tf_op jit(solution)/shard_map/ppermute | solution.py:26
  40.9 0.0 collective-permute-done.5.panel_ref
  40.9 0.7 fusion.1.mask_ref
  41.6 1.4 %step_above.1.early_ref = f32[256,128]{1,0:T(8,128)S(1)} custom-call(s32[1,4,3,12]{3,2,1,0:T(4,128)S(1)} %copy.8.lists_ref, s32[1,4]{1,0:T(1,128)S(1)} %copy-done.1, s32[38]{0:T(128)S(1)} %fusion.1.mask_ref, bf16[2448,128]{1,0:T(8,128)(2,1)} %collective-permute-done.5.panel_ref, bf16[24,128,128]{2,1,0:T(8,128)(2,1)S(1)} %copy-done, ...), custom_call_target="tpu_custom_call" | custom-call | bytes 1024 | tf_op jit(solution)/shard_map/step_above/pallas_call | solution.py:142
  43.0 0.0 collective-permute-done.1.handed_ref
  43.0 55.6 %collective-permute-done.4.around_ref = bf16[2448,128]{1,0:T(8,128)(2,1)S(1)} collective-permute-done((bf16[2448,128]{1,0:T(8,128)(2,1)}, bf16[2448,128]{1,0:T(8,128)(2,1)S(1)}, u32[]{:S(2)}, u32[]{:S(2)}) %collective-permute-start.4) | collective-permute-done | bytes 626720 | tf_op jit(solution)/shard_map/ppermute | solution.py:26
  98.6 2.2 %lay_below.1 = (bf16[256,1536]{1,0:T(8,128)(2,1)S(1)}, f32[256,128]{1,0:T(8,128)S(1)}) custom-call(s32[1,4,3,12]{3,2,1,0:T(4,128)S(1)} %copy.8.lists_ref, s32[1,4]{1,0:T(1,128)S(1)} %copy-done.1, s32[38]{0:T(128)S(1)} %fusion.3.two_mask_ref, s32[38]{0:T(128)S(1)} %fusion.one_mask_ref, s32[38]{0:T(128)S(1)} %fusion.2.around_mask_ref, ...), custom_call_target="tpu_custom_call" | custom-call | bytes 1024 | tf_op jit(solution)/shard_map/lay_below/pallas_call | solution.py:193
  100.8 0.0 collective-permute-done.6
  100.8 1.0 last_product.1
  (4 shorter events, 0.0 us)
Async XLA Ops:
  0.0 37.0 %copy-start = (bf16[24,128,128]{2,1,0:T(8,128)(2,1)S(1)}, bf16[24,128,128]{2,1,0:T(8,128)(2,1)}, u32[]{:S(2)}) copy-start(bf16[24,128,128]{2,1,0:T(8,128)(2,1)} %right_ref.7) | copy-start | bytes 2359300
  0.0 37.0 %copy-start.2 = (s32[38]{0:T(128)S(1)}, s32[38]{0:T(128)}, u32[]{:S(2)}) copy-start(s32[38]{0:T(128)} %mask_ref.3) | copy-start | bytes 460
  0.0 34.7 %copy-start.4 = (s32[1,4,3,12]{3,1,2,0:T(4,128)S(1)}, s32[1,4,3,12]{3,1,2,0:T(4,128)}, u32[]{:S(2)}) copy-start(s32[1,4,3,12]{3,1,2,0:T(4,128)} %param.8) | copy-start | bytes 1732
  0.0 37.0 %copy-start.1 = (s32[1,4]{1,0:T(1,128)S(1)}, s32[1,4]{1,0:T(1,128)}, u32[]{:S(2)}) copy-start(s32[1,4]{1,0:T(1,128)} %counts_ref.5) | copy-start | bytes 52
  3.1 31.7 %collective-permute-start.2 = (bf16[2448,128]{1,0:T(8,128)(2,1)}, bf16[2448,128]{1,0:T(8,128)(2,1)S(1)}, u32[]{:S(2)}, u32[]{:S(2)}) collective-permute-start(bf16[2448,128]{1,0:T(8,128)(2,1)} %get-tuple-element.9.panel_ref), channel_id=1, source_target_pairs={{0,1},{1,2},{2,3},{4,5},{5,6},{6,7},{8,9},{9,10},{10,11},{12,13},{... | collective-permute-start | bytes 1880072 | tf_op jit(solution)/shard_map/ppermute | solution.py:26
  4.4 31.9 %collective-permute-start = (bf16[2448,128]{1,0:T(8,128)(2,1)}, bf16[2448,128]{1,0:T(8,128)(2,1)S(1)}, u32[]{:S(2)}, u32[]{:S(2)}) collective-permute-start(bf16[2448,128]{1,0:T(8,128)(2,1)} %get-tuple-element.9.panel_ref), channel_id=1, source_target_pairs={{0,2},{1,3},{2,4},{3,5},{4,6},{5,7},{6,8},{7,9},{8,10},{9,11},{10,... | collective-permute-start | bytes 1880072 | tf_op jit(solution)/shard_map/ppermute | solution.py:26
  6.3 34.6 %collective-permute-start.5 = (bf16[2448,128]{1,0:T(8,128)(2,1)}, bf16[2448,128]{1,0:T(8,128)(2,1)}, u32[]{:S(2)}, u32[]{:S(2)}) collective-permute-start(bf16[2448,128]{1,0:T(8,128)(2,1)} %get-tuple-element.9.panel_ref), channel_id=1, source_target_pairs={{1,0},{2,1},{3,2},{4,3},{5,4},{6,5},{7,6},{8,7},{9,8},{10,9},{11,1... | collective-permute-start | bytes 1880072 | tf_op jit(solution)/shard_map/ppermute | solution.py:26
  11.2 89.7 %collective-permute-start.6 = (bf16[12,128,128]{2,1,0:T(8,128)(2,1)}, bf16[12,128,128]{2,1,0:T(8,128)(2,1)S(1)}, u32[]{:S(2)}, u32[]{:S(2)}) collective-permute-start(bf16[12,128,128]{2,1,0:T(8,128)(2,1)} %get-tuple-element.11), channel_id=1, source_target_pairs={{0,64},{1,65},{2,66},{3,67},{4,68},{5,69},{6,70},{7,71},{8,72},{9,... | collective-permute-start | bytes 1179656 | tf_op jit(solution)/shard_map/ppermute | solution.py:26
  34.8 4.9 %collective-permute-start.3 = (bf16[2448,128]{1,0:T(8,128)(2,1)S(1)}, bf16[2448,128]{1,0:T(8,128)(2,1)}, u32[]{:S(2)}, u32[]{:S(2)}) collective-permute-start(bf16[2448,128]{1,0:T(8,128)(2,1)S(1)} %collective-permute-done.2.one_ref), channel_id=1, source_target_pairs={{1,61},{65,125},{129,189},{193,253},{257,317},{321,381},{385,445},... | collective-permute-start | bytes 1880072 | tf_op jit(solution)/shard_map/ppermute | solution.py:26
  36.3 6.7 %collective-permute-start.1 = (bf16[2448,128]{1,0:T(8,128)(2,1)S(1)}, bf16[2448,128]{1,0:T(8,128)(2,1)S(1)}, u32[]{:S(2)}, u32[]{:S(2)}) collective-permute-start(bf16[2448,128]{1,0:T(8,128)(2,1)S(1)} %collective-permute-done.two_ref), channel_id=1, source_target_pairs={{1,0},{5,4},{9,8},{13,12},{17,16},{21,20},{25,24},{29,28},{33,32},... | collective-permute-start | bytes 1880072 | tf_op jit(solution)/shard_map/ppermute | solution.py:26
  37.0 1.1 %copy-start.3 = (bf16[2448,128]{1,0:T(8,128)(2,1)S(1)}, bf16[2448,128]{1,0:T(8,128)(2,1)}, u32[]{:S(2)}) copy-start(bf16[2448,128]{1,0:T(8,128)(2,1)} %get-tuple-element.9.panel_ref) | copy-start | bytes 1880068
  39.6 58.9 %collective-permute-start.4 = (bf16[2448,128]{1,0:T(8,128)(2,1)}, bf16[2448,128]{1,0:T(8,128)(2,1)S(1)}, u32[]{:S(2)}, u32[]{:S(2)}) collective-permute-start(bf16[2448,128]{1,0:T(8,128)(2,1)} %collective-permute-done.3), channel_id=1, source_target_pairs={{61,63},{125,127},{189,191},{253,255},{317,319},{381,383},{445,447... | collective-permute-start | bytes 1880072 | tf_op jit(solution)/shard_map/ppermute | solution.py:26

commit v10 on v7

--- a/solution.py
+++ b/solution.py
@@ -82,12 +82,6 @@
         copy.wait()
 
 
-def second_kernel(mask_ref, left_ref, after_ref, packed_ref, sem):
-    del after_ref
-    pack_into(mask_ref, left_ref, packed_ref, sem)
-    wait_packed(packed_ref, sem)
-
-
 def first_stage(left_mask, lists, counts, left_blocks, right_blocks):
     return pl.pallas_call(
         first_kernel,
@@ -105,19 +99,6 @@
         cost_estimate=CHEAP,
         name="pack_and_cut",
     )(left_mask, lists, counts, left_blocks, right_blocks)
-
-
-def second_stage(left_mask, left_blocks, after):
-    return pl.pallas_call(
-        second_kernel,
-        out_shape=jax.ShapeDtypeStruct((CAP_L * BS + META, BS), jnp.bfloat16),
-        in_specs=[SMEM, ANY, ANY],
-        out_specs=VMEM,
-        scratch_shapes=[pltpu.SemaphoreType.DMA],
-        compiler_params=WIDE,
-        cost_estimate=CHEAP,
-        name="pack_again",
-    )(left_mask, left_blocks, after)
 
 
 def mask_of(packed, panel):
@@ -274,10 +255,8 @@
     )
     two_below = by_pairs(packed, shift(0, 2, always))
     right_before = by_pairs(sent_right, shift(1, 0, always))
-    mark = by_pairs(packed[:META], [(0, 1)])
-    again = second_stage(left_mask, left_blocks, mark)
-    one_above = by_pairs(again, shift(0, -1, lambda c: c > 0))
-    one_below = by_pairs(again, shift(0, 1, lambda c: c % RING < RING - 1))
+    one_above = by_pairs(packed, shift(0, -1, lambda c: c > 0))
+    one_below = by_pairs(packed, shift(0, 1, lambda c: c % RING < RING - 1))
     asked = by_pairs(ask, shift(0, 1, lambda c: c == last))
     handed = by_pairs(two_below, shift(0, -1, lambda c: c % RING == 1))
 
@@ -286,7 +265,8 @@
         0, 0, always, listed[: 3 * PCAP].reshape(1, 1, 3, PCAP), listed[3 * PCAP :].reshape(1, 1),
         left_mask, packed, asked[: CAPM * BS].reshape(CAPM, BS, BS), None, CHEAP, "answer",
     )
-    answer = by_pairs(answer, shift(0, -1, lambda c: c == 0))
+    answer = by_pairs(answer, shift(0, -3, lambda c: c == 0))
+    answer = by_pairs(answer, shift(0, 2, lambda c: c == last - 2))
 
     known = one_step(
         2, 0, always, pair_lists, pair_counts, left_mask, packed, right_blocks, None,
@@ -294,7 +274,7 @@
     )
     known = one_step(
         3, CAPM, lambda c: c < last, pair_lists, pair_counts, mask_of(one_above, panel),
-        one_above, right_blocks, known, CHEAP, "step_above",
+        one_above, right_blocks, known, DEAR, "step_above",
     )
     first = lax.axis_index("pcol") % RING == 0
     mask_one = jnp.where(first, mask_of(handed, panel), mask_of(one_below, panel))

time: 92.5 us -> 101 us (1.092)
  the two profiles are of different devices: /device:TPU:1022 before, /device:TPU:1 now
where the time goes in v10:
time: 101 us; the launch traced here: 99.9 us
  starting transfers between devices  62.1 us (61%)
  waiting for transfers between devices  21.4 us (21%)
  Pallas kernels  11.3 us (11%)
  local copies, waits for them, and re-layouts  4.23 us (4%)
    ppermute x8, starting transfers between devices, by_pairs(): return lax.ppermute(array, ('prow', 'pcol'), pairs)  62.1 us
    ppermute x8, waiting for transfers between devices, by_pairs(): return lax.ppermute(array, ('prow', 'pcol'), pairs)  21.4 us
    pallas_call x3, Pallas kernels, one_step(): pl.pallas_call(functools.partial(one_kernel, u, first, here), out_shape=j...  5.65 us
    unnamed x13, local copies, waits for them, and re-layouts  3.46 us
    pallas_call x1, Pallas kernels, first_stage(): pl.pallas_call(first_kernel, out_shape=[jax.ShapeDtypeStruct((CAP_L * BS...  3.32 us
  transfers between devices with their start and end apart: 8, of which 2 were waited for; matrix products, arithmetic and copies ran while one was open for 1% of the time, Pallas kernels for 7%

profile of v10, /device:TPU:1, one launch (start us, length us, event | category | flops | bytes accessed | tf_op | source)
XLA Modules:
  0.0 99.9 jit_solution(9143565739192560736)
XLA Ops:
  0.0 0.0 copy-start.4
  0.0 1.3 %copy.13.lists_ref = s32[1,4,3,12]{3,2,1,0:T(4,128)} copy(s32[1,4,3,12]{3,1,2,0:T(4,128)} %param.8) | data formatting | bytes 1152 | tf_op args[3]
  1.3 0.0 copy-start
  1.3 0.0 copy-start.3
  1.3 0.0 copy-start.5
  1.3 3.3 %pack_and_cut.1 = (bf16[2448,128]{1,0:T(8,128)(2,1)}, bf16[12,128,128]{2,1,0:T(8,128)(2,1)}, bf16[784,128]{1,0:T(8,128)(2,1)}) custom-call(s32[38]{0:T(128)} %mask_ref.5, s32[1,4,3,12]{3,2,1,0:T(4,128)} %copy.13.lists_ref, s32[1,4]{1,0:T(1,128)} %counts_ref.7, bf16[38,128,128]{2,1,0:T(8,128)(2,1)} %left_ref.1, bf16[24,128,128]{2,1,0:T(8,128)(2,1)} %right_ref.5), custom_call_target="tpu_custom_call" | custom-call | bytes 1024 | tf_op jit(solution)/shard_map/pack_and_cut/pallas_call | solution.py:86
  4.6 1.3 %collective-permute-start.4 = (bf16[784,128]{1,0:T(8,128)(2,1)}, bf16[784,128]{1,0:T(8,128)(2,1)S(1)}, u32[]{:S(2)}, u32[]{:S(2)}) collective-permute-start(bf16[784,128]{1,0:T(8,128)(2,1)} %get-tuple-element.11), channel_id=1, source_target_pairs={{63,0},{127,64},{191,128},{255,192},{319,256},{383,320},{447,384},... | collective-permute-start | bytes 602120 | tf_op jit(solution)/shard_map/ppermute | solution.py:27
  5.9 1.3 %collective-permute-start.3 = (bf16[2448,128]{1,0:T(8,128)(2,1)}, bf16[2448,128]{1,0:T(8,128)(2,1)}, u32[]{:S(2)}, u32[]{:S(2)}) collective-permute-start(bf16[2448,128]{1,0:T(8,128)(2,1)} %get-tuple-element.10.panel_ref), channel_id=1, source_target_pairs={{1,0},{2,1},{3,2},{4,3},{5,4},{6,5},{7,6},{8,7},{9,8},{10,9},{11,1... | collective-permute-start | bytes 1880072 | tf_op jit(solution)/shard_map/ppermute | solution.py:27
  7.2 4.0 %collective-permute-start.2 = (bf16[2448,128]{1,0:T(8,128)(2,1)}, bf16[2448,128]{1,0:T(8,128)(2,1)S(1)}, u32[]{:S(2)}, u32[]{:S(2)}) collective-permute-start(bf16[2448,128]{1,0:T(8,128)(2,1)} %get-tuple-element.10.panel_ref), channel_id=1, source_target_pairs={{0,1},{1,2},{2,3},{4,5},{5,6},{6,7},{8,9},{9,10},{10,11},{12,13},{... | collective-permute-start | bytes 1880072 | tf_op jit(solution)/shard_map/ppermute | solution.py:27
  11.3 5.0 %collective-permute-start = (bf16[2448,128]{1,0:T(8,128)(2,1)}, bf16[2448,128]{1,0:T(8,128)(2,1)S(1)}, u32[]{:S(2)}, u32[]{:S(2)}) collective-permute-start(bf16[2448,128]{1,0:T(8,128)(2,1)} %get-tuple-element.10.panel_ref), channel_id=1, source_target_pairs={{0,2},{1,3},{2,4},{3,5},{4,6},{5,7},{6,8},{7,9},{8,10},{9,11},{10,... | collective-permute-start | bytes 1880072 | tf_op jit(solution)/shard_map/ppermute | solution.py:27
  16.3 30.2 %collective-permute-start.7 = (bf16[12,128,128]{2,1,0:T(8,128)(2,1)}, bf16[12,128,128]{2,1,0:T(8,128)(2,1)S(1)}, u32[]{:S(2)}, u32[]{:S(2)}) collective-permute-start(bf16[12,128,128]{2,1,0:T(8,128)(2,1)} %get-tuple-element.13), channel_id=1, source_target_pairs={{0,64},{1,65},{2,66},{3,67},{4,68},{5,69},{6,70},{7,71},{8,72},{9,... | collective-permute-start | bytes 1179656 | tf_op jit(solution)/shard_map/ppermute | solution.py:27
  46.5 0.0 collective-permute-done.4
  46.5 0.7 slice.32.counts_ref
  47.2 0.1 reshape.23.lists_ref
  47.3 0.0 copy-done.4
  47.3 0.0 copy-start.1
  47.3 1.1 %copy-done.1 = bf16[2448,128]{1,0:T(8,128)(2,1)S(1)} copy-done((bf16[2448,128]{1,0:T(8,128)(2,1)S(1)}, bf16[2448,128]{1,0:T(8,128)(2,1)}, u32[]{:S(2)}) %copy-start.1) | copy-done | bytes 626712
  48.4 2.1 %answer.1 = f32[256,128]{1,0:T(8,128)S(1)} custom-call(s32[1,1,3,12]{3,2,1,0:T(4,128)S(1)} %reshape.23.lists_ref, s32[1,1]{1,0:T(1,128)} %slice.32.counts_ref, s32[38]{0:T(128)S(1)} %copy-done.4, bf16[2448,128]{1,0:T(8,128)(2,1)S(1)} %copy-done.1, bf16[6,128,128]{2,1,0:T(8,128)(2,1)S(1)} %bitcast.14), custom_call_target="tpu_custom_call" | custom-call | bytes 1024 | tf_op jit(solution)/shard_map/answer/pallas_call | solution.py:170
  50.4 18.4 %collective-permute-start.5 = (f32[256,128]{1,0:T(8,128)S(1)}, f32[256,128]{1,0:T(8,128)S(1)}, u32[]{:S(2)}, u32[]{:S(2)}) collective-permute-start(f32[256,128]{1,0:T(8,128)S(1)} %answer.1), channel_id=1, source_target_pairs={{0,61},{64,125},{128,189},{192,253},{256,317},{320,381},{384,445},... | collective-permute-start | bytes 393224 | tf_op jit(solution)/shard_map/ppermute | solution.py:27
  68.8 0.0 copy-done
  68.8 0.0 copy-done.3
  68.8 0.0 copy-done.5
  68.8 0.0 copy-start.2
  68.9 1.1 %copy-done.2 = bf16[2448,128]{1,0:T(8,128)(2,1)S(1)} copy-done((bf16[2448,128]{1,0:T(8,128)(2,1)S(1)}, bf16[2448,128]{1,0:T(8,128)(2,1)}, u32[]{:S(2)}) %copy-start.2) | copy-done | bytes 626712
  69.9 1.5 %own_step.1.refs_0_ = f32[256,128]{1,0:T(8,128)S(1)} custom-call(s32[1,4,3,12]{3,2,1,0:T(4,128)S(1)} %copy-done.3, s32[1,4]{1,0:T(1,128)S(1)} %copy-done.5, s32[38]{0:T(128)S(1)} %copy-done.4, bf16[2448,128]{1,0:T(8,128)(2,1)S(1)} %copy-done.2, bf16[24,128,128]{2,1,0:T(8,128)(2,1)S(1)} %copy-done), custom_call_target="tpu_custom_call" | custom-call | flops 34359738368 | bytes 1048576 | tf_op jit(solution)/shard_map/own_step/pallas_call | solution.py:170
  71.4 8.8 %collective-permute-done.5 = f32[256,128]{1,0:T(8,128)S(1)} collective-permute-done((f32[256,128]{1,0:T(8,128)S(1)}, f32[256,128]{1,0:T(8,128)S(1)}, u32[]{:S(2)}, u32[]{:S(2)}) %collective-permute-start.5) | collective-permute-done | bytes 131104 | tf_op jit(solution)/shard_map/ppermute | solution.py:27
  80.2 0.7 collective-permute-start.6
  80.9 0.0 collective-permute-done.3.panel_ref
  80.9 0.7 fusion.1.mask_ref
  81.6 0.0 collective-permute-done.two_ref
  81.6 1.3 %collective-permute-start.1 = (bf16[2448,128]{1,0:T(8,128)(2,1)S(1)}, bf16[2448,128]{1,0:T(8,128)(2,1)S(1)}, u32[]{:S(2)}, u32[]{:S(2)}) collective-permute-start(bf16[2448,128]{1,0:T(8,128)(2,1)S(1)} %collective-permute-done.two_ref), channel_id=1, source_target_pairs={{1,0},{5,4},{9,8},{13,12},{17,16},{21,20},{25,24},{29,28},{33,32},... | collective-permute-start | bytes 1880072 | tf_op jit(solution)/shard_map/ppermute | solution.py:27
  82.9 2.1 %step_above.1.early_ref = f32[256,128]{1,0:T(8,128)S(1)} custom-call(s32[1,4,3,12]{3,2,1,0:T(4,128)S(1)} %copy-done.3, s32[1,4]{1,0:T(1,128)S(1)} %copy-done.5, s32[38]{0:T(128)S(1)} %fusion.1.mask_ref, bf16[2448,128]{1,0:T(8,128)(2,1)} %collective-permute-done.3.panel_ref, bf16[24,128,128]{2,1,0:T(8,128)(2,1)S(1)} %copy-done, f32[256,128]{1,0:T(8,128)S(1)} %own_step.1.refs_0_), custom_call_target="tpu_custom_call" | custom-call | flops 34359738368 | bytes 1048576 | tf_op jit(solution)/shard_map/step_above/pallas_call | solution.py:170
  85.0 0.0 collective-permute-done.2.one_ref
  85.0 12.5 %collective-permute-done.1.handed_ref = bf16[2448,128]{1,0:T(8,128)(2,1)S(1)} collective-permute-done((bf16[2448,128]{1,0:T(8,128)(2,1)S(1)}, bf16[2448,128]{1,0:T(8,128)(2,1)S(1)}, u32[]{:S(2)}, u32[]{:S(2)}) %collective-permute-start.1) | collective-permute-done | bytes 626720 | tf_op jit(solution)/shard_map/ppermute | solution.py:27
  97.6 0.0 collective-permute-done.6.answer_ref
  97.6 1.3 %lay_below.1 = (bf16[256,1536]{1,0:T(8,128)(2,1)S(1)}, f32[256,128]{1,0:T(8,128)S(1)}) custom-call(s32[1,4,3,12]{3,2,1,0:T(4,128)S(1)} %copy-done.3, s32[1,4]{1,0:T(1,128)S(1)} %copy-done.5, s32[38]{0:T(128)S(1)} %fusion.2.two_mask_ref, s32[38]{0:T(128)S(1)} %fusion.one_mask_ref, bf16[2448,128]{1,0:T(8,128)(2,1)S(1)} %collective-permute-done.two_ref, ...), custom_call_target="tpu_custom_call" | custom-call | bytes 1024 | tf_op jit(solution)/shard_map/lay_below/pallas_call | solution.py:205
  98.9 0.0 collective-permute-done.7
  98.9 1.0 last_product.1
  (5 shorter events, 0.1 us)
Async XLA Ops:
  0.0 47.3 %copy-start.4 = (s32[38]{0:T(128)S(1)}, s32[38]{0:T(128)}, u32[]{:S(2)}) copy-start(s32[38]{0:T(128)} %mask_ref.5) | copy-start | bytes 460
  1.3 67.5 %copy-start = (bf16[24,128,128]{2,1,0:T(8,128)(2,1)S(1)}, bf16[24,128,128]{2,1,0:T(8,128)(2,1)}, u32[]{:S(2)}) copy-start(bf16[24,128,128]{2,1,0:T(8,128)(2,1)} %right_ref.5) | copy-start | bytes 2359300
  1.3 67.5 %copy-start.3 = (s32[1,4,3,12]{3,2,1,0:T(4,128)S(1)}, s32[1,4,3,12]{3,2,1,0:T(4,128)}, u32[]{:S(2)}) copy-start(s32[1,4,3,12]{3,2,1,0:T(4,128)} %copy.13.lists_ref) | copy-start | bytes 1732
  1.3 67.5 %copy-start.5 = (s32[1,4]{1,0:T(1,128)S(1)}, s32[1,4]{1,0:T(1,128)}, u32[]{:S(2)}) copy-start(s32[1,4]{1,0:T(1,128)} %counts_ref.7) | copy-start | bytes 52
  4.6 41.8 %collective-permute-start.4 = (bf16[784,128]{1,0:T(8,128)(2,1)}, bf16[784,128]{1,0:T(8,128)(2,1)S(1)}, u32[]{:S(2)}, u32[]{:S(2)}) collective-permute-start(bf16[784,128]{1,0:T(8,128)(2,1)} %get-tuple-element.11), channel_id=1, source_target_pairs={{63,0},{127,64},{191,128},{255,192},{319,256},{383,320},{447,384},... | collective-permute-start | bytes 602120 | tf_op jit(solution)/shard_map/ppermute | solution.py:27
  5.9 75.0 %collective-permute-start.3 = (bf16[2448,128]{1,0:T(8,128)(2,1)}, bf16[2448,128]{1,0:T(8,128)(2,1)}, u32[]{:S(2)}, u32[]{:S(2)}) collective-permute-start(bf16[2448,128]{1,0:T(8,128)(2,1)} %get-tuple-element.10.panel_ref), channel_id=1, source_target_pairs={{1,0},{2,1},{3,2},{4,3},{5,4},{6,5},{7,6},{8,7},{9,8},{10,9},{11,1... | collective-permute-start | bytes 1880072 | tf_op jit(solution)/shard_map/ppermute | solution.py:27
  7.2 77.8 %collective-permute-start.2 = (bf16[2448,128]{1,0:T(8,128)(2,1)}, bf16[2448,128]{1,0:T(8,128)(2,1)S(1)}, u32[]{:S(2)}, u32[]{:S(2)}) collective-permute-start(bf16[2448,128]{1,0:T(8,128)(2,1)} %get-tuple-element.10.panel_ref), channel_id=1, source_target_pairs={{0,1},{1,2},{2,3},{4,5},{5,6},{6,7},{8,9},{9,10},{10,11},{12,13},{... | collective-permute-start | bytes 1880072 | tf_op jit(solution)/shard_map/ppermute | solution.py:27
  11.3 70.3 %collective-permute-start = (bf16[2448,128]{1,0:T(8,128)(2,1)}, bf16[2448,128]{1,0:T(8,128)(2,1)S(1)}, u32[]{:S(2)}, u32[]{:S(2)}) collective-permute-start(bf16[2448,128]{1,0:T(8,128)(2,1)} %get-tuple-element.10.panel_ref), channel_id=1, source_target_pairs={{0,2},{1,3},{2,4},{3,5},{4,6},{5,7},{6,8},{7,9},{8,10},{9,11},{10,... | collective-permute-start | bytes 1880072 | tf_op jit(solution)/shard_map/ppermute | solution.py:27
  16.3 82.6 %collective-permute-start.7 = (bf16[12,128,128]{2,1,0:T(8,128)(2,1)}, bf16[12,128,128]{2,1,0:T(8,128)(2,1)S(1)}, u32[]{:S(2)}, u32[]{:S(2)}) collective-permute-start(bf16[12,128,128]{2,1,0:T(8,128)(2,1)} %get-tuple-element.13), channel_id=1, source_target_pairs={{0,64},{1,65},{2,66},{3,67},{4,68},{5,69},{6,70},{7,71},{8,72},{9,... | collective-permute-start | bytes 1179656 | tf_op jit(solution)/shard_map/ppermute | solution.py:27
  47.3 1.1 %copy-start.1 = (bf16[2448,128]{1,0:T(8,128)(2,1)S(1)}, bf16[2448,128]{1,0:T(8,128)(2,1)}, u32[]{:S(2)}) copy-start(bf16[2448,128]{1,0:T(8,128)(2,1)} %get-tuple-element.10.panel_ref) | copy-start | bytes 1880068
  50.4 29.8 %collective-permute-start.5 = (f32[256,128]{1,0:T(8,128)S(1)}, f32[256,128]{1,0:T(8,128)S(1)}, u32[]{:S(2)}, u32[]{:S(2)}) collective-permute-start(f32[256,128]{1,0:T(8,128)S(1)} %answer.1), channel_id=1, source_target_pairs={{0,61},{64,125},{128,189},{192,253},{256,317},{320,381},{384,445},... | collective-permute-start | bytes 393224 | tf_op jit(solution)/shard_map/ppermute | solution.py:27
  68.8 1.1 %copy-start.2 = (bf16[2448,128]{1,0:T(8,128)(2,1)S(1)}, bf16[2448,128]{1,0:T(8,128)(2,1)}, u32[]{:S(2)}) copy-start(bf16[2448,128]{1,0:T(8,128)(2,1)} %get-tuple-element.10.panel_ref) | copy-start | bytes 1880068
  80.2 17.3 %collective-permute-start.6 = (f32[256,128]{1,0:T(8,128)S(1)}, f32[256,128]{1,0:T(8,128)S(1)}, u32[]{:S(2)}, u32[]{:S(2)}) collective-permute-start(f32[256,128]{1,0:T(8,128)S(1)} %collective-permute-done.5), channel_id=1, source_target_pairs={{61,63},{125,127},{189,191},{253,255},{317,319},{381,383},{445,447... | collective-permute-start | bytes 393224 | tf_op jit(solution)/shard_map/ppermute | solution.py:27
  81.6 16.0 %collective-permute-start.1 = (bf16[2448,128]{1,0:T(8,128)(2,1)S(1)}, bf16[2448,128]{1,0:T(8,128)(2,1)S(1)}, u32[]{:S(2)}, u32[]{:S(2)}) collective-permute-start(bf16[2448,128]{1,0:T(8,128)(2,1)S(1)} %collective-permute-done.two_ref), channel_id=1, source_target_pairs={{1,0},{5,4},{9,8},{13,12},{17,16},{21,20},{25,24},{29,28},{33,32},... | collective-permute-start | bytes 1880072 | tf_op jit(solution)/shard_map/ppermute | solution.py:27

commit v11 on v8

--- a/solution.py
+++ b/solution.py
@@ -56,25 +56,29 @@
     pltpu.make_async_copy(blocks, blocks, sem).wait()
 
 
-def cut_kernel(right_ref, after_ref, part_ref, sem):
-    del after_ref
+def first_kernel(mask_ref, left_ref, right_ref, packed_ref, part_ref, sem, part_sem):
     half = part_ref.shape[0]
-    part = pltpu.make_async_copy(right_ref.at[pl.ds(half, half)], part_ref, sem)
+    part = pltpu.make_async_copy(right_ref.at[pl.ds(half, half)], part_ref, part_sem)
     part.start()
+    pack_into(mask_ref, left_ref, packed_ref, sem)
+    wait_packed(packed_ref, sem)
     part.wait()
 
 
-def cut(right_blocks, after):
-    return pl.pallas_call(
-        cut_kernel,
-        out_shape=jax.ShapeDtypeStruct((2 * CAPM, BS, BS), jnp.bfloat16),
-        in_specs=[ANY, ANY],
-        out_specs=VMEM,
-        scratch_shapes=[pltpu.SemaphoreType.DMA],
+def first_stage(left_mask, left_blocks, right_blocks):
+    return pl.pallas_call(
+        first_kernel,
+        out_shape=[
+            jax.ShapeDtypeStruct((CAP_L * BS + META, BS), jnp.bfloat16),
+            jax.ShapeDtypeStruct((2 * CAPM, BS, BS), jnp.bfloat16),
+        ],
+        in_specs=[SMEM, ANY, ANY],
+        out_specs=[VMEM, VMEM],
+        scratch_shapes=[pltpu.SemaphoreType.DMA, pltpu.SemaphoreType.DMA],
         compiler_params=WIDE,
         cost_estimate=CHEAP,
-        name="cut_right",
-    )(right_blocks, after)
+        name="pack_and_cut",
+    )(left_mask, left_blocks, right_blocks)
 
 
 def pack_kernel(mask_ref, left_ref, after_ref, packed_ref, sem):
@@ -181,11 +185,11 @@
 
 
 def late_kernel(
-    lists_ref, counts_ref, one_mask_ref, two_mask_ref,
-    two_ref, wrapped_ref, one_ref, handed_ref, laid_ref, rank_ref, sem,
+    lists_ref, counts_ref, two_mask_ref, one_mask_ref, two_ref, one_ref, handed_ref,
+    laid_ref, rank_ref, sem,
 ):
     laid_ref[...] = jnp.zeros_like(laid_ref)
-    two = ((two_ref, lambda c: c >= 2), (wrapped_ref, lambda c: c < 2))
+    two = ((two_ref, lambda c: c >= 0),)
     one = (
         (one_ref, lambda c: lax.rem(c, RING) != 0),
         (handed_ref, lambda c: lax.rem(c, RING) == 0),
@@ -199,43 +203,13 @@
     return pl.pallas_call(
         late_kernel,
         out_shape=jax.ShapeDtypeStruct((BR * BS, 2 * CAPM * BS), jnp.bfloat16),
-        in_specs=[SMEM] * 4 + [ANY] * 4,
+        in_specs=[SMEM] * 4 + [ANY] * 3,
         out_specs=VMEM,
         scratch_shapes=[pltpu.SMEM((masks[0].shape[0],), jnp.int32), pltpu.SemaphoreType.DMA],
         compiler_params=ROOM,
         cost_estimate=CHEAP,
         name="lay_below",
     )(lists, counts, *masks, *panels)
-
-
-def pass_kernel(two_ref, wrapped_ref, after_ref, passed_ref, sem):
-    del after_ref
-    column = lax.axis_index("pcol")
-
-    @pl.when(column == 1)
-    def _():
-        copy = pltpu.make_async_copy(wrapped_ref, passed_ref, sem)
-        copy.start()
-        copy.wait()
-
-    @pl.when(jnp.logical_and(column != 1, lax.rem(column, RING) == 1))
-    def _():
-        copy = pltpu.make_async_copy(two_ref, passed_ref, sem)
-        copy.start()
-        copy.wait()
-
-
-def pass_on(two_below, wrapped, after):
-    return pl.pallas_call(
-        pass_kernel,
-        out_shape=jax.ShapeDtypeStruct(two_below.shape, two_below.dtype),
-        in_specs=[ANY] * 3,
-        out_specs=VMEM,
-        scratch_shapes=[pltpu.SemaphoreType.DMA],
-        compiler_params=ROOM,
-        cost_estimate=CHEAP,
-        name="pass_on",
-    )(two_below, wrapped, after)
 
 
 def last_kernel(known_ref, left_ref, right_ref, out_ref):
@@ -257,7 +231,6 @@
 
 def on_device(n_row, n_col, left_blocks, left_mask, right_blocks, pair_lists, pair_counts):
     panel = left_blocks.shape[0]
-    last = n_col - 1
     half = 2 * CAPM
 
     def shift(rows, cols, chosen):
@@ -271,33 +244,28 @@
     def always(c):
         return c >= 0
 
-    column = lax.axis_index("pcol")
+    packed, sent_right = first_stage(left_mask, left_blocks, right_blocks)
+    two_below = by_pairs(packed, shift(0, 2, always))
+    right_before = by_pairs(sent_right, shift(1, 0, always))
     mark = by_pairs(left_mask, [(0, 1)])
-    mark_again = by_pairs(mark, [(1, 0)])
-    packed = pack(left_mask, left_blocks, left_mask, "pack_panel")
-    wrapped = by_pairs(packed, shift(0, 2, lambda c: c >= last - 1))
-    right_before = by_pairs(cut(right_blocks, mark), shift(1, 0, always))
-    again = pack(left_mask, left_blocks, mark_again, "pack_again")
-    two_below = by_pairs(again, shift(0, 2, lambda c: c < last - 1))
+    again = pack(left_mask, left_blocks, mark, "pack_again")
     one_above = by_pairs(again, shift(0, -1, always))
     one_below = by_pairs(again, shift(0, 1, lambda c: c % RING < RING - 1))
+    handed = by_pairs(two_below, shift(0, -1, lambda c: c % RING == 1))
+
     known = one_step(
-        2, 0, always, pair_lists, pair_counts, left_mask, again, right_blocks, None,
+        2, 0, always, pair_lists, pair_counts, left_mask, packed, right_blocks, None,
         DEAR, "own_step",
     )
-    passed = pass_on(two_below, wrapped, known)
-    handed = by_pairs(passed, shift(0, -1, lambda c: c % RING == 1))
     known = one_step(
         3, CAPM, always, pair_lists, pair_counts, mask_of(one_above, panel),
-        one_above, right_blocks, known, DEAR, "step_above",
-    )
-    mask_two = jnp.where(column < 2, mask_of(wrapped, panel), mask_of(two_below, panel))
-    mask_one = jnp.where(
-        column % RING != 0, mask_of(one_below, panel), mask_of(handed, panel)
-    )
+        one_above, right_blocks, known, CHEAP, "step_above",
+    )
+    first = lax.axis_index("pcol") % RING == 0
+    mask_one = jnp.where(first, mask_of(handed, panel), mask_of(one_below, panel))
     laid = late(
-        pair_lists, pair_counts, [mask_one, mask_two],
-        [two_below, wrapped, one_below, handed],
+        pair_lists, pair_counts, [mask_of(two_below, panel), mask_one],
+        [two_below, one_below, handed],
     )
     return last_product(known, laid, right_before.reshape(half * BS, BS))
 

time: 100 us -> 89.2 us (0.89)
  the two profiles are of different devices: /device:TPU:33 before, /device:TPU:1 now
where the time goes in v11:
time: 89.2 us; the launch traced here: 88.6 us
  starting transfers between devices  58 us (65%)
  waiting for transfers between devices  16.3 us (18%)
  Pallas kernels  11.8 us (13%)
  local copies, waits for them, and re-layouts  1.61 us (2%)
    ppermute x6, starting transfers between devices, by_pairs(): return lax.ppermute(array, ('prow', 'pcol'), pairs)  58 us
    ppermute x6, waiting for transfers between devices, by_pairs(): return lax.ppermute(array, ('prow', 'pcol'), pairs)  16.3 us
    pallas_call x2, Pallas kernels, one_step(): pl.pallas_call(functools.partial(one_kernel, u, first, here), out_shape=j...  3.58 us
    pallas_call x1, Pallas kernels, first_stage(): pl.pallas_call(first_kernel, out_shape=[jax.ShapeDtypeStruct((CAP_L * BS...  3.09 us
    pallas_call x1, Pallas kernels, pack(): pl.pallas_call(pack_kernel, out_shape=jax.ShapeDtypeStruct((CAP_L * BS +...  2.81 us
  transfers between devices with their start and end apart: 6, of which 1 were waited for; matrix products, arithmetic and copies ran while one was open for 1% of the time, Pallas kernels for 9%

profile of v11, /device:TPU:1, one launch (start us, length us, event | category | flops | bytes accessed | tf_op | source)
XLA Modules:
  0.0 88.6 jit_solution(17542055303623455001)
XLA Ops:
  0.0 0.0 copy-start.1
  0.0 0.0 copy-start.5
  0.0 3.1 %pack_and_cut.1 = (bf16[2448,128]{1,0:T(8,128)(2,1)}, bf16[12,128,128]{2,1,0:T(8,128)(2,1)}) custom-call(s32[38]{0:T(128)} %mask_ref.5, bf16[38,128,128]{2,1,0:T(8,128)(2,1)} %left_ref.3, bf16[24,128,128]{2,1,0:T(8,128)(2,1)} %right_ref.5), custom_call_target="tpu_custom_call" | custom-call | bytes 1024 | tf_op jit(solution)/shard_map/pack_and_cut/pallas_call | solution.py:69
  3.1 0.0 copy-start
  3.1 0.0 copy-start.2
  3.1 0.0 copy-start.3
  3.1 5.7 %collective-permute-start.2 = (bf16[2448,128]{1,0:T(8,128)(2,1)}, bf16[2448,128]{1,0:T(8,128)(2,1)S(1)}, u32[]{:S(2)}, u32[]{:S(2)}) collective-permute-start(bf16[2448,128]{1,0:T(8,128)(2,1)} %get-tuple-element.7.panel_ref), channel_id=1, source_target_pairs={{0,2},{1,3},{2,4},{3,5},{4,6},{5,7},{6,8},{7,9},{8,10},{9,11},{10,... | collective-permute-start | bytes 1880072 | tf_op jit(solution)/shard_map/ppermute | solution.py:26
  8.9 0.0 copy-done.1
  8.9 0.7 collective-permute-start
  9.5 29.5 %collective-permute-start.5 = (bf16[12,128,128]{2,1,0:T(8,128)(2,1)}, bf16[12,128,128]{2,1,0:T(8,128)(2,1)S(1)}, u32[]{:S(2)}, u32[]{:S(2)}) collective-permute-start(bf16[12,128,128]{2,1,0:T(8,128)(2,1)} %get-tuple-element.8), channel_id=1, source_target_pairs={{0,64},{1,65},{2,66},{3,67},{4,68},{5,69},{6,70},{7,71},{8,72},{9,... | collective-permute-start | bytes 1179656 | tf_op jit(solution)/shard_map/ppermute | solution.py:26
  39.1 0.0 copy-done.5
  39.1 0.0 collective-permute-done.after_ref
  39.1 0.0 copy-start.6
  39.1 0.5 copy-done.6
  39.6 2.8 %pack_again.1 = bf16[2448,128]{1,0:T(8,128)(2,1)} custom-call(s32[38]{0:T(128)} %mask_ref.5, bf16[38,128,128]{2,1,0:T(8,128)(2,1)} %left_ref.3, s32[38]{0:T(128)} %copy-done.6), custom_call_target="tpu_custom_call" | custom-call | bytes 1024 | tf_op jit(solution)/shard_map/pack_again/pallas_call | solution.py:91
  42.4 2.1 %collective-permute-start.4 = (bf16[2448,128]{1,0:T(8,128)(2,1)}, bf16[2448,128]{1,0:T(8,128)(2,1)S(1)}, u32[]{:S(2)}, u32[]{:S(2)}) collective-permute-start(bf16[2448,128]{1,0:T(8,128)(2,1)} %pack_again.1), channel_id=1, source_target_pairs={{0,1},{1,2},{2,3},{4,5},{5,6},{6,7},{8,9},{9,10},{10,11},{12,13},{... | collective-permute-start | bytes 1880072 | tf_op jit(solution)/shard_map/ppermute | solution.py:26
  44.5 18.8 %collective-permute-start.1 = (bf16[2448,128]{1,0:T(8,128)(2,1)}, bf16[2448,128]{1,0:T(8,128)(2,1)}, u32[]{:S(2)}, u32[]{:S(2)}) collective-permute-start(bf16[2448,128]{1,0:T(8,128)(2,1)} %pack_again.1), channel_id=1, source_target_pairs={{0,63},{1,0},{2,1},{3,2},{4,3},{5,4},{6,5},{7,6},{8,7},{9,8},{10,9... | collective-permute-start | bytes 1880072 | tf_op jit(solution)/shard_map/ppermute | solution.py:26
  63.3 0.0 collective-permute-done.2.two_ref
  63.3 1.3 %collective-permute-start.3 = (bf16[2448,128]{1,0:T(8,128)(2,1)S(1)}, bf16[2448,128]{1,0:T(8,128)(2,1)S(1)}, u32[]{:S(2)}, u32[]{:S(2)}) collective-permute-start(bf16[2448,128]{1,0:T(8,128)(2,1)S(1)} %collective-permute-done.2.two_ref), channel_id=1, source_target_pairs={{1,0},{5,4},{9,8},{13,12},{17,16},{21,20},{25,24},{29,28},{33,32},... | collective-permute-start | bytes 1880072 | tf_op jit(solution)/shard_map/ppermute | solution.py:26
  64.6 0.0 copy-done
  64.6 0.0 copy-done.2
  64.6 0.0 copy-done.3
  64.6 0.0 copy-start.4
  64.6 1.1 %copy-done.4 = bf16[2448,128]{1,0:T(8,128)(2,1)S(1)} copy-done((bf16[2448,128]{1,0:T(8,128)(2,1)S(1)}, bf16[2448,128]{1,0:T(8,128)(2,1)}, u32[]{:S(2)}) %copy-start.4) | copy-done | bytes 626712
  65.7 1.5 %own_step.1.refs_0_ = f32[256,128]{1,0:T(8,128)S(1)} custom-call(s32[1,4,3,12]{3,2,1,0:T(4,128)S(1)} %copy.7.lists_ref, s32[1,4]{1,0:T(1,128)S(1)} %copy-done.3, s32[38]{0:T(128)S(1)} %copy-done.2, bf16[2448,128]{1,0:T(8,128)(2,1)S(1)} %copy-done.4, bf16[24,128,128]{2,1,0:T(8,128)(2,1)S(1)} %copy-done), custom_call_target="tpu_custom_call" | custom-call | flops 34359738368 | bytes 1048576 | tf_op jit(solution)/shard_map/own_step/pallas_call | solution.py:169
  67.2 16.3 %collective-permute-done.1.panel_ref = bf16[2448,128]{1,0:T(8,128)(2,1)} collective-permute-done((bf16[2448,128]{1,0:T(8,128)(2,1)}, bf16[2448,128]{1,0:T(8,128)(2,1)}, u32[]{:S(2)}, u32[]{:S(2)}) %collective-permute-start.1) | collective-permute-done | bytes 626720 | tf_op jit(solution)/shard_map/ppermute | solution.py:26
  83.5 0.7 fusion.2.mask_ref
  84.2 2.1 %step_above.1.known_ref = f32[256,128]{1,0:T(8,128)S(1)} custom-call(s32[1,4,3,12]{3,2,1,0:T(4,128)S(1)} %copy.7.lists_ref, s32[1,4]{1,0:T(1,128)S(1)} %copy-done.3, s32[38]{0:T(128)S(1)} %fusion.2.mask_ref, bf16[2448,128]{1,0:T(8,128)(2,1)} %collective-permute-done.1.panel_ref, bf16[24,128,128]{2,1,0:T(8,128)(2,1)S(1)} %copy-done, ...), custom_call_target="tpu_custom_call" | custom-call | bytes 1024 | tf_op jit(solution)/shard_map/step_above/pallas_call | solution.py:169
  86.3 0.0 collective-permute-done.4.one_ref
  86.3 0.0 collective-permute-done.3.handed_ref
  86.3 1.3 %lay_below.1.left_ref = bf16[256,1536]{1,0:T(8,128)(2,1)S(1)} custom-call(s32[1,4,3,12]{3,2,1,0:T(4,128)S(1)} %copy.7.lists_ref, s32[1,4]{1,0:T(1,128)S(1)} %copy-done.3, s32[38]{0:T(128)S(1)} %fusion.1.two_mask_ref, s32[38]{0:T(128)S(1)} %fusion.one_mask_ref, bf16[2448,128]{1,0:T(8,128)(2,1)S(1)} %collective-permute-done.2.two_ref, ...), custom_call_target="tpu_custom_call" | custom-call | bytes 1024 | tf_op jit(solution)/shard_map/lay_below/pallas_call | solution.py:203
  87.6 0.0 collective-permute-done.5
  87.7 1.0 %last_product.1 = bf16[256,128]{1,0:T(8,128)(2,1)} custom-call(f32[256,128]{1,0:T(8,128)S(1)} %step_above.1.known_ref, bf16[256,1536]{1,0:T(8,128)(2,1)S(1)} %lay_below.1.left_ref, bf16[1536,128]{1,0:T(8,128)(2,1)S(1)} %bitcast.13), custom_call_target="tpu_custom_call" | custom-call | bytes 1024 | tf_op jit(solution)/shard_map/last_product/pallas_call | solution.py:221
  (3 shorter events, 0.0 us)
Async XLA Ops:
  0.0 8.9 %copy-start.1 = (s32[38]{0:T(128)S(1)}, s32[38]{0:T(128)}, u32[]{:S(2)}) copy-start(s32[38]{0:T(128)} %mask_ref.5) | copy-start | bytes 460
  0.0 39.1 %copy-start.5 = (s32[1,4,3,12]{3,1,2,0:T(4,128)S(1)}, s32[1,4,3,12]{3,1,2,0:T(4,128)}, u32[]{:S(2)}) copy-start(s32[1,4,3,12]{3,1,2,0:T(4,128)} %param.8) | copy-start | bytes 1732
  3.1 61.5 %copy-start = (bf16[24,128,128]{2,1,0:T(8,128)(2,1)S(1)}, bf16[24,128,128]{2,1,0:T(8,128)(2,1)}, u32[]{:S(2)}) copy-start(bf16[24,128,128]{2,1,0:T(8,128)(2,1)} %right_ref.5) | copy-start | bytes 2359300
  3.1 61.5 %copy-start.2 = (s32[38]{0:T(128)S(1)}, s32[38]{0:T(128)}, u32[]{:S(2)}) copy-start(s32[38]{0:T(128)} %mask_ref.5) | copy-start | bytes 460
  3.1 61.5 %copy-start.3 = (s32[1,4]{1,0:T(1,128)S(1)}, s32[1,4]{1,0:T(1,128)}, u32[]{:S(2)}) copy-start(s32[1,4]{1,0:T(1,128)} %counts_ref.5) | copy-start | bytes 52
  3.1 60.2 %collective-permute-start.2 = (bf16[2448,128]{1,0:T(8,128)(2,1)}, bf16[2448,128]{1,0:T(8,128)(2,1)S(1)}, u32[]{:S(2)}, u32[]{:S(2)}) collective-permute-start(bf16[2448,128]{1,0:T(8,128)(2,1)} %get-tuple-element.7.panel_ref), channel_id=1, source_target_pairs={{0,2},{1,3},{2,4},{3,5},{4,6},{5,7},{6,8},{7,9},{8,10},{9,11},{10,... | collective-permute-start | bytes 1880072 | tf_op jit(solution)/shard_map/ppermute | solution.py:26
  8.9 30.2 %collective-permute-start = (s32[38]{0:T(128)S(1)}, s32[38]{0:T(128)S(1)}, u32[]{:S(2)}, u32[]{:S(2)}) collective-permute-start(s32[38]{0:T(128)S(1)} %copy-done.1), channel_id=1, source_target_pairs={{0,1}} | collective-permute-start | bytes 464 | tf_op jit(solution)/shard_map/ppermute | solution.py:26
  9.5 78.1 %collective-permute-start.5 = (bf16[12,128,128]{2,1,0:T(8,128)(2,1)}, bf16[12,128,128]{2,1,0:T(8,128)(2,1)S(1)}, u32[]{:S(2)}, u32[]{:S(2)}) collective-permute-start(bf16[12,128,128]{2,1,0:T(8,128)(2,1)} %get-tuple-element.8), channel_id=1, source_target_pairs={{0,64},{1,65},{2,66},{3,67},{4,68},{5,69},{6,70},{7,71},{8,72},{9,... | collective-permute-start | bytes 1179656 | tf_op jit(solution)/shard_map/ppermute | solution.py:26
  39.1 0.5 copy-start.6
  42.4 43.8 %collective-permute-start.4 = (bf16[2448,128]{1,0:T(8,128)(2,1)}, bf16[2448,128]{1,0:T(8,128)(2,1)S(1)}, u32[]{:S(2)}, u32[]{:S(2)}) collective-permute-start(bf16[2448,128]{1,0:T(8,128)(2,1)} %pack_again.1), channel_id=1, source_target_pairs={{0,1},{1,2},{2,3},{4,5},{5,6},{6,7},{8,9},{9,10},{10,11},{12,13},{... | collective-permute-start | bytes 1880072 | tf_op jit(solution)/shard_map/ppermute | solution.py:26
  44.5 39.0 %collective-permute-start.1 = (bf16[2448,128]{1,0:T(8,128)(2,1)}, bf16[2448,128]{1,0:T(8,128)(2,1)}, u32[]{:S(2)}, u32[]{:S(2)}) collective-permute-start(bf16[2448,128]{1,0:T(8,128)(2,1)} %pack_again.1), channel_id=1, source_target_pairs={{0,63},{1,0},{2,1},{3,2},{4,3},{5,4},{6,5},{7,6},{8,7},{9,8},{10,9... | collective-permute-start | bytes 1880072 | tf_op jit(solution)/shard_map/ppermute | solution.py:26
  63.3 23.0 %collective-permute-start.3 = (bf16[2448,128]{1,0:T(8,128)(2,1)S(1)}, bf16[2448,128]{1,0:T(8,128)(2,1)S(1)}, u32[]{:S(2)}, u32[]{:S(2)}) collective-permute-start(bf16[2448,128]{1,0:T(8,128)(2,1)S(1)} %collective-permute-done.2.two_ref), channel_id=1, source_target_pairs={{1,0},{5,4},{9,8},{13,12},{17,16},{21,20},{25,24},{29,28},{33,32},... | collective-permute-start | bytes 1880072 | tf_op jit(solution)/shard_map/ppermute | solution.py:26
  64.6 1.1 %copy-start.4 = (bf16[2448,128]{1,0:T(8,128)(2,1)S(1)}, bf16[2448,128]{1,0:T(8,128)(2,1)}, u32[]{:S(2)}) copy-start(bf16[2448,128]{1,0:T(8,128)(2,1)} %get-tuple-element.7.panel_ref) | copy-start | bytes 1880068

commit v12 on v11

--- a/solution.py
+++ b/solution.py
@@ -149,7 +149,7 @@
 def one_kernel(
     u, first, here, lists_ref, counts_ref, mask_ref, panel_ref, right_ref, *refs,
 ):
-    before_ref = refs[0] if len(refs) == 7 else None
+    before_ref = refs[0] if len(refs) == 8 else None
     known_ref, left_ref, held_ref, rank_ref, sem, right_sem = refs[-6:]
     fetch_right = pltpu.make_async_copy(
         right_ref.at[pl.ds(first, CAPM)], held_ref, right_sem
@@ -164,12 +164,12 @@
     multiply(left_ref, held_ref, known_ref)
 
 
-def one_step(u, first, here, lists, counts, mask, panel, right, before, cost, name):
-    more = [] if before is None else [before]
+def one_step(u, first, here, lists, counts, mask, panel, right, before, after, cost, name):
+    more = [] if before is None else [before, after]
     return pl.pallas_call(
         functools.partial(one_kernel, u, first, here),
         out_shape=jax.ShapeDtypeStruct((BR * BS, BS), jnp.float32),
-        in_specs=[SMEM] * 3 + [ANY] * 2 + [VMEM] * len(more),
+        in_specs=[SMEM] * 3 + [ANY] * 2 + [VMEM, ANY][: len(more)],
         out_specs=VMEM,
         scratch_shapes=[
             pltpu.VMEM((BR * BS, CAPM * BS), jnp.bfloat16),
@@ -255,17 +255,19 @@
 
     known = one_step(
         2, 0, always, pair_lists, pair_counts, left_mask, packed, right_blocks, None,
-        DEAR, "own_step",
-    )
-    known = one_step(
-        3, CAPM, always, pair_lists, pair_counts, mask_of(one_above, panel),
-        one_above, right_blocks, known, CHEAP, "step_above",
+        None, DEAR, "own_step",
     )
     first = lax.axis_index("pcol") % RING == 0
     mask_one = jnp.where(first, mask_of(handed, panel), mask_of(one_below, panel))
     laid = late(
         pair_lists, pair_counts, [mask_of(two_below, panel), mask_one],
         [two_below, one_below, handed],
+    )
+    ordered = laid[0, :panel] * jnp.bfloat16(0)
+    mask_above = (one_above[CAP_L * BS, :panel] + ordered).astype(jnp.int32)
+    known = one_step(
+        3, CAPM, always, pair_lists, pair_counts, mask_above,
+        one_above, right_blocks, known, laid, CHEAP, "step_above",
     )
     return last_product(known, laid, right_before.reshape(half * BS, BS))
 

time: 89.2 us -> 88.1 us (0.988)
  waiting for transfers between devices: 16.3 us -> 14.8 us
    ppermute x6, waiting for transfers between devices: 16.3 us -> 14.8 us  [by_pairs(): return lax.ppermute(array, ('prow', 'pcol'), pairs)]
  transfers between devices with their start and end apart: 6 -> 6, of which waited for: 1 -> 2; matrix products, arithmetic and copies ran while one was open for 1% -> 1% of each run, Pallas kernels for 9% -> 9%
where the time goes in v12:
time: 88.1 us; the launch traced here: 87.3 us
  starting transfers between devices  58.4 us (66%)
  waiting for transfers between devices  14.8 us (17%)
  Pallas kernels  11.6 us (13%)
  local copies, waits for them, and re-layouts  1.61 us (2%)
    ppermute x6, starting transfers between devices, by_pairs(): return lax.ppermute(array, ('prow', 'pcol'), pairs)  58.4 us
    ppermute x6, waiting for transfers between devices, by_pairs(): return lax.ppermute(array, ('prow', 'pcol'), pairs)  14.8 us
    pallas_call x2, Pallas kernels, one_step(): pl.pallas_call(functools.partial(one_kernel, u, first, here), out_shape=j...  3.59 us
    pallas_call x1, Pallas kernels, first_stage(): pl.pallas_call(first_kernel, out_shape=[jax.ShapeDtypeStruct((CAP_L * BS...  3.03 us
    pallas_call x1, Pallas kernels, pack(): pl.pallas_call(pack_kernel, out_shape=jax.ShapeDtypeStruct((CAP_L * BS +...  2.61 us
  transfers between devices with their start and end apart: 6, of which 2 were waited for; matrix products, arithmetic and copies ran while one was open for 1% of the time, Pallas kernels for 9%

profile of v12, /device:TPU:1, one launch (start us, length us, event | category | flops | bytes accessed | tf_op | source)
XLA Modules:
  0.0 87.3 jit_solution(10258210220885911762)
XLA Ops:
  0.0 0.0 copy-start.1
  0.0 0.0 copy-start.5
  0.0 3.0 %pack_and_cut.1 = (bf16[2448,128]{1,0:T(8,128)(2,1)}, bf16[12,128,128]{2,1,0:T(8,128)(2,1)}) custom-call(s32[38]{0:T(128)} %mask_ref.5, bf16[38,128,128]{2,1,0:T(8,128)(2,1)} %left_ref.3, bf16[24,128,128]{2,1,0:T(8,128)(2,1)} %right_ref.5), custom_call_target="tpu_custom_call" | custom-call | bytes 1024 | tf_op jit(solution)/shard_map/pack_and_cut/pallas_call | solution.py:69
  3.0 0.0 copy-start
  3.1 0.0 copy-start.2
  3.1 0.0 copy-start.3
  3.1 5.7 %collective-permute-start.2 = (bf16[2448,128]{1,0:T(8,128)(2,1)}, bf16[2448,128]{1,0:T(8,128)(2,1)S(1)}, u32[]{:S(2)}, u32[]{:S(2)}) collective-permute-start(bf16[2448,128]{1,0:T(8,128)(2,1)} %get-tuple-element.7.panel_ref), channel_id=1, source_target_pairs={{0,2},{1,3},{2,4},{3,5},{4,6},{5,7},{6,8},{7,9},{8,10},{9,11},{10,... | collective-permute-start | bytes 1880072 | tf_op jit(solution)/shard_map/ppermute | solution.py:26
  8.8 0.0 copy-done.1
  8.8 0.7 collective-permute-start
  9.5 29.6 %collective-permute-start.5 = (bf16[12,128,128]{2,1,0:T(8,128)(2,1)}, bf16[12,128,128]{2,1,0:T(8,128)(2,1)S(1)}, u32[]{:S(2)}, u32[]{:S(2)}) collective-permute-start(bf16[12,128,128]{2,1,0:T(8,128)(2,1)} %get-tuple-element.8), channel_id=1, source_target_pairs={{0,64},{1,65},{2,66},{3,67},{4,68},{5,69},{6,70},{7,71},{8,72},{9,... | collective-permute-start | bytes 1179656 | tf_op jit(solution)/shard_map/ppermute | solution.py:26
  39.1 0.0 copy-done.5
  39.1 0.0 collective-permute-done.after_ref
  39.1 0.0 copy-start.6
  39.1 0.5 copy-done.6
  39.6 2.6 %pack_again.1 = bf16[2448,128]{1,0:T(8,128)(2,1)} custom-call(s32[38]{0:T(128)} %mask_ref.5, bf16[38,128,128]{2,1,0:T(8,128)(2,1)} %left_ref.3, s32[38]{0:T(128)} %copy-done.6), custom_call_target="tpu_custom_call" | custom-call | bytes 1024 | tf_op jit(solution)/shard_map/pack_again/pallas_call | solution.py:91
  42.2 2.3 %collective-permute-start.4 = (bf16[2448,128]{1,0:T(8,128)(2,1)}, bf16[2448,128]{1,0:T(8,128)(2,1)S(1)}, u32[]{:S(2)}, u32[]{:S(2)}) collective-permute-start(bf16[2448,128]{1,0:T(8,128)(2,1)} %pack_again.1), channel_id=1, source_target_pairs={{0,1},{1,2},{2,3},{4,5},{5,6},{6,7},{8,9},{9,10},{10,11},{12,13},{... | collective-permute-start | bytes 1880072 | tf_op jit(solution)/shard_map/ppermute | solution.py:26
  44.6 18.8 %collective-permute-start.1 = (bf16[2448,128]{1,0:T(8,128)(2,1)}, bf16[2448,128]{1,0:T(8,128)(2,1)}, u32[]{:S(2)}, u32[]{:S(2)}) collective-permute-start(bf16[2448,128]{1,0:T(8,128)(2,1)} %pack_again.1), channel_id=1, source_target_pairs={{0,63},{1,0},{2,1},{3,2},{4,3},{5,4},{6,5},{7,6},{8,7},{9,8},{10,9... | collective-permute-start | bytes 1880072 | tf_op jit(solution)/shard_map/ppermute | solution.py:26
  63.4 0.0 collective-permute-done.2.two_ref
  63.4 1.3 %collective-permute-start.3 = (bf16[2448,128]{1,0:T(8,128)(2,1)S(1)}, bf16[2448,128]{1,0:T(8,128)(2,1)S(1)}, u32[]{:S(2)}, u32[]{:S(2)}) collective-permute-start(bf16[2448,128]{1,0:T(8,128)(2,1)S(1)} %collective-permute-done.2.two_ref), channel_id=1, source_target_pairs={{1,0},{5,4},{9,8},{13,12},{17,16},{21,20},{25,24},{29,28},{33,32},... | collective-permute-start | bytes 1880072 | tf_op jit(solution)/shard_map/ppermute | solution.py:26
  64.7 0.0 copy-done
  64.7 0.0 copy-done.2
  64.7 0.0 copy-done.3
  64.8 0.0 copy-start.4
  64.8 1.1 %copy-done.4 = bf16[2448,128]{1,0:T(8,128)(2,1)S(1)} copy-done((bf16[2448,128]{1,0:T(8,128)(2,1)S(1)}, bf16[2448,128]{1,0:T(8,128)(2,1)}, u32[]{:S(2)}) %copy-start.4) | copy-done | bytes 626712
  65.8 1.5 %own_step.1.refs_0_ = f32[256,128]{1,0:T(8,128)S(1)} custom-call(s32[1,4,3,12]{3,2,1,0:T(4,128)S(1)} %copy.8.lists_ref, s32[1,4]{1,0:T(1,128)S(1)} %copy-done.3, s32[38]{0:T(128)S(1)} %copy-done.2, bf16[2448,128]{1,0:T(8,128)(2,1)S(1)} %copy-done.4, bf16[24,128,128]{2,1,0:T(8,128)(2,1)S(1)} %copy-done), custom_call_target="tpu_custom_call" | custom-call | flops 34359738368 | bytes 1048576 | tf_op jit(solution)/shard_map/own_step/pallas_call | solution.py:169
  67.4 0.0 collective-permute-done.4.one_ref
  67.4 7.1 %collective-permute-done.3.handed_ref = bf16[2448,128]{1,0:T(8,128)(2,1)S(1)} collective-permute-done((bf16[2448,128]{1,0:T(8,128)(2,1)S(1)}, bf16[2448,128]{1,0:T(8,128)(2,1)S(1)}, u32[]{:S(2)}, u32[]{:S(2)}) %collective-permute-start.3) | collective-permute-done | bytes 626720 | tf_op jit(solution)/shard_map/ppermute | solution.py:26
  74.5 1.3 %lay_below.1.refs_1_.left_ref = bf16[256,1536]{1,0:T(8,128)(2,1)S(1)} custom-call(s32[1,4,3,12]{3,2,1,0:T(4,128)S(1)} %copy.8.lists_ref, s32[1,4]{1,0:T(1,128)S(1)} %copy-done.3, s32[38]{0:T(128)S(1)} %fusion.2.two_mask_ref, s32[38]{0:T(128)S(1)} %fusion.one_mask_ref, bf16[2448,128]{1,0:T(8,128)(2,1)S(1)} %collective-permute-done.2.two_ref, ...), custom_call_target="tpu_custom_call" | custom-call | bytes 1024 | tf_op jit(solution)/shard_map/lay_below/pallas_call | solution.py:203
  75.8 7.7 %collective-permute-done.1.panel_ref = bf16[2448,128]{1,0:T(8,128)(2,1)} collective-permute-done((bf16[2448,128]{1,0:T(8,128)(2,1)}, bf16[2448,128]{1,0:T(8,128)(2,1)}, u32[]{:S(2)}, u32[]{:S(2)}) %collective-permute-start.1) | collective-permute-done | bytes 626720 | tf_op jit(solution)/shard_map/ppermute | solution.py:26
  83.5 0.7 bitcast_convert_fusion.mask_ref
  84.2 2.1 %step_above.1.known_ref = f32[256,128]{1,0:T(8,128)S(1)} custom-call(s32[1,4,3,12]{3,2,1,0:T(4,128)S(1)} %copy.8.lists_ref, s32[1,4]{1,0:T(1,128)S(1)} %copy-done.3, s32[38]{0:T(128)S(1)} %bitcast_convert_fusion.mask_ref, bf16[2448,128]{1,0:T(8,128)(2,1)} %collective-permute-done.1.panel_ref, bf16[24,128,128]{2,1,0:T(8,128)(2,1)S(1)} %copy-done, ...), custom_call_target="tpu_custom_call" | custom-call | bytes 1024 | tf_op jit(solution)/shard_map/step_above/pallas_call | solution.py:169
  86.3 0.0 collective-permute-done.5
  86.3 1.0 %last_product.1 = bf16[256,128]{1,0:T(8,128)(2,1)} custom-call(f32[256,128]{1,0:T(8,128)S(1)} %step_above.1.known_ref, bf16[256,1536]{1,0:T(8,128)(2,1)S(1)} %lay_below.1.refs_1_.left_ref, bf16[1536,128]{1,0:T(8,128)(2,1)S(1)} %bitcast.11), custom_call_target="tpu_custom_call" | custom-call | bytes 1024 | tf_op jit(solution)/shard_map/last_product/pallas_call | solution.py:221
  (3 shorter events, 0.0 us)
Async XLA Ops:
  0.0 8.8 %copy-start.1 = (s32[38]{0:T(128)S(1)}, s32[38]{0:T(128)}, u32[]{:S(2)}) copy-start(s32[38]{0:T(128)} %mask_ref.5) | copy-start | bytes 460
  0.0 39.1 %copy-start.5 = (s32[1,4,3,12]{3,1,2,0:T(4,128)S(1)}, s32[1,4,3,12]{3,1,2,0:T(4,128)}, u32[]{:S(2)}) copy-start(s32[1,4,3,12]{3,1,2,0:T(4,128)} %param.8) | copy-start | bytes 1732
  3.0 61.7 %copy-start = (bf16[24,128,128]{2,1,0:T(8,128)(2,1)S(1)}, bf16[24,128,128]{2,1,0:T(8,128)(2,1)}, u32[]{:S(2)}) copy-start(bf16[24,128,128]{2,1,0:T(8,128)(2,1)} %right_ref.5) | copy-start | bytes 2359300
  3.1 61.7 %copy-start.2 = (s32[38]{0:T(128)S(1)}, s32[38]{0:T(128)}, u32[]{:S(2)}) copy-start(s32[38]{0:T(128)} %mask_ref.5) | copy-start | bytes 460
  3.1 61.7 %copy-start.3 = (s32[1,4]{1,0:T(1,128)S(1)}, s32[1,4]{1,0:T(1,128)}, u32[]{:S(2)}) copy-start(s32[1,4]{1,0:T(1,128)} %counts_ref.5) | copy-start | bytes 52
  3.1 60.3 %collective-permute-start.2 = (bf16[2448,128]{1,0:T(8,128)(2,1)}, bf16[2448,128]{1,0:T(8,128)(2,1)S(1)}, u32[]{:S(2)}, u32[]{:S(2)}) collective-permute-start(bf16[2448,128]{1,0:T(8,128)(2,1)} %get-tuple-element.7.panel_ref), channel_id=1, source_target_pairs={{0,2},{1,3},{2,4},{3,5},{4,6},{5,7},{6,8},{7,9},{8,10},{9,11},{10,... | collective-permute-start | bytes 1880072 | tf_op jit(solution)/shard_map/ppermute | solution.py:26
  8.8 30.3 %collective-permute-start = (s32[38]{0:T(128)S(1)}, s32[38]{0:T(128)S(1)}, u32[]{:S(2)}, u32[]{:S(2)}) collective-permute-start(s32[38]{0:T(128)S(1)} %copy-done.1), channel_id=1, source_target_pairs={{0,1}} | collective-permute-start | bytes 464 | tf_op jit(solution)/shard_map/ppermute | solution.py:26
  9.5 76.8 %collective-permute-start.5 = (bf16[12,128,128]{2,1,0:T(8,128)(2,1)}, bf16[12,128,128]{2,1,0:T(8,128)(2,1)S(1)}, u32[]{:S(2)}, u32[]{:S(2)}) collective-permute-start(bf16[12,128,128]{2,1,0:T(8,128)(2,1)} %get-tuple-element.8), channel_id=1, source_target_pairs={{0,64},{1,65},{2,66},{3,67},{4,68},{5,69},{6,70},{7,71},{8,72},{9,... | collective-permute-start | bytes 1179656 | tf_op jit(solution)/shard_map/ppermute | solution.py:26
  39.1 0.5 copy-start.6
  42.2 25.1 %collective-permute-start.4 = (bf16[2448,128]{1,0:T(8,128)(2,1)}, bf16[2448,128]{1,0:T(8,128)(2,1)S(1)}, u32[]{:S(2)}, u32[]{:S(2)}) collective-permute-start(bf16[2448,128]{1,0:T(8,128)(2,1)} %pack_again.1), channel_id=1, source_target_pairs={{0,1},{1,2},{2,3},{4,5},{5,6},{6,7},{8,9},{9,10},{10,11},{12,13},{... | collective-permute-start | bytes 1880072 | tf_op jit(solution)/shard_map/ppermute | solution.py:26
  44.6 38.9 %collective-permute-start.1 = (bf16[2448,128]{1,0:T(8,128)(2,1)}, bf16[2448,128]{1,0:T(8,128)(2,1)}, u32[]{:S(2)}, u32[]{:S(2)}) collective-permute-start(bf16[2448,128]{1,0:T(8,128)(2,1)} %pack_again.1), channel_id=1, source_target_pairs={{0,63},{1,0},{2,1},{3,2},{4,3},{5,4},{6,5},{7,6},{8,7},{9,8},{10,9... | collective-permute-start | bytes 1880072 | tf_op jit(solution)/shard_map/ppermute | solution.py:26
  63.4 11.0 %collective-permute-start.3 = (bf16[2448,128]{1,0:T(8,128)(2,1)S(1)}, bf16[2448,128]{1,0:T(8,128)(2,1)S(1)}, u32[]{:S(2)}, u32[]{:S(2)}) collective-permute-start(bf16[2448,128]{1,0:T(8,128)(2,1)S(1)} %collective-permute-done.2.two_ref), channel_id=1, source_target_pairs={{1,0},{5,4},{9,8},{13,12},{17,16},{21,20},{25,24},{29,28},{33,32},... | collective-permute-start | bytes 1880072 | tf_op jit(solution)/shard_map/ppermute | solution.py:26
  64.8 1.1 %copy-start.4 = (bf16[2448,128]{1,0:T(8,128)(2,1)S(1)}, bf16[2448,128]{1,0:T(8,128)(2,1)}, u32[]{:S(2)}) copy-start(bf16[2448,128]{1,0:T(8,128)(2,1)} %get-tuple-element.7.panel_ref) | copy-start | bytes 1880068

commit v13 on v12

--- a/solution.py
+++ b/solution.py
@@ -247,7 +247,7 @@
     packed, sent_right = first_stage(left_mask, left_blocks, right_blocks)
     two_below = by_pairs(packed, shift(0, 2, always))
     right_before = by_pairs(sent_right, shift(1, 0, always))
-    mark = by_pairs(left_mask, [(0, 1)])
+    mark = by_pairs(left_mask, [(n_col // 2, n_col + n_col // 2)])
     again = pack(left_mask, left_blocks, mark, "pack_again")
     one_above = by_pairs(again, shift(0, -1, always))
     one_below = by_pairs(again, shift(0, 1, lambda c: c % RING < RING - 1))

time: 88.1 us -> 88.1 us (level)
  no operation moved by 1% of the time
where the time goes in v13:
time: 88.1 us; the launch traced here: 87.3 us
  starting transfers between devices  58.7 us (67%)
  waiting for transfers between devices  14.6 us (17%)
  Pallas kernels  11.5 us (13%)
  local copies, waits for them, and re-layouts  1.61 us (2%)
    ppermute x6, starting transfers between devices, by_pairs(): return lax.ppermute(array, ('prow', 'pcol'), pairs)  58.7 us
    ppermute x6, waiting for transfers between devices, by_pairs(): return lax.ppermute(array, ('prow', 'pcol'), pairs)  14.6 us
    pallas_call x2, Pallas kernels, one_step(): pl.pallas_call(functools.partial(one_kernel, u, first, here), out_shape=j...  3.59 us
    pallas_call x1, Pallas kernels, first_stage(): pl.pallas_call(first_kernel, out_shape=[jax.ShapeDtypeStruct((CAP_L * BS...  2.97 us
    pallas_call x1, Pallas kernels, pack(): pl.pallas_call(pack_kernel, out_shape=jax.ShapeDtypeStruct((CAP_L * BS +...  2.61 us
  transfers between devices with their start and end apart: 6, of which 2 were waited for; matrix products, arithmetic and copies ran while one was open for 1% of the time, Pallas kernels for 9%

profile of v13, /device:TPU:1, one launch (start us, length us, event | category | flops | bytes accessed | tf_op | source)
XLA Modules:
  0.0 87.3 jit_solution(16110374557079073075)
XLA Ops:
  0.0 0.0 copy-start.1
  0.0 0.0 copy-start.5
  0.0 3.0 %pack_and_cut.1 = (bf16[2448,128]{1,0:T(8,128)(2,1)}, bf16[12,128,128]{2,1,0:T(8,128)(2,1)}) custom-call(s32[38]{0:T(128)} %mask_ref.5, bf16[38,128,128]{2,1,0:T(8,128)(2,1)} %left_ref.3, bf16[24,128,128]{2,1,0:T(8,128)(2,1)} %right_ref.5), custom_call_target="tpu_custom_call" | custom-call | bytes 1024 | tf_op jit(solution)/shard_map/pack_and_cut/pallas_call | solution.py:69
  3.0 0.0 copy-start
  3.0 0.0 copy-start.2
  3.0 0.0 copy-start.3
  3.0 5.9 %collective-permute-start.2 = (bf16[2448,128]{1,0:T(8,128)(2,1)}, bf16[2448,128]{1,0:T(8,128)(2,1)S(1)}, u32[]{:S(2)}, u32[]{:S(2)}) collective-permute-start(bf16[2448,128]{1,0:T(8,128)(2,1)} %get-tuple-element.7.panel_ref), channel_id=1, source_target_pairs={{0,2},{1,3},{2,4},{3,5},{4,6},{5,7},{6,8},{7,9},{8,10},{9,11},{10,... | collective-permute-start | bytes 1880072 | tf_op jit(solution)/shard_map/ppermute | solution.py:26
  8.9 0.0 copy-done.1
  8.9 0.7 collective-permute-start
  9.6 29.5 %collective-permute-start.5 = (bf16[12,128,128]{2,1,0:T(8,128)(2,1)}, bf16[12,128,128]{2,1,0:T(8,128)(2,1)S(1)}, u32[]{:S(2)}, u32[]{:S(2)}) collective-permute-start(bf16[12,128,128]{2,1,0:T(8,128)(2,1)} %get-tuple-element.8), channel_id=1, source_target_pairs={{0,64},{1,65},{2,66},{3,67},{4,68},{5,69},{6,70},{7,71},{8,72},{9,... | collective-permute-start | bytes 1179656 | tf_op jit(solution)/shard_map/ppermute | solution.py:26
  39.1 0.0 copy-done.5
  39.1 0.0 collective-permute-done.after_ref
  39.1 0.0 copy-start.6
  39.1 0.5 copy-done.6
  39.6 2.6 %pack_again.1 = bf16[2448,128]{1,0:T(8,128)(2,1)} custom-call(s32[38]{0:T(128)} %mask_ref.5, bf16[38,128,128]{2,1,0:T(8,128)(2,1)} %left_ref.3, s32[38]{0:T(128)} %copy-done.6), custom_call_target="tpu_custom_call" | custom-call | bytes 1024 | tf_op jit(solution)/shard_map/pack_again/pallas_call | solution.py:91
  42.2 2.3 %collective-permute-start.4 = (bf16[2448,128]{1,0:T(8,128)(2,1)}, bf16[2448,128]{1,0:T(8,128)(2,1)S(1)}, u32[]{:S(2)}, u32[]{:S(2)}) collective-permute-start(bf16[2448,128]{1,0:T(8,128)(2,1)} %pack_again.1), channel_id=1, source_target_pairs={{0,1},{1,2},{2,3},{4,5},{5,6},{6,7},{8,9},{9,10},{10,11},{12,13},{... | collective-permute-start | bytes 1880072 | tf_op jit(solution)/shard_map/ppermute | solution.py:26
  44.5 19.1 %collective-permute-start.1 = (bf16[2448,128]{1,0:T(8,128)(2,1)}, bf16[2448,128]{1,0:T(8,128)(2,1)}, u32[]{:S(2)}, u32[]{:S(2)}) collective-permute-start(bf16[2448,128]{1,0:T(8,128)(2,1)} %pack_again.1), channel_id=1, source_target_pairs={{0,63},{1,0},{2,1},{3,2},{4,3},{5,4},{6,5},{7,6},{8,7},{9,8},{10,9... | collective-permute-start | bytes 1880072 | tf_op jit(solution)/shard_map/ppermute | solution.py:26
  63.6 0.0 collective-permute-done.2.two_ref
  63.6 1.3 %collective-permute-start.3 = (bf16[2448,128]{1,0:T(8,128)(2,1)S(1)}, bf16[2448,128]{1,0:T(8,128)(2,1)S(1)}, u32[]{:S(2)}, u32[]{:S(2)}) collective-permute-start(bf16[2448,128]{1,0:T(8,128)(2,1)S(1)} %collective-permute-done.2.two_ref), channel_id=1, source_target_pairs={{1,0},{5,4},{9,8},{13,12},{17,16},{21,20},{25,24},{29,28},{33,32},... | collective-permute-start | bytes 1880072 | tf_op jit(solution)/shard_map/ppermute | solution.py:26
  64.9 0.0 copy-done
  64.9 0.0 copy-done.2
  64.9 0.0 copy-done.3
  64.9 0.0 copy-start.4
  64.9 1.1 %copy-done.4 = bf16[2448,128]{1,0:T(8,128)(2,1)S(1)} copy-done((bf16[2448,128]{1,0:T(8,128)(2,1)S(1)}, bf16[2448,128]{1,0:T(8,128)(2,1)}, u32[]{:S(2)}) %copy-start.4) | copy-done | bytes 626712
  66.0 1.5 %own_step.1.refs_0_ = f32[256,128]{1,0:T(8,128)S(1)} custom-call(s32[1,4,3,12]{3,2,1,0:T(4,128)S(1)} %copy.8.lists_ref, s32[1,4]{1,0:T(1,128)S(1)} %copy-done.3, s32[38]{0:T(128)S(1)} %copy-done.2, bf16[2448,128]{1,0:T(8,128)(2,1)S(1)} %copy-done.4, bf16[24,128,128]{2,1,0:T(8,128)(2,1)S(1)} %copy-done), custom_call_target="tpu_custom_call" | custom-call | flops 34359738368 | bytes 1048576 | tf_op jit(solution)/shard_map/own_step/pallas_call | solution.py:169
  67.5 0.0 collective-permute-done.4.one_ref
  67.5 7.1 %collective-permute-done.3.handed_ref = bf16[2448,128]{1,0:T(8,128)(2,1)S(1)} collective-permute-done((bf16[2448,128]{1,0:T(8,128)(2,1)S(1)}, bf16[2448,128]{1,0:T(8,128)(2,1)S(1)}, u32[]{:S(2)}, u32[]{:S(2)}) %collective-permute-start.3) | collective-permute-done | bytes 626720 | tf_op jit(solution)/shard_map/ppermute | solution.py:26
  74.6 1.3 %lay_below.1.refs_1_.left_ref = bf16[256,1536]{1,0:T(8,128)(2,1)S(1)} custom-call(s32[1,4,3,12]{3,2,1,0:T(4,128)S(1)} %copy.8.lists_ref, s32[1,4]{1,0:T(1,128)S(1)} %copy-done.3, s32[38]{0:T(128)S(1)} %fusion.2.two_mask_ref, s32[38]{0:T(128)S(1)} %fusion.one_mask_ref, bf16[2448,128]{1,0:T(8,128)(2,1)S(1)} %collective-permute-done.2.two_ref, ...), custom_call_target="tpu_custom_call" | custom-call | bytes 1024 | tf_op jit(solution)/shard_map/lay_below/pallas_call | solution.py:203
  76.0 7.5 %collective-permute-done.1.panel_ref = bf16[2448,128]{1,0:T(8,128)(2,1)} collective-permute-done((bf16[2448,128]{1,0:T(8,128)(2,1)}, bf16[2448,128]{1,0:T(8,128)(2,1)}, u32[]{:S(2)}, u32[]{:S(2)}) %collective-permute-start.1) | collective-permute-done | bytes 626720 | tf_op jit(solution)/shard_map/ppermute | solution.py:26
  83.5 0.7 bitcast_convert_fusion.mask_ref
  84.2 2.1 %step_above.1.known_ref = f32[256,128]{1,0:T(8,128)S(1)} custom-call(s32[1,4,3,12]{3,2,1,0:T(4,128)S(1)} %copy.8.lists_ref, s32[1,4]{1,0:T(1,128)S(1)} %copy-done.3, s32[38]{0:T(128)S(1)} %bitcast_convert_fusion.mask_ref, bf16[2448,128]{1,0:T(8,128)(2,1)} %collective-permute-done.1.panel_ref, bf16[24,128,128]{2,1,0:T(8,128)(2,1)S(1)} %copy-done, ...), custom_call_target="tpu_custom_call" | custom-call | bytes 1024 | tf_op jit(solution)/shard_map/step_above/pallas_call | solution.py:169
  86.3 0.0 collective-permute-done.5
  86.3 1.0 %last_product.1 = bf16[256,128]{1,0:T(8,128)(2,1)} custom-call(f32[256,128]{1,0:T(8,128)S(1)} %step_above.1.known_ref, bf16[256,1536]{1,0:T(8,128)(2,1)S(1)} %lay_below.1.refs_1_.left_ref, bf16[1536,128]{1,0:T(8,128)(2,1)S(1)} %bitcast.11), custom_call_target="tpu_custom_call" | custom-call | bytes 1024 | tf_op jit(solution)/shard_map/last_product/pallas_call | solution.py:221
  (3 shorter events, 0.0 us)
Async XLA Ops:
  0.0 8.9 %copy-start.1 = (s32[38]{0:T(128)S(1)}, s32[38]{0:T(128)}, u32[]{:S(2)}) copy-start(s32[38]{0:T(128)} %mask_ref.5) | copy-start | bytes 460
  0.0 39.1 %copy-start.5 = (s32[1,4,3,12]{3,1,2,0:T(4,128)S(1)}, s32[1,4,3,12]{3,1,2,0:T(4,128)}, u32[]{:S(2)}) copy-start(s32[1,4,3,12]{3,1,2,0:T(4,128)} %param.8) | copy-start | bytes 1732
  3.0 61.9 %copy-start = (bf16[24,128,128]{2,1,0:T(8,128)(2,1)S(1)}, bf16[24,128,128]{2,1,0:T(8,128)(2,1)}, u32[]{:S(2)}) copy-start(bf16[24,128,128]{2,1,0:T(8,128)(2,1)} %right_ref.5) | copy-start | bytes 2359300
  3.0 61.9 %copy-start.2 = (s32[38]{0:T(128)S(1)}, s32[38]{0:T(128)}, u32[]{:S(2)}) copy-start(s32[38]{0:T(128)} %mask_ref.5) | copy-start | bytes 460
  3.0 61.9 %copy-start.3 = (s32[1,4]{1,0:T(1,128)S(1)}, s32[1,4]{1,0:T(1,128)}, u32[]{:S(2)}) copy-start(s32[1,4]{1,0:T(1,128)} %counts_ref.5) | copy-start | bytes 52
  3.0 60.6 %collective-permute-start.2 = (bf16[2448,128]{1,0:T(8,128)(2,1)}, bf16[2448,128]{1,0:T(8,128)(2,1)S(1)}, u32[]{:S(2)}, u32[]{:S(2)}) collective-permute-start(bf16[2448,128]{1,0:T(8,128)(2,1)} %get-tuple-element.7.panel_ref), channel_id=1, source_target_pairs={{0,2},{1,3},{2,4},{3,5},{4,6},{5,7},{6,8},{7,9},{8,10},{9,11},{10,... | collective-permute-start | bytes 1880072 | tf_op jit(solution)/shard_map/ppermute | solution.py:26
  8.9 30.2 %collective-permute-start = (s32[38]{0:T(128)S(1)}, s32[38]{0:T(128)S(1)}, u32[]{:S(2)}, u32[]{:S(2)}) collective-permute-start(s32[38]{0:T(128)S(1)} %copy-done.1), channel_id=1, source_target_pairs={{32,96}} | collective-permute-start | bytes 464 | tf_op jit(solution)/shard_map/ppermute | solution.py:26
  9.6 76.7 %collective-permute-start.5 = (bf16[12,128,128]{2,1,0:T(8,128)(2,1)}, bf16[12,128,128]{2,1,0:T(8,128)(2,1)S(1)}, u32[]{:S(2)}, u32[]{:S(2)}) collective-permute-start(bf16[12,128,128]{2,1,0:T(8,128)(2,1)} %get-tuple-element.8), channel_id=1, source_target_pairs={{0,64},{1,65},{2,66},{3,67},{4,68},{5,69},{6,70},{7,71},{8,72},{9,... | collective-permute-start | bytes 1179656 | tf_op jit(solution)/shard_map/ppermute | solution.py:26
  39.1 0.5 copy-start.6
  42.2 25.3 %collective-permute-start.4 = (bf16[2448,128]{1,0:T(8,128)(2,1)}, bf16[2448,128]{1,0:T(8,128)(2,1)S(1)}, u32[]{:S(2)}, u32[]{:S(2)}) collective-permute-start(bf16[2448,128]{1,0:T(8,128)(2,1)} %pack_again.1), channel_id=1, source_target_pairs={{0,1},{1,2},{2,3},{4,5},{5,6},{6,7},{8,9},{9,10},{10,11},{12,13},{... | collective-permute-start | bytes 1880072 | tf_op jit(solution)/shard_map/ppermute | solution.py:26
  44.5 39.0 %collective-permute-start.1 = (bf16[2448,128]{1,0:T(8,128)(2,1)}, bf16[2448,128]{1,0:T(8,128)(2,1)}, u32[]{:S(2)}, u32[]{:S(2)}) collective-permute-start(bf16[2448,128]{1,0:T(8,128)(2,1)} %pack_again.1), channel_id=1, source_target_pairs={{0,63},{1,0},{2,1},{3,2},{4,3},{5,4},{6,5},{7,6},{8,7},{9,8},{10,9... | collective-permute-start | bytes 1880072 | tf_op jit(solution)/shard_map/ppermute | solution.py:26
  63.6 11.0 %collective-permute-start.3 = (bf16[2448,128]{1,0:T(8,128)(2,1)S(1)}, bf16[2448,128]{1,0:T(8,128)(2,1)S(1)}, u32[]{:S(2)}, u32[]{:S(2)}) collective-permute-start(bf16[2448,128]{1,0:T(8,128)(2,1)S(1)} %collective-permute-done.2.two_ref), channel_id=1, source_target_pairs={{1,0},{5,4},{9,8},{13,12},{17,16},{21,20},{25,24},{29,28},{33,32},... | collective-permute-start | bytes 1880072 | tf_op jit(solution)/shard_map/ppermute | solution.py:26
  64.9 1.1 %copy-start.4 = (bf16[2448,128]{1,0:T(8,128)(2,1)S(1)}, bf16[2448,128]{1,0:T(8,128)(2,1)}, u32[]{:S(2)}) copy-start(bf16[2448,128]{1,0:T(8,128)(2,1)} %get-tuple-element.7.panel_ref) | copy-start | bytes 1880068
